TPU v7x, 32 devices: a whole 2x2x4 slice. The times are simulated.
32 devices in a mesh: seq: 4 (over x, core), head: 8 (over z, y).
Axes of the slice: x: 2, y: 2, z: 4, core: 2. Of those that a mesh axis runs over, the one named last changes fastest.
Arguments:
- x_rows: bfloat16 [20480, 3072], P('seq', 'head'), may hold values from -16 to 16
- z_rows: bfloat16 [20480, 3072], P('seq', 'head'), may hold values from -6 to 6
- b_rows: bfloat16 [20480, 128], P('seq', 'head'), may hold values from -6 to 6
- c_rows: bfloat16 [20480, 128], P('seq', 'head'), may hold values from -0.5 to 0.5
- step_raw: float32 [20480, 48], P('seq', 'head'), may hold values from -4 to 4
- conv_x: bfloat16 [4, 3072], P(None, 'head'), may hold values from -3 to 3
- conv_b: bfloat16 [4, 128], P(None, 'head'), may hold values from -3 to 3
- conv_c: bfloat16 [4, 128], P(None, 'head'), may hold values from -3 to 3
- decay_rate: float32 [48], P('head'), may hold values from 0 to 1, as said below
- norm_gain: float32 [3072], P('head'), may hold values from 0.5 to 1.5
Outputs:
- normed: bfloat16 [20480, 3072], P('seq', 'head')
Inputs may be any that keep to these rules, and one draw needn't show every extreme that they name: `decay_rate`: positive rates.
All inputs are finite; a program needn't handle non-finite values.
Results may differ from a plain program's by a relative error of at most 0.011.
Values may be sent and summed in bfloat16 or wider, within the bound.
No kernel may reach another device: no remote copies, remote signals or barrier semaphores. Data moves between devices by JAX's collectives and lax.ppermute only.
A program may use at most 128 MiB of HBM per device.

v0:
```python
import jax
import jax.numpy as jnp
from jax import lax
from jax.sharding import PartitionSpec as P

GROUP = 256


def shifted(value, axis, steps):
    count = lax.axis_size(axis)
    first, last = (max(0, -steps), min(count, count - steps))
    return lax.ppermute(value, axis, [(source, source + steps) for source in range(first, last)])


def carried_in(value, axis, join, neutral):
    count, mine = (lax.axis_size(axis), lax.axis_index(axis))
    pieces = jax.tree.map(lambda part: lax.all_gather(part, axis), value)
    subtotal = jax.tree.map(
        lambda part, zero: jnp.full_like(part, 0) + jnp.asarray(zero, part.dtype), value, neutral
    )

    def hop(position, subtotal):
        longer = join(subtotal, jax.tree.map(lambda part: part[position], pieces))
        return jax.tree.map(lambda new, old: jnp.where(position < mine, new, old), longer, subtotal)

    return lax.fori_loop(0, count - 1, hop, subtotal)


def conv_valid(padded, weights, length):
    total = jnp.zeros((length, padded.shape[1]), jnp.float32)
    for k in range(weights.shape[0]):
        total = total + weights[k].astype(jnp.float32)[None, :] * padded[k : k + length].astype(
            jnp.float32
        )
    return jax.nn.silu(total).astype(jnp.bfloat16)


def block_parts(x_block, b_block, c_block, step_block, cum_block):
    scores = jnp.dot(c_block, b_block.T, preferred_element_type=jnp.float32)
    order = jnp.arange(x_block.shape[0])
    causal = order[:, None] >= order[None, :]
    gap = cum_block.T[:, :, None] - cum_block.T[:, None, :]
    gap = jnp.where(causal[None], gap, -jnp.inf)
    mixing = (scores[None] * jnp.exp(gap) * step_block.T[:, None, :]).astype(jnp.bfloat16)
    diag = jnp.einsum("hts,shp->thp", mixing, x_block, preferred_element_type=jnp.float32)
    tail = jnp.exp(cum_block[-1][None, :] - cum_block) * step_block
    weighted = (tail[:, :, None] * x_block.astype(jnp.float32)).astype(jnp.bfloat16)
    block_state = jnp.einsum("shp,sn->hpn", weighted, b_block, preferred_element_type=jnp.float32)
    return (diag, block_state)


def join_states(earlier, later):
    return (earlier[0] + later[0], jnp.exp(later[0])[:, None, None] * earlier[1] + later[1])


def body(x_rows, z_rows, b_rows, c_rows, step_raw, conv_x, conv_b, conv_c, decay_rate, norm_gain):
    length = x_rows.shape[0]
    width = conv_x.shape[0]
    local_heads = decay_rate.shape[0]
    x_width = x_rows.shape[1]
    head_size = x_width // local_heads
    state_cols = b_rows.shape[1]
    tails = jnp.concatenate(
        [x_rows[length - width + 1 :], b_rows[length - width + 1 :], c_rows[length - width + 1 :]],
        axis=1,
    )
    before = shifted(tails, "seq", 1)
    ext_x = jnp.concatenate([before[:, :x_width], x_rows], axis=0)
    ext_b = jnp.concatenate([before[:, x_width : x_width + state_cols], b_rows], axis=0)
    ext_c = jnp.concatenate([before[:, x_width + state_cols :], c_rows], axis=0)
    xs = conv_valid(ext_x, conv_x, length)
    whole_b, whole_c, taps_b, taps_c = (
        lax.all_gather(ext_b, "head", axis=1, tiled=True),
        lax.all_gather(ext_c, "head", axis=1, tiled=True),
        lax.all_gather(conv_b, "head", axis=1, tiled=True),
        lax.all_gather(conv_c, "head", axis=1, tiled=True),
    )
    bs = conv_valid(whole_b, taps_b, length)
    cs = conv_valid(whole_c, taps_c, length)
    state_size = bs.shape[1]
    step = jax.nn.softplus(step_raw)
    log_decay = -step * decay_rate[None, :]
    count = length // GROUP
    c_blocks = cs.reshape(count, GROUP, state_size)
    pieces = (
        xs.reshape(count, GROUP, local_heads, head_size),
        bs.reshape(count, GROUP, state_size),
        c_blocks,
        step.reshape(count, GROUP, local_heads),
        log_decay.reshape(count, GROUP, local_heads),
    )

    def advance(state, piece):
        x_block, b_block, c_block, step_block, decay_block = piece
        cum = jnp.cumsum(decay_block, axis=0)
        diag, block_state = block_parts(x_block, b_block, c_block, step_block, cum)
        new_state = jnp.exp(cum[-1])[:, None, None] * state + block_state
        return (new_state, (diag.reshape(GROUP, x_width), state, cum))

    start = jnp.zeros((local_heads, head_size, state_size), jnp.float32)
    last_state, (diags, local_states, cums) = lax.scan(advance, start, pieces)
    block_totals = cums[:, -1, :]
    device_decay = jnp.sum(block_totals, axis=0)
    _, carry_in = carried_in(
        (device_decay, last_state),
        "seq",
        join_states,
        (jnp.zeros_like(device_decay), jnp.zeros_like(last_state)),
    )
    preceding = jnp.cumsum(block_totals, axis=0) - block_totals
    full_states = local_states + jnp.exp(preceding)[:, :, None, None] * carry_in[None]
    carried = (
        jnp.einsum(
            "chpn,ctn->cthp",
            full_states,
            c_blocks.astype(jnp.float32),
            precision=lax.Precision.HIGHEST,
        )
        * jnp.exp(cums)[:, :, :, None]
    )
    y_rows = (diags + carried.reshape(count, GROUP, x_width)).reshape(length, x_width)
    gated = y_rows * jax.nn.silu(z_rows.astype(jnp.float32))
    total = lax.psum(jnp.sum(gated * gated, axis=1), "head")
    mean_sq = total[:, None] / (lax.axis_size("head") * x_width)
    return (gated * lax.rsqrt(mean_sq + 1e-05) * norm_gain[None, :]).astype(jnp.bfloat16)


def solution(mesh):
    placed = (
        P("seq", "head"),
        P("seq", "head"),
        P("seq", "head"),
        P("seq", "head"),
        P("seq", "head"),
        P(None, "head"),
        P(None, "head"),
        P(None, "head"),
        P("head"),
        P("head"),
    )
    return jax.shard_map(
        body, mesh=mesh, in_specs=placed, out_specs=P("seq", "head"), check_vma=False
    )
```

profile of v0, /device:TPU:0, one launch (start us, length us, event | category | flops | bytes accessed | tf_op | source)
XLA Modules:
  0.0 360.6 jit_solution(18341518797804462944)
XLA Ops:
  9.0 2.3 collective-permute-start
  12.4 1.7 pad_maximum_fusion.2
  15.1 21.9 %all-gather.3 = bf16[8,16,4]{1,2,0:T(4,128)(2,1)S(1)} all-gather(bf16[1,16,4]{1,2,0:T(4,128)(2,1)} %bitcast.161), channel_id=1, replica_groups=mesh['seq'=4,'head'=8] {'head'}, dimensions={0}, use_global_device_ids=true | all-gather | bytes 1152 | tf_op jit(solution)/shard_map/all_gather | solution.py:76
  37.0 16.6 %all-gather.2 = bf16[8,16,4]{1,2,0:T(4,128)(2,1)S(1)} all-gather(bf16[1,16,4]{1,2,0:T(4,128)(2,1)} %bitcast.162), channel_id=1, replica_groups=mesh['seq'=4,'head'=8] {'head'}, dimensions={0}, use_global_device_ids=true | all-gather | bytes 1152 | tf_op jit(solution)/shard_map/all_gather | solution.py:75
  53.7 1.3 dynamic-slice
  56.8 1.7 pad_maximum_fusion.1
  58.5 11.5 %multiply_convert_fusion.4 = bf16[5120,384]{1,0:T(8,128)(2,1)} fusion(bf16[5120,384]{1,0:T(8,128)(2,1)} %param.14, bf16[3,384]{1,0:T(4,128)(2,1)S(1)} %slice.135, f32[384]{0:T(512)S(1)} %get-tuple-element.262, f32[384]{0:T(512)S(1)} %get-tuple-element.263, f32[384]{0:T(512)S(1)} %get-tuple-element.261, f32[384]{0:T(512)S(1)} %get-tuple-element.260), kind=kLoop, calls=%fused_computation.49 | loop fusion | flops 49152000 | bytes 7872768 | tf_op jit(solution)/shard_map/convert_element_type | solution.py:35
  70.0 6.3 %copy.91 = bf16[5120,384]{0,1:T(8,128)(2,1)} copy(bf16[5120,384]{1,0:T(8,128)(2,1)} %multiply_convert_fusion.4) | data formatting | bytes 7864320 | tf_op jit(solution)/shard_map/convert_element_type | solution.py:35
  76.4 7.6 %reshape.106 = bf16[20,256,6,64]{1,0,3,2:T(8,128)(2,1)} reshape(bf16[5120,384]{0,1:T(8,128)(2,1)} %copy.91) | data formatting | bytes 7864320 | tf_op jit(solution)/shard_map/reshape | solution.py:86
  84.0 5.2 %copy.98 = bf16[20,256,6,64]{1,3,2,0:T(8,128)(2,1)} copy(bf16[20,256,6,64]{1,0,3,2:T(8,128)(2,1)} %reshape.106) | data formatting | bytes 7864320
  89.1 5.8 %multiply_convert_fusion.5 = bf16[5120,128]{0,1:T(8,128)(2,1)S(1)} fusion(bf16[5123,128]{0,1:T(8,128)(2,1)} %all-gather.9.cloned.1.call-done, f32[128]{0:T(128)S(1)} %get-tuple-element.305, f32[128]{0:T(128)S(1)} %get-tuple-element.306, f32[128]{0:T(128)S(1)} %get-tuple-element.307, f32[128]{0:T(128)S(1)} %get-tuple-element.304), kind=kLoop, calls=%fused_computation.59 | loop fusion | flops 10485760 | bytes 6555648 | tf_op jit(solution)/shard_map/convert_element_type | solution.py:35
  95.7 8.5 %all-gather.7.cloned.1.call-done = bf16[5123,128]{0,1:T(8,128)(2,1)} async-done(((bf16[5123,16]{0,1:T(8,128)(2,1)}), bf16[5123,128]{0,1:T(8,128)(2,1)}) %all-gather.7.cloned.1.call-update) | async-done | bytes 1311504 | tf_op jit(solution)/shard_map/all_gather | solution.py:73
  104.2 5.9 %multiply_convert_fusion.6 = bf16[5120,128]{0,1:T(8,128)(2,1)S(1)} fusion(bf16[5123,128]{0,1:T(8,128)(2,1)} %all-gather.7.cloned.1.call-done, f32[128]{0:T(128)S(1)} %get-tuple-element.309, f32[128]{0:T(128)S(1)} %get-tuple-element.310, f32[128]{0:T(128)S(1)} %get-tuple-element.311, f32[128]{0:T(128)S(1)} %get-tuple-element.308), kind=kLoop, calls=%fused_computation.60 | loop fusion | flops 10485760 | bytes 6555648 | tf_op jit(solution)/shard_map/convert_element_type | solution.py:35
  110.1 1.5 copy.94
  111.6 156.0 %while.31 = (s32[]{:T(128)}, f32[6,64,128]{2,1,0:T(8,128)S(1)}, f32[20,256,384]{1,2,0:T(8,128)}, f32[20,6,64,128]{3,2,1,0:T(8,128)}, f32[20,256,6]{1,2,0:T(8,128...) while((s32[]{:T(128)}, f32[6,64,128]{2,1,0:T(8,128)S(1)}, ...), condition=%wide.region_3.4_spmd.clone, body=%wide.region_0.3_spmd.clone.sunk | while | flops 94997520 | bytes 3352916 | solution.py:101
  111.6 1.8 reduce-window.14
  114.9 1.5 fusion.55
  119.4 1.8 reduce-window.14
  122.7 1.5 fusion.55
  127.2 1.8 reduce-window.14
  130.5 1.5 fusion.55
  135.0 1.8 reduce-window.14
  138.3 1.5 fusion.55
  142.8 1.8 reduce-window.14
  146.1 1.5 fusion.55
  149.4 1.2 convolution_add_fusion.2
  150.6 1.8 reduce-window.14
  153.9 1.5 fusion.55
  158.4 1.8 reduce-window.14
  161.7 1.5 fusion.55
  166.2 1.8 reduce-window.14
  169.5 1.5 fusion.55
  174.0 1.8 reduce-window.14
  177.3 1.5 fusion.55
  181.8 1.8 reduce-window.14
  185.1 1.5 fusion.55
  189.6 1.8 reduce-window.14
  192.9 1.5 fusion.55
  197.4 1.8 reduce-window.14
  200.7 1.5 fusion.55
  205.2 1.8 reduce-window.14
  208.5 1.5 fusion.55
  213.0 1.8 reduce-window.14
  216.3 1.5 fusion.55
  220.8 1.8 reduce-window.14
  224.1 1.5 fusion.55
  228.6 1.8 reduce-window.14
  231.9 1.5 fusion.55
  236.4 1.8 reduce-window.14
  239.7 1.5 fusion.55
  244.2 1.8 reduce-window.14
  247.5 1.5 fusion.55
  252.0 1.8 reduce-window.14
  255.3 1.5 fusion.55
  259.8 1.8 reduce-window.14
  263.1 1.5 fusion.55
  268.6 5.8 %all-reduce = f32[24]{0:T(128)S(1)} all-reduce(f32[24]{0:T(128)S(1)} %dynamic-update-slice), channel_id=2, replica_groups=mesh['seq'=4,'head'=8] {'seq'}, use_global_device_ids=true, to_apply=%add | all-reduce | flops 24 | bytes 192
  274.5 8.8 %all-gather.1 = f32[24,64,128]{2,1,0:T(8,128)S(1)} all-gather(f32[6,64,128]{2,1,0:T(8,128)S(1)} %get-tuple-element.157), channel_id=3, replica_groups=mesh['seq'=4,'head'=8] {'seq'}, dimensions={0}, use_global_device_ids=true | all-gather | bytes 983040 | tf_op jit(solution)/shard_map/all_gather | solution.py:17
  283.7 5.6 %broadcast_multiply_fusion = f32[20,256,6,64]{1,3,2,0:T(8,128)S(1)} fusion(f32[20,256,6]{1,2,0:T(8,128)S(1)} %exp.60, bf16[20,256,128,1]{2,1,3,0:T(8,128)(2,1)S(1)} %bitcast.151, f32[20,6,64,128]{3,2,1,0:T(8,128)} %get-tuple-element.155, f32[6,64,128]{2,1,0:T(8,128)S(1)} %get-tuple-element.158, f32[20,6]{1,0:T(8,128)S(1)} %subtract_exponential_fusion), kind=kOutput, calls=%fused_computation.55 | convolution fusion | flops 3023831040 | bytes 13427168 | tf_op jit(solution)/shard_map/chpn,ctn->cthp/dot_general | solution.py:113
  289.3 7.6 %bitcast_add_fusion.1 = f32[20,256,384]{1,2,0:T(8,128)} fusion(f32[20,256,384]{1,2,0:T(8,128)} %get-tuple-element.154, f32[20,256,6,64]{1,3,2,0:T(8,128)S(1)} %broadcast_multiply_fusion), kind=kLoop, calls=%fused_computation.46 | loop fusion | flops 1966080 | bytes 23592960 | tf_op jit(solution)/shard_map/add | solution.py:121
  297.0 9.1 %copy.102 = f32[20,256,384]{2,1,0:T(8,128)} copy(f32[20,256,384]{1,2,0:T(8,128)} %bitcast_add_fusion.1) | data formatting | bytes 15728640 | tf_op jit(solution)/shard_map/add | solution.py:121
  306.0 5.7 %multiply_reduce_fusion = f32[5120]{0:T(1024)S(1)} fusion(bf16[5120,384]{1,0:T(8,128)(2,1)} %param.15, f32[20,256,384]{2,1,0:T(8,128)} %copy.102), kind=kLoop, calls=%fused_computation.48 | loop fusion | flops 15723520 | bytes 11816960 | tf_op jit(solution)/shard_map/reduce_sum | solution.py:123
  311.7 34.8 %psum.7 = f32[5120]{0:T(1024)S(1)} all-reduce(f32[5120]{0:T(1024)S(1)} %multiply_reduce_fusion), channel_id=1, replica_groups=mesh['seq'=4,'head'=8] {'head'}, use_global_device_ids=true, to_apply=%region_9.10 | all-reduce | flops 5120 | bytes 40960 | tf_op jit(solution)/shard_map/psum | solution.py:123
  346.6 7.2 %multiply_convert_fusion.3 = bf16[5120,384]{1,0:T(8,128)(2,1)} fusion(f32[384]{0:T(512)S(1)} %copy-done, f32[5120]{0:T(1024)S(1)} %add_rsqrt_fusion, bf16[5120,384]{1,0:T(8,128)(2,1)} %param.15, f32[20,256,384]{2,1,0:T(8,128)} %copy.102), kind=kLoop, calls=%fused_computation.47 | loop fusion | flops 17694720 | bytes 15750656 | tf_op jit(solution)/shard_map/convert_element_type | solution.py:125
  (408 shorter events, 94.7 us)
Async XLA Ops:
  6.5 82.6 %all-gather.9.cloned.1.call-start = ((), (), s32[]{:S(2)}) async-start(), calls=%async_computation.1 | async-start | bytes 1511424 | tf_op jit(solution)/shard_map/all_gather | solution.py:74
  9.0 3.2 collective-permute-start
  14.1 90.2 %all-gather.7.cloned.1.call-start = ((), (), s32[]{:S(2)}) async-start(), calls=%async_computation | async-start | bytes 1511424 | tf_op jit(solution)/shard_map/all_gather | solution.py:73
  306.0 40.5 %copy-start = (f32[384]{0:T(512)S(1)}, f32[384]{0:T(512)}, u32[]{:S(2)}) copy-start(f32[384]{0:T(512)} %param.23) | copy-start | bytes 4612
Sparse Core Ops, SparseCore 0:
  14.2 46.7 all-gather.8
  63.1 41.0 all-gather.6
where the time goes:
time: 363 us; the launch traced here: 361 us
  other arithmetic  104 us (29%)
  blocking collectives  87.9 us (24%)
  matrix products  79.7 us (22%)
  local copies, waits for them, and re-layouts  61.2 us (17%)
  between operations  14.2 us (4%)
  waiting for transfers between devices  9.36 us (3%)
    another operation x40, other arithmetic  37.3 us
    psum x1, blocking collectives, body(): total = lax.psum(jnp.sum(gated * gated, axis=1), 'head')  34.8 us
    dot_general x20, matrix products, block_parts(): jnp.einsum('hts,shp->thp', mixing, x_block, preferred_element_type=jnp.fl...  30.6 us
    convert_element_type x3, other arithmetic, conv_valid(): return jax.nn.silu(total).astype(jnp.bfloat16)  23.1 us
    dot_general x20, matrix products, block_parts(): jnp.einsum('shp,sn->hpn', weighted, b_block, preferred_element_type=jnp.f...  23.1 us
    all_gather x1, blocking collectives, body(): lax.all_gather(conv_c, 'head', axis=1, tiled=True)  21.9 us
    dot_general x20, matrix products, block_parts(): scores = jnp.dot(c_block, b_block.T, preferred_element_type=jnp.float32)  20.5 us
    all_gather x1, blocking collectives, body(): lax.all_gather(conv_b, 'head', axis=1, tiled=True)  16.6 us
  transfers between devices with their start and end apart: 3, of which 2 were waited for; matrix products, arithmetic and copies ran while one was open for 12% of the time, Pallas kernels for 0%

commit v1 on v0

v1 whole, which is shorter than its diff:
```python
import functools
import math

import jax
import jax.numpy as jnp
from jax import lax
from jax.experimental import pallas as pl
from jax.experimental.pallas import tpu as pltpu
from jax.sharding import PartitionSpec as P

SUB = 128
ROWS = 16
TILE = 8 * SUB
LOG2E = math.log2(math.e)
MIB = 1024 * 1024
F32, BF16 = jnp.float32, jnp.bfloat16


def params(mib=16):
    return pltpu.CompilerParams(vmem_limit_bytes=mib * MIB)


def in_hbm(value):
    return pltpu.with_memory_space_constraint(value, pltpu.HBM)


def in_vmem(values):
    return [pltpu.with_memory_space_constraint(value, pltpu.VMEM) for value in values]


IN_VMEM = pl.BlockSpec(memory_space=pltpu.VMEM)
BRIEF = pl.CostEstimate(flops=1000, bytes_accessed=1000, transcendentals=0)
ANYWHERE = pl.BlockSpec(memory_space=pl.ANY)


def silu(value):
    half = 0.5 * value
    return half * jnp.tanh(half) + half


def factors(count):
    inner = max(d for d in range(1, math.isqrt(count) + 1) if count % d == 0)
    return count // inner, inner


def outer_pairs(d):
    outer, inner = factors(lax.axis_size("head"))
    return [(z * inner + y, (z + d) % outer * inner + y) for z in range(outer) for y in range(inner)]


def inner_pairs(e):
    outer, inner = factors(lax.axis_size("head"))
    return [(z * inner + y, z * inner + (y + e) % inner) for z in range(outer) for y in range(inner)]


def along_outer(piece):
    outer, _ = factors(lax.axis_size("head"))
    return [lax.ppermute(piece, "head", outer_pairs(d)) for d in range(1, outer)]


def along_inner(pieces):
    _, inner = factors(lax.axis_size("head"))
    return [lax.ppermute(p, "head", inner_pairs(e)) for e in range(1, inner) for p in pieces]


def tie_kernel(*refs):
    pass


def after(values, *tokens):
    out = pl.pallas_call(
        tie_kernel,
        in_specs=[ANYWHERE] * (len(values) + len(tokens)),
        out_specs=[ANYWHERE] * len(values),
        out_shape=[jax.ShapeDtypeStruct(v.shape, v.dtype) for v in values],
        input_output_aliases={i: i for i in range(len(values))},
        compiler_params=params(1),
        cost_estimate=BRIEF,
        name="tie",
    )(*values, *tokens)
    return list(out)


def pack_kernel(rows, cuts, *refs):
    outs = refs[len(refs) - len(cuts) + 1 :]
    for out_ref, first_token, last_token in zip(outs, cuts[:-1], cuts[1:]):
        row = 0
        for ref, (first, last) in zip(refs, rows):
            out_ref[row : row + last - first] = ref[first:last, first_token:last_token]
            row += last - first


def pack(pieces, rows, *tokens, cuts=None):
    cuts = cuts or [0, pieces[0].shape[1]]
    count = sum(last - first for first, last in rows)
    return pl.pallas_call(
        functools.partial(pack_kernel, rows, cuts),
        in_specs=[IN_VMEM] * len(pieces) + [ANYWHERE] * len(tokens),
        out_specs=[IN_VMEM] * (len(cuts) - 1),
        out_shape=[
            pltpu.VMEM((count, last - first), pieces[0].dtype) for first, last in zip(cuts[:-1], cuts[1:])
        ],
        compiler_params=params(),
        cost_estimate=BRIEF,
        name="pack",
    )(*in_vmem(pieces), *tokens)


def tails_kernel(x_ref, b_ref, c_ref, out_ref, b_out, c_out):
    cols, length = b_ref.shape
    out_ref[...] = jnp.zeros_like(out_ref)
    out_ref[:16] = x_ref[...]
    out_ref[16 : 16 + cols, :SUB] = b_ref[:, length - SUB :]
    out_ref[32 : 32 + cols, :SUB] = c_ref[:, length - SUB :]
    b_out[...] = b_ref[...]
    c_out[...] = c_ref[...]


def tails(x_rows, b_cols, c_cols):
    length, width = x_rows.shape
    cols = b_cols.shape[0]
    whole = pl.BlockSpec((cols, length), lambda i: (0, 0))
    held = pltpu.VMEM((cols, length), BF16)
    return pl.pallas_call(
        tails_kernel,
        grid=(1,),
        in_specs=[pl.BlockSpec((16, width), lambda i: (length // 16 - 1, 0)), whole, whole],
        out_specs=[pl.BlockSpec((48, width), lambda i: (0, 0)), IN_VMEM, IN_VMEM],
        out_shape=[jax.ShapeDtypeStruct((48, width), BF16), held, held],
        compiler_params=params(),
        cost_estimate=BRIEF,
        name="tails",
    )(in_hbm(x_rows), in_hbm(b_cols), in_hbm(c_cols))


def conv_columns(rows, halo, taps):
    wide = jnp.concatenate([halo, rows], axis=1).astype(F32)
    width = taps.shape[1]
    total = None
    for k in range(width):
        lag = width - 1 - k
        moved = pltpu.roll(wide, lag, axis=1) if lag else wide
        term = taps[:, k : k + 1] * moved[:, SUB:]
        total = term if total is None else total + term
    return silu(total).astype(BF16)


def shared_conv_kernel(b_ref, c_ref, halo_ref, tb_ref, tc_ref, bs_ref, cs_ref, again_ref):
    cols = b_ref.shape[0]
    bs_ref[...] = conv_columns(b_ref[...], halo_ref[16 : 16 + cols, :SUB], tb_ref[...])
    cs = conv_columns(c_ref[...], halo_ref[32 : 32 + cols, :SUB], tc_ref[...])
    cs_ref[...], again_ref[...] = cs, cs


def shared_conv(b_cols, c_cols, halo, taps_b, taps_c):
    operands = [b_cols, c_cols, halo, taps_b, taps_c]
    return pl.pallas_call(
        shared_conv_kernel,
        in_specs=[IN_VMEM] * 5,
        out_specs=[IN_VMEM] * 3,
        out_shape=[pltpu.VMEM(b_cols.shape, BF16)] * 3,
        compiler_params=params(),
        cost_estimate=BRIEF,
        name="shared_conv",
    )(*in_vmem(operands))


def parts_of(value, count):
    parts = []
    for _ in range(count):
        part = value.astype(BF16).astype(F32)
        parts.append(part)
        value = value - part
    return jnp.concatenate(parts, axis=0)


def spread_matrix(first, last, count, width, size):
    i = lax.broadcasted_iota(jnp.int32, (count, width), 0)
    j = lax.broadcasted_iota(jnp.int32, (count, width), 1)
    head = jnp.bitwise_and(i, 7) * size
    lanes = jnp.logical_and(j >= head, j < head + size)
    return jnp.logical_and(lanes, jnp.logical_and(i >= first, i < last)).astype(F32).astype(BF16)


def rows_kernel(step_ref, rate_ref, q_ref, column_ref, decay_ref, sp, ld):
    heads, length = step_ref.shape
    width = decay_ref.shape[1]
    subs = length // SUB
    raw = step_ref[...]
    soft = jnp.maximum(raw, 0.0) + jnp.log(1.0 + jnp.exp(-jnp.abs(raw)))
    sp[...] = jnp.ones_like(sp)
    ld[...] = jnp.zeros_like(ld)
    sp[:heads] = soft
    ld[:heads] = soft * (rate_ref[...] * -LOG2E)
    i = lax.broadcasted_iota(jnp.int32, (SUB, SUB), 0)
    j = lax.broadcasted_iota(jnp.int32, (SUB, SUB), 1)
    upper = (i <= j).astype(F32)
    logs = ld[...]
    stacked = jnp.concatenate([logs[:, s * SUB : (s + 1) * SUB] for s in range(subs)], axis=0)
    sums = jnp.dot(stacked, upper, precision=lax.Precision.HIGHEST, preferred_element_type=F32)
    log_step = jnp.log(sp[...]) * LOG2E
    lasts = []
    for s in range(subs):
        at = slice(s * SUB, (s + 1) * SUB)
        cum = sums[s * 8 : (s + 1) * 8]
        q = cum - log_step[:, at]
        q_ref[:, at] = q
        weight = jnp.exp2(cum[:, SUB - 1 :] - q)
        columns = jnp.concatenate([parts_of(weight, 2), parts_of(cum, 3)], axis=0).T
        column_ref[at] = columns.astype(BF16)
        lasts.append(columns[SUB - 1 :])
    whole = jnp.concatenate(lasts, axis=0).astype(BF16)
    to_lanes = spread_matrix(16, 40, 40, width, width // heads)
    decay_ref[...] = jnp.exp2(jnp.dot(whole, to_lanes, preferred_element_type=F32))


def rows_of(steps, rates, width):
    heads, length = steps.shape
    return pl.pallas_call(
        rows_kernel,
        in_specs=[IN_VMEM] * 2,
        out_specs=[IN_VMEM] * 3,
        out_shape=[
            pltpu.VMEM((8, length), F32),
            pltpu.VMEM((length, 40), BF16),
            pltpu.VMEM((length // SUB, width), F32),
        ],
        scratch_shapes=[pltpu.VMEM((8, length), F32), pltpu.VMEM((8, length), F32)],
        compiler_params=params(),
        cost_estimate=BRIEF,
        name="rows",
    )(*in_vmem([steps, rates]))


def head_conv_kernel(first, heads, x_ref, before_ref, halo_ref, taps_ref, column_ref, *refs):
    xs_ref, wt_ref, ext, spread = refs[-4:]
    length, width = x_ref.shape
    taps = taps_ref.shape[0]
    pairs = width // SUB

    @pl.when(pl.program_id(0) == 0)
    def _():
        for p in range(pairs):
            rows = before_ref if first else halo_ref
            ext[p, :8] = rows[8:16, p * SUB : (p + 1) * SUB].astype(F32)

    for p in range(pairs):
        ext[p, 8:] = x_ref[:, p * SUB : (p + 1) * SUB].astype(F32)
    count = column_ref.shape[1]
    spread[...] = jnp.dot(
        column_ref[...],
        spread_matrix(0, 16, count, width, width // heads),
        preferred_element_type=F32,
    )
    for s in range(length // SUB):
        at = slice(s * SUB, (s + 1) * SUB)
        for p in range(pairs):
            cols = slice(p * SUB, (p + 1) * SUB)
            total = None
            for k in range(taps):
                start = 8 - (taps - 1) + k + s * SUB
                term = taps_ref[k : k + 1, cols] * ext[p, start : start + SUB]
                total = term if total is None else total + term
            xs = silu(total).astype(BF16)
            xs_ref[at, cols] = xs
            wt_ref[at, cols] = (spread[at, cols] * xs.astype(F32)).astype(BF16)
    for p in range(pairs):
        ext[p, :8] = ext[p, length : length + 8]


def head_conv(x_rows, halo, taps, columns, heads, first, count, filled=()):
    length, width = x_rows.shape
    wide = pl.BlockSpec((TILE, width), lambda i: (first + i, 0))
    whole = lambda a: pl.BlockSpec(a.shape, lambda i: (0, 0))
    return pl.pallas_call(
        functools.partial(head_conv_kernel, first, heads),
        grid=(count,),
        in_specs=[
            wide,
            pl.BlockSpec((16, width), lambda i: (max(first * TILE // 16 - 1, 0), 0)),
            whole(halo),
            whole(taps),
            pl.BlockSpec((TILE, columns.shape[1]), lambda i: (first + i, 0)),
        ]
        + [ANYWHERE] * len(filled),
        out_specs=[wide, wide],
        out_shape=[jax.ShapeDtypeStruct((length, width), BF16)] * 2,
        scratch_shapes=[
            pltpu.VMEM((width // SUB, TILE + 8, SUB), F32),
            pltpu.VMEM((TILE, width), F32),
        ],
        compiler_params=params(),
        input_output_aliases={5 + i: i for i in range(len(filled))},
        cost_estimate=BRIEF,
        name="head_conv",
    )(in_hbm(x_rows), in_hbm(x_rows), halo, taps, columns, *filled)


def gates_kernel(z_ref, column_ref, q_ref, gate_ref, factor_ref, start_ref, spread):
    length, width = z_ref.shape
    heads = factor_ref.shape[0] // (length // ROWS)
    size = width // heads
    subs, groups = length // SUB, SUB // ROWS
    columns = column_ref[...]
    to_lanes = spread_matrix(16, 40, columns.shape[1], width, size)
    for p in range(width // SUB):
        spread[p] = jnp.dot(
            columns, to_lanes[:, p * SUB : (p + 1) * SUB], preferred_element_type=F32
        )
    for s in range(subs):
        at = slice(s * SUB, (s + 1) * SUB)
        starts = []
        for p in range(width // SUB):
            cols = slice(p * SUB, (p + 1) * SUB)
            cum = spread[p, at].reshape(groups, ROWS // 8, 8, SUB)
            grown = jnp.exp2(cum - cum[:, ROWS // 16 : ROWS // 16 + 1, :1]).reshape(SUB, SUB)
            gate_ref[at, cols] = grown * silu(z_ref[at, cols].astype(F32))
            start = spread[p, pl.ds(s * SUB + ROWS // 2, groups, stride=ROWS)]
            start_ref[p, s * groups : (s + 1) * groups] = jnp.exp2(start)
            starts.append(start)
        for h in range(heads):
            lane = h * size % SUB
            start = jnp.broadcast_to(starts[h * size // SUB][:, lane : lane + 1], (groups, SUB))
            row = (s * heads + h) * groups
            factor_ref[row : row + groups] = jnp.exp2(
                jnp.minimum(start - q_ref[h : h + 1, at], 64.0)
            )


def gates(z_rows, columns, q, heads):
    length, width = z_rows.shape
    wide = pl.BlockSpec((TILE, width), lambda i: (i, 0))
    rows = pl.BlockSpec((8, TILE), lambda i: (0, i))
    return pl.pallas_call(
        gates_kernel,
        grid=(length // TILE,),
        in_specs=[wide, pl.BlockSpec((TILE, columns.shape[1]), lambda i: (i, 0)), rows],
        out_specs=[
            wide,
            pl.BlockSpec((TILE // ROWS * heads, SUB), lambda i: (i, 0)),
            pl.BlockSpec((width // SUB, TILE // ROWS, SUB), lambda i: (0, i, 0)),
        ],
        out_shape=[
            jax.ShapeDtypeStruct((length, width), F32),
            jax.ShapeDtypeStruct((length // ROWS * heads, SUB), F32),
            jax.ShapeDtypeStruct((width // SUB, length // ROWS, SUB), F32),
        ],
        scratch_shapes=[pltpu.VMEM((width // SUB, TILE, SUB), F32)],
        compiler_params=params(),
        cost_estimate=BRIEF,
        name="gates",
    )(z_rows, columns, q)


def columns_of(refs, rows, at):
    return jnp.concatenate([ref[first:last, at] for ref, (first, last) in zip(refs, rows)], axis=0)


def columns_from(refs, rows, begins, start):
    parts = [
        ref[first:last, pl.ds(pl.multiple_of(start - begin, SUB), SUB)]
        for ref, (first, last), begin in zip(refs, rows, begins)
    ]
    return jnp.concatenate(parts, axis=0)


def last_state_kernel(rows, wt_ref, decay_ref, *refs):
    pieces, (out_ref, local_ref, before_ref, state, total) = refs[:-5], refs[-5:]
    size = state.shape[0]
    subs = TILE // SUB
    state[...] = jnp.zeros_like(state)
    total[...] = jnp.ones_like(total)

    def tile(t, _):
        held, grown = state[...], total[:1]
        row = pl.multiple_of(t * subs, subs)
        decays = decay_ref[pl.ds(row, subs)]
        products = []
        for s in range(subs):
            at = pl.ds(pl.multiple_of(t * TILE + s * SUB, SUB), SUB)
            b_cols = columns_of(pieces, rows, at)
            added = jnp.dot(b_cols, wt_ref[at], preferred_element_type=F32)
            local_ref[pl.ds(pl.multiple_of((t * subs + s) * size, size), size)] = held
            products.append(grown)
            held = held * decays[s : s + 1] + added
            grown = grown * decays[s : s + 1]
        before_ref[pl.ds(row, subs)] = jnp.concatenate(products, axis=0)
        state[...] = held
        total[...] = jnp.broadcast_to(grown, total.shape)
        return 0

    lax.fori_loop(0, wt_ref.shape[0] // TILE, tile, 0)
    out_ref[:size] = state[...].astype(BF16)
    out_ref[size:] = jnp.broadcast_to(total[:1], (16, total.shape[1])).astype(BF16)


def last_state(weighted, decays, pieces, rows):
    length, width = weighted.shape
    size = sum(last - first for first, last in rows)
    count = length // SUB
    return pl.pallas_call(
        functools.partial(last_state_kernel, rows),
        in_specs=[IN_VMEM] * (2 + len(pieces)),
        out_specs=[IN_VMEM] * 3,
        out_shape=[
            jax.ShapeDtypeStruct((size + 16, width), BF16),
            pltpu.VMEM((count * size, width), F32),
            pltpu.VMEM((count, width), F32),
        ],
        scratch_shapes=[pltpu.VMEM((size, width), F32), pltpu.VMEM((8, width), F32)],
        compiler_params=params(),
        cost_estimate=BRIEF,
        name="last_state",
    )(*in_vmem([weighted, decays, *pieces]))


def join_kernel(early_ref, late_ref, token_ref, out_ref):
    size = late_ref.shape[0] - 16
    early, late = early_ref[...].astype(F32), late_ref[...].astype(F32)
    decay = late[size : size + 1]
    out_ref[:size] = (early[:size] * decay + late[:size]).astype(BF16)
    out_ref[size:] = (early[size:] * decay).astype(BF16)


def join(early, late, token):
    return pl.pallas_call(
        join_kernel,
        in_specs=[IN_VMEM] * 2 + [ANYWHERE],
        out_specs=IN_VMEM,
        out_shape=jax.ShapeDtypeStruct(late.shape, BF16),
        compiler_params=params(),
        cost_estimate=BRIEF,
        name="join",
    )(*in_vmem([early, late]), token)


def enter_kernel(local_ref, before_ref, *refs):
    earlier, (out_ref, state) = refs[:-2], refs[-2:]
    size = state.shape[0]
    carry = jnp.zeros(state.shape, F32)
    for ref in reversed(earlier):
        carry = carry * ref[size : size + 1].astype(F32) + ref[:size].astype(F32)
    state[...] = carry
    some = 8

    def group(t, _):
        row = pl.multiple_of(t * some, some)
        decays = before_ref[pl.ds(row, some)]
        held = state[...]
        for s in range(some):
            at = pl.ds(pl.multiple_of((t * some + s) * size, size), size)
            out_ref[at] = (local_ref[at] + held * decays[s : s + 1]).astype(BF16)
        return 0

    lax.fori_loop(0, before_ref.shape[0] // some, group, 0)


def enter(local, before, earlier):
    rows, width = local.shape
    size = rows // before.shape[0]
    operands = [local, before, *earlier]
    return pl.pallas_call(
        enter_kernel,
        in_specs=[IN_VMEM] * len(operands),
        out_specs=IN_VMEM,
        out_shape=pltpu.VMEM((rows, width), BF16),
        scratch_shapes=[pltpu.VMEM((size, width), F32)],
        compiler_params=params(),
        cost_estimate=BRIEF,
        name="enter",
    )(*in_vmem(operands))


def scan_kernel(
    span, b_rows, b_picks, c_rows_of, c_picks, c_begins, gate_ref, factor_ref, start_ref, xs_ref, state_ref, *refs
):
    b_refs, c_refs = [refs[i] for i in b_picks], [refs[i] for i in c_picks]
    gated_ref, square_ref, c_rows, scores, carried, squares = refs[-6:]
    length, width = gate_ref.shape
    heads = factor_ref.shape[0] // (length // ROWS)
    groups, subs, pairs = SUB // ROWS, TILE // SUB, width // SUB
    size = state_ref.shape[0] // square_ref.shape[0]
    i = lax.broadcasted_iota(jnp.int32, (SUB, SUB), 0)
    j = lax.broadcasted_iota(jnp.int32, (SUB, SUB), 1)
    causal = i >= j
    low = (j < SUB // 2).astype(F32)
    keep_low, keep_high = low.astype(BF16), (1.0 - low).astype(BF16)

    def rows_times(value, load):
        rows = [value[g * ROWS : (g + 1) * ROWS] * load(g) for g in range(groups)]
        return jnp.concatenate(rows, axis=0)

    def repeated(ref, row):
        return jnp.broadcast_to(ref[pl.ds(row, 1)], (ROWS, SUB))

    local = [slice(s * SUB, (s + 1) * SUB) for s in range(subs)]

    def tile(t, _):
        whole = [pl.ds(pl.multiple_of(t * TILE + s * SUB, SUB), SUB) for s in range(subs)]
        row = pl.multiple_of(t * subs, subs)
        factors = pl.multiple_of(t * (subs * heads * groups), subs * heads * groups)
        starts = pl.multiple_of(t * (subs * groups), subs * groups)

        def turn(s):
            c_rows[local[s]] = columns_from(c_refs, c_rows_of, c_begins, t * TILE + s * SUB).T

        def products(s):
            b_cols = columns_of(b_refs, b_rows, whole[s])
            held = pl.ds(pl.multiple_of((t * subs + s) * size, size), size)
            both = jnp.dot(
                c_rows[local[s]],
                jnp.concatenate([b_cols, state_ref[held]], axis=1),
                preferred_element_type=F32,
            )
            scores[local[s]] = jnp.where(causal, both[:, :SUB], 0.0)
            carried[local[s]] = both[:, SUB:]

        turn(0)
        turn(1)
        products(0)
        for s, at in enumerate(whole):
            if s + 2 < subs:
                turn(s + 2)
            if s + 1 < subs:
                products(s + 1)
            total = None
            score = scores[local[s]]
            for p in range(pairs):
                cols = slice(p * SUB, (p + 1) * SUB)
                mixing = []
                for h in (2 * p, 2 * p + 1):
                    base = factors + (s * heads + h) * groups
                    mixing.append(rows_times(score, lambda g: repeated(factor_ref, base + g)).astype(BF16))
                xs = xs_ref[at, cols]
                mixed = jnp.dot(
                    jnp.concatenate(mixing, axis=1),
                    jnp.concatenate([xs * keep_low, xs * keep_high], axis=0),
                    preferred_element_type=F32,
                )
                base = starts + s * groups
                before = rows_times(carried[local[s], cols], lambda g: repeated(start_ref.at[p], base + g))
                gated = gate_ref[at, cols] * (mixed + before)
                gated_ref[at, cols] = gated.astype(BF16)
                square = gated * gated
                total = square if total is None else total + square
            squares[local[s]] = total.astype(BF16)
        sums = lax.dot_general(
            jnp.ones((8, SUB), BF16), squares[...], (((1,), (1,)), ((), ())), preferred_element_type=F32
        )
        square_ref[pl.ds(row, subs)] = jnp.concatenate([sums[:1, at] for at in local], axis=0)
        return 0

    lax.fori_loop(*span, tile, 0)


def scan(span, gate, factor, start, xs, states, b_pieces, b_rows, c_pieces, c_rows, c_begins, filled=()):
    length, width = xs.shape
    size = sum(last - first for first, last in b_rows)
    pieces = []
    for piece in b_pieces + c_pieces:
        if not any(piece is other for other in pieces):
            pieces.append(piece)
    picks = lambda some: [next(i for i, q in enumerate(pieces) if q is p) for p in some]
    operands = [gate, factor, start, xs, states, *pieces, *filled]
    first = len(operands) - len(filled)
    return pl.pallas_call(
        functools.partial(
            scan_kernel, span, b_rows, picks(b_pieces), c_rows, picks(c_pieces), c_begins
        ),
        in_specs=[IN_VMEM] * len(operands),
        out_specs=[IN_VMEM, IN_VMEM],
        out_shape=[pltpu.VMEM((length, width), BF16), pltpu.VMEM((length // SUB, SUB), F32)],
        scratch_shapes=[
            pltpu.VMEM((TILE, size), BF16),
            pltpu.VMEM((TILE, SUB), F32),
            pltpu.VMEM((TILE, width), F32),
            pltpu.VMEM((TILE, SUB), BF16),
        ],
        input_output_aliases={first + i: i for i in range(len(filled))},
        compiler_params=params(),
        cost_estimate=BRIEF,
        name="scan",
    )(*in_vmem(operands))


def norm_kernel(channels, gated_ref, gain_ref, *refs):
    squares, (out_ref, rows, sems) = refs[:-3], refs[-3:]
    total = squares[0][...]
    for ref in squares[1:]:
        total = total + ref[...]
    scale = lax.rsqrt(total * (1.0 / channels) + 1e-05).T
    gain = gain_ref[...]
    step = TILE // 2
    copies = []
    for t in range(gated_ref.shape[0] // step):
        for s in range(t * step // SUB, (t + 1) * step // SUB):
            at = slice(s * SUB, (s + 1) * SUB)
            rows[at] = (gated_ref[at].astype(F32) * scale[:, s : s + 1] * gain).astype(BF16)
        at = slice(t * step, (t + 1) * step)
        copies.append(pltpu.make_async_copy(rows.at[at], out_ref.at[at], sems.at[t]))
        copies[-1].start()
    for copy in copies:
        copy.wait()


def norm(channels, gated, gain, squares):
    length, width = gated.shape
    operands = [gated, gain, *squares]
    return pl.pallas_call(
        functools.partial(norm_kernel, channels),
        in_specs=[IN_VMEM] * len(operands),
        out_specs=ANYWHERE,
        out_shape=pltpu.HBM((length, width), BF16),
        scratch_shapes=[
            pltpu.VMEM((length, width), BF16),
            pltpu.SemaphoreType.DMA((2 * length // TILE,)),
        ],
        compiler_params=params(),
        cost_estimate=BRIEF,
        name="norm",
    )(*in_vmem(operands))


def body(x_rows, z_rows, b_rows, c_rows, step_raw, conv_x, conv_b, conv_c, decay_rate, norm_gain):
    length, width = x_rows.shape
    local_heads = decay_rate.shape[0]
    seq, heads = lax.axis_size("seq"), lax.axis_size("head")
    b_cols, c_cols = b_rows.T, c_rows.T
    ahead = lambda d: [(s, s + d) for s in range(seq - d)]
    ends, b_cols, c_cols = tails(x_rows, b_cols, c_cols)
    halo = lax.ppermute(ends, "seq", ahead(1))
    bs, cs, cs_sent = shared_conv(b_cols, c_cols, halo, conv_b.T.astype(F32), conv_c.T.astype(F32))
    cols = bs.shape[0]
    outer, _ = factors(heads)
    tiles = x_rows.shape[0] // TILE
    q, columns, decays = rows_of(step_raw.T, decay_rate[:, None], width)
    conv = functools.partial(head_conv, x_rows, halo, conv_x.astype(F32), columns, local_heads)
    if cols % 16 or factors(heads) != (4, 2):
        b_pieces, c_pieces = [
            [jnp.concatenate(near + along_inner(near), axis=0)]
            for near in ([own] + along_outer(own) for own in (bs, cs))
        ]
        b_rows = c_rows = [(0, b_pieces[0].shape[0])]
        xs, weighted = conv(0, tiles)
        mine, local, before = last_state(weighted, decays, b_pieces, b_rows)
        gate, factor, start = gates(z_rows, columns, q, local_heads)
        token, tail, runs = mine, [], [((0, tiles), None, None)]
    else:
        one, two = (0, cols), (0, 2 * cols)
        b_outer, own = along_outer(bs), along_inner([bs])
        xs, weighted = conv(0, tiles)
        (b_packed,) = pack(b_outer, [one] * 3, xs, *own)
        b_passed = along_inner([b_packed])
        cs_sent, columns = after([cs_sent, columns], b_packed)
        c_outer = along_outer(cs_sent)
        gate, factor, start = gates(z_rows, columns, q, local_heads)
        (c_first,) = pack([cs, c_outer[0]], [one] * 2, start)
        c_passed = along_inner([c_first])
        (decays,) = after([decays], c_first)
        b_pieces = [bs, *own, *b_outer, *b_passed]
        b_rows = [one] * 5 + [(0, 3 * cols)]
        mine, local, before = last_state(weighted, decays, b_pieces, b_rows)
        cut = -(-tiles // 2) * TILE
        c_rest = pack(c_outer[1:], [one] * 2, mine, cuts=[0, cut, length])
        c_ends = along_inner(c_rest)
        c_pieces = [cs, *c_passed, *c_outer, *c_passed]
        c_rows = [one] * 5 + [(cols, 2 * cols)]
        token, tail = c_rest[0], [two]
        runs = [((0, cut // TILE), c_ends[0], 0), ((cut // TILE, tiles), c_ends[1], cut)]
    earlier, reach, ends = [], 1, mine
    while True:
        earlier.append(lax.ppermute(ends, "seq", ahead(reach)))
        reach *= 2
        if reach >= seq:
            break
        ends = join(earlier[-1], ends, token)
    states = enter(local, before, earlier)
    filled = ()
    for span, piece, begin in runs:
        filled = scan(
            span, gate, factor, start, xs, states, b_pieces, b_rows,
            c_pieces + [piece] * len(tail), c_rows + tail, [0] * len(c_pieces) + [begin], filled,
        )
    gated, square = filled
    square = square + sum(along_outer(square))
    squares = [square] + along_inner([square])
    return norm(heads * width, gated, norm_gain[None, :], squares)


def solution(mesh):
    placed = (
        P("seq", "head"),
        P("seq", "head"),
        P("seq", "head"),
        P("seq", "head"),
        P("seq", "head"),
        P(None, "head"),
        P(None, "head"),
        P(None, "head"),
        P("head"),
        P("head"),
    )
    return jax.shard_map(
        body, mesh=mesh, in_specs=placed, out_specs=P("seq", "head"), check_vma=False
    )
```

time: 363 us -> 72.5 us (0.20)
  other arithmetic: 104 us -> 0.01 us
  blocking collectives: 87.9 us -> 0 us
  matrix products: 79.7 us -> 0 us
  local copies, waits for them, and re-layouts: 61.2 us -> 0.3 us
  starting transfers between devices: 2.39 us -> 35.3 us
  Pallas kernels: 0 us -> 25.2 us
  between operations: 14.2 us -> 0.18 us
    dot_general x61 -> x0, matrix products: 79.7 us -> none  [the longest x20 30.6 us: block_parts(): jnp.einsum('hts,shp->thp', mixing, x_block, preferred_element_type=jnp.fl...]
    all_gather x3 -> x0, blocking collectives: 47.3 us -> none  [the longest x1 21.9 us: body(): lax.all_gather(conv_c, 'head', axis=1, tiled=True)]
    another operation x42 -> x0, other arithmetic: 37.4 us -> none
    psum x1 -> x0, blocking collectives: 34.8 us -> none  [body(): total = lax.psum(jnp.sum(gated * gated, axis=1), 'head')]
    ppermute x1 -> x18, starting transfers between devices: 2.34 us -> 35.3 us  [the longest x9 18.8 us: along_outer(): lax.ppermute(piece, 'head', outer_pairs(d))]
    convert_element_type x4 -> x1, other arithmetic: 30.3 us -> 0.01 us  [body(): conv_x.astype(F32)]
    pallas_call x0 -> x16, Pallas kernels: none -> 25.2 us  [the longest x1 6.83 us: head_conv(): pl.pallas_call(functools.partial(head_conv_kernel, first, heads), grid=(c...]
    dynamic_update_slice x40 -> x0, local copies, waits for them, and re-layouts: 15.8 us -> none  [body(): last_state, (diags, local_states, cums) = lax.scan(advance, start, pieces)]
  transfers between devices with their start and end apart: 3 -> 18, of which waited for: 2 -> 9; matrix products, arithmetic and copies ran while one was open for 12% -> 0% of each run, Pallas kernels for 0% -> 26%
where the time goes in v1:
time: 72.5 us; the launch traced here: 72.2 us
  starting transfers between devices  35.3 us (49%)
  Pallas kernels  25.2 us (35%)
  waiting for transfers between devices  11.2 us (15%)
    ppermute x9, starting transfers between devices, along_outer(): lax.ppermute(piece, 'head', outer_pairs(d))  18.8 us
    ppermute x6, starting transfers between devices, along_inner(): lax.ppermute(p, 'head', inner_pairs(e))  7.72 us
    pallas_call x1, Pallas kernels, head_conv(): pl.pallas_call(functools.partial(head_conv_kernel, first, heads), grid=(c...  6.83 us
    pallas_call x2, Pallas kernels, scan(): pl.pallas_call(functools.partial(scan_kernel, span, b_rows, picks(b_piece...  6.82 us
    ppermute x2, starting transfers between devices, body(): earlier.append(lax.ppermute(ends, 'seq', ahead(reach)))  6.31 us
    ppermute x9, waiting for transfers between devices, along_outer(): lax.ppermute(piece, 'head', outer_pairs(d))  4.46 us
    ppermute x6, waiting for transfers between devices, along_inner(): lax.ppermute(p, 'head', inner_pairs(e))  3.8 us
    pallas_call x1, Pallas kernels, gates(): pl.pallas_call(gates_kernel, grid=(length // TILE,), in_specs=[wide, pl.B...  3.14 us
  transfers between devices with their start and end apart: 18, of which 9 were waited for; matrix products, arithmetic and copies ran while one was open for 0% of the time, Pallas kernels for 26%

profile of v1, /device:TPU:0, one launch (start us, length us, event | category | flops | bytes accessed | tf_op | source)
XLA Modules:
  0.0 72.2 jit_solution(15716743256841507068)
XLA Ops:
  0.0 0.0 copy-start.4
  0.0 0.0 copy-start.5
  0.0 0.0 copy-start.6
  0.0 0.0 copy-start.1
  0.0 0.0 copy-start.2
  0.0 1.1 %tails.1 = (bf16[48,384]{1,0:T(8,128)(2,1)S(1)}, bf16[16,5120]{1,0:T(8,128)(2,1)S(1)}, bf16[16,5120]{1,0:T(8,128)(2,1)S(1)}) custom-call(bf16[5120,384]{1,0:T(8,128)(2,1)} %before_ref.1, bf16[16,5120]{1,0:T(8,128)(2,1)} %bitcast.9, bf16[16,5120]{1,0:T(8,128)(2,1)} %bitcast.10), custom_call_target="tpu_custom_call" | custom-call | flops 1000 | bytes 1000 | tf_op jit(solution)/shard_map/tails/pallas_call | solution.py:124
  1.1 2.4 %collective-permute-start = (bf16[48,384]{1,0:T(8,128)(2,1)S(1)}, bf16[48,384]{1,0:T(8,128)(2,1)S(1)}, u32[]{:S(2)}, u32[]{:S(2)}) collective-permute-start(bf16[48,384]{1,0:T(8,128)(2,1)S(1)} %get-tuple-element.32), channel_id=1, source_target_pairs={{0,8},{8,16},{16,24},{1,9},{9,17},{17,25},{2,10},{10,18},{18,26},{... | collective-permute-start | bytes 110600 | tf_op jit(solution)/shard_map/ppermute | solution.py:631
  3.5 0.0 copy-done.4
  3.5 0.1 copy.19
  3.6 0.0 copy-done.5
  3.6 0.1 copy.20
  3.7 0.7 collective-permute-done.halo_ref
  4.4 0.6 shared_conv.1
  5.0 2.5 %collective-permute-start.1 = (bf16[16,5120]{1,0:T(8,128)(2,1)S(1)}, bf16[16,5120]{1,0:T(8,128)(2,1)S(1)}, u32[]{:S(2)}, u32[]{:S(2)}) collective-permute-start(bf16[16,5120]{1,0:T(8,128)(2,1)S(1)} %get-tuple-element.35.refs_0_), channel_id=1, source_target_pairs={{0,2},{1,3},{2,4},{3,5},{4,6},{5,7},{6,0},{7,1},{8,10},{9,11},{10,... | collective-permute-start | bytes 491528 | tf_op jit(solution)/shard_map/ppermute | solution.py:58
  7.4 2.6 %collective-permute-start.2 = (bf16[16,5120]{1,0:T(8,128)(2,1)S(1)}, bf16[16,5120]{1,0:T(8,128)(2,1)S(1)}, u32[]{:S(2)}, u32[]{:S(2)}) collective-permute-start(bf16[16,5120]{1,0:T(8,128)(2,1)S(1)} %get-tuple-element.35.refs_0_), channel_id=1, source_target_pairs={{0,4},{1,5},{2,6},{3,7},{4,0},{5,1},{6,2},{7,3},{8,12},{9,13},{10,... | collective-permute-start | bytes 491528 | tf_op jit(solution)/shard_map/ppermute | solution.py:58
  10.0 1.3 %collective-permute-start.3 = (bf16[16,5120]{1,0:T(8,128)(2,1)S(1)}, bf16[16,5120]{1,0:T(8,128)(2,1)S(1)}, u32[]{:S(2)}, u32[]{:S(2)}) collective-permute-start(bf16[16,5120]{1,0:T(8,128)(2,1)S(1)} %get-tuple-element.35.refs_0_), channel_id=1, source_target_pairs={{0,6},{1,7},{2,0},{3,1},{4,2},{5,3},{6,4},{7,5},{8,14},{9,15},{10,... | collective-permute-start | bytes 491528 | tf_op jit(solution)/shard_map/ppermute | solution.py:58
  11.4 1.5 %collective-permute-start.4 = (bf16[16,5120]{1,0:T(8,128)(2,1)S(1)}, bf16[16,5120]{1,0:T(8,128)(2,1)S(1)}, u32[]{:S(2)}, u32[]{:S(2)}) collective-permute-start(bf16[16,5120]{1,0:T(8,128)(2,1)S(1)} %get-tuple-element.35.refs_0_), channel_id=1, source_target_pairs={{0,1},{1,0},{2,3},{3,2},{4,5},{5,4},{6,7},{7,6},{8,9},{9,8},{10,11... | collective-permute-start | bytes 491528 | tf_op jit(solution)/shard_map/ppermute | solution.py:63
  12.9 0.0 copy-done.6
  12.9 0.1 copy.21.rate_ref
  13.0 0.0 copy-done.1
  13.0 1.3 %rows.1 = (f32[8,5120]{1,0:T(8,128)S(1)}, bf16[5120,40]{1,0:T(8,128)(2,1)S(1)}, f32[40,384]{1,0:T(8,128)S(1)}) custom-call(f32[6,5120]{1,0:T(8,128)S(1)} %bitcast.6, f32[6,1]{1,0:T(8,128)S(1)} %copy.21.rate_ref), custom_call_target="tpu_custom_call" | custom-call | flops 1000 | bytes 1000 | tf_op jit(solution)/shard_map/rows/pallas_call | solution.py:219
  14.3 0.0 copy-done.2
  14.3 6.8 %head_conv.1 = (bf16[5120,384]{1,0:T(8,128)(2,1)S(1)}, bf16[5120,384]{1,0:T(8,128)(2,1)S(1)}) custom-call(bf16[5120,384]{1,0:T(8,128)(2,1)} %before_ref.1, bf16[5120,384]{1,0:T(8,128)(2,1)} %before_ref.1, bf16[48,384]{1,0:T(8,128)(2,1)S(1)} %collective-permute-done.halo_ref, f32[4,384]{1,0:T(4,128)S(1)} %convert_element_type.17.taps_ref, ...), custom_call_target="tpu_custom_call" | custom-call | flops 1000 | bytes 1000 | tf_op jit(solution)/shard_map/head_conv/pallas_call | solution.py:275
  21.1 0.0 copy-start
  21.1 0.0 collective-permute-done.1.refs_0_.refs_2_
  21.2 0.4 collective-permute-done.2.refs_1_.refs_3_
  21.6 0.0 collective-permute-done.3.refs_2_.refs_4_
  21.6 0.0 collective-permute-done.4.refs_4_.refs_1_
  21.6 1.7 %collective-permute-start.6 = (bf16[48,5120]{1,0:T(8,128)(2,1)S(1)}, bf16[48,5120]{1,0:T(8,128)(2,1)S(1)}, u32[]{:S(2)}, u32[]{:S(2)}) collective-permute-start(bf16[48,5120]{1,0:T(8,128)(2,1)S(1)} %pack.3.refs_2_), channel_id=1, source_target_pairs={{0,1},{1,0},{2,3},{3,2},{4,5},{5,4},{6,7},{7,6},{8,9},{9,8},{10,11... | collective-permute-start | bytes 1474568 | tf_op jit(solution)/shard_map/ppermute | solution.py:63
  23.3 4.1 %collective-permute-start.5 = (bf16[16,5120]{1,0:T(8,128)(2,1)S(1)}, bf16[16,5120]{1,0:T(8,128)(2,1)S(1)}, u32[]{:S(2)}, u32[]{:S(2)}) collective-permute-start(bf16[16,5120]{1,0:T(8,128)(2,1)S(1)} %get-tuple-element.45), channel_id=1, source_target_pairs={{0,2},{1,3},{2,4},{3,5},{4,6},{5,7},{6,0},{7,1},{8,10},{9,11},{10,... | collective-permute-start | bytes 491528 | tf_op jit(solution)/shard_map/ppermute | solution.py:58
  27.4 0.8 %collective-permute-start.8 = (bf16[16,5120]{1,0:T(8,128)(2,1)S(1)}, bf16[16,5120]{1,0:T(8,128)(2,1)S(1)}, u32[]{:S(2)}, u32[]{:S(2)}) collective-permute-start(bf16[16,5120]{1,0:T(8,128)(2,1)S(1)} %get-tuple-element.45), channel_id=1, source_target_pairs={{0,4},{1,5},{2,6},{3,7},{4,0},{5,1},{6,2},{7,3},{8,12},{9,13},{10,... | collective-permute-start | bytes 491528 | tf_op jit(solution)/shard_map/ppermute | solution.py:58
  28.1 1.6 %collective-permute-start.9 = (bf16[16,5120]{1,0:T(8,128)(2,1)S(1)}, bf16[16,5120]{1,0:T(8,128)(2,1)S(1)}, u32[]{:S(2)}, u32[]{:S(2)}) collective-permute-start(bf16[16,5120]{1,0:T(8,128)(2,1)S(1)} %get-tuple-element.45), channel_id=1, source_target_pairs={{0,6},{1,7},{2,0},{3,1},{4,2},{5,3},{6,4},{7,5},{8,14},{9,15},{10,... | collective-permute-start | bytes 491528 | tf_op jit(solution)/shard_map/ppermute | solution.py:58
  29.7 0.0 copy-done
  29.8 3.1 %gates.1 = (f32[5120,384]{1,0:T(8,128)S(1)}, f32[1920,128]{1,0:T(8,128)S(1)}, f32[3,320,128]{2,1,0:T(8,128)S(1)}) custom-call(bf16[5120,384]{1,0:T(8,128)(2,1)S(1)} %copy-done, bf16[5120,40]{1,0:T(8,128)(2,1)S(1)} %get-tuple-element.37.column_ref, f32[8,5120]{1,0:T(8,128)S(1)} %get-tuple-element.38.q_ref), custom_call_target="tpu_custom_call" | custom-call | flops 1000 | bytes 1000 | tf_op jit(solution)/shard_map/gates/pallas_call | solution.py:334
  32.9 0.0 collective-permute-done.5.refs_1_.refs_8_
  32.9 0.4 collective-permute-start.11
  33.4 1.9 %collective-permute-done.6.refs_5_ = bf16[48,5120]{1,0:T(8,128)(2,1)S(1)} collective-permute-done((bf16[48,5120]{1,0:T(8,128)(2,1)S(1)}, bf16[48,5120]{1,0:T(8,128)(2,1)S(1)}, u32[]{:S(2)}, u32[]{:S(2)}) %collective-permute-start.6) | collective-permute-done | bytes 491552 | tf_op jit(solution)/shard_map/ppermute | solution.py:63
  35.3 1.9 %last_state.1 = (bf16[144,384]{1,0:T(8,128)(2,1)S(1)}, f32[5120,384]{1,0:T(8,128)S(1)}, f32[40,384]{1,0:T(8,128)S(1)}) custom-call(bf16[5120,384]{1,0:T(8,128)(2,1)S(1)} %get-tuple-element.42.wt_ref, f32[40,384]{1,0:T(8,128)S(1)} %tie.3.decay_ref, bf16[16,5120]{1,0:T(8,128)(2,1)S(1)} %get-tuple-element.35.refs_0_, ...), custom_call_target="tpu_custom_call" | custom-call | flops 1000 | bytes 1000 | tf_op jit(solution)/shard_map/last_state/pallas_call | solution.py:401
  37.2 1.6 %collective-permute-start.7 = (bf16[144,384]{1,0:T(8,128)(2,1)S(1)}, bf16[144,384]{1,0:T(8,128)(2,1)S(1)}, u32[]{:S(2)}, u32[]{:S(2)}) collective-permute-start(bf16[144,384]{1,0:T(8,128)(2,1)S(1)} %get-tuple-element.48.refs_2_.late_ref), channel_id=1, source_target_pairs={{0,8},{8,16},{16,24},{1,9},{9,17},{17,25},{2,10},{10,18},{18,26},{... | collective-permute-start | bytes 331784 | tf_op jit(solution)/shard_map/ppermute | solution.py:672
  38.8 0.8 %collective-permute-done.8.refs_0_.refs_9_ = bf16[16,5120]{1,0:T(8,128)(2,1)S(1)} collective-permute-done((bf16[16,5120]{1,0:T(8,128)(2,1)S(1)}, bf16[16,5120]{1,0:T(8,128)(2,1)S(1)}, u32[]{:S(2)}, u32[]{:S(2)}) %collective-permute-start.8) | collective-permute-done | bytes 163872 | tf_op jit(solution)/shard_map/ppermute | solution.py:58
  39.6 0.0 collective-permute-done.9.refs_1_.refs_10_
  39.7 1.1 %collective-permute-start.13 = (bf16[32,3072]{1,0:T(8,128)(2,1)S(1)}, bf16[32,3072]{1,0:T(8,128)(2,1)S(1)}, u32[]{:S(2)}, u32[]{:S(2)}) collective-permute-start(bf16[32,3072]{1,0:T(8,128)(2,1)S(1)} %get-tuple-element.49.token_ref), channel_id=1, source_target_pairs={{0,1},{1,0},{2,3},{3,2},{4,5},{5,4},{6,7},{7,6},{8,9},{9,8},{10,11... | collective-permute-start | bytes 589832 | tf_op jit(solution)/shard_map/ppermute | solution.py:63
  40.7 1.0 %collective-permute-start.12 = (bf16[32,2048]{1,0:T(8,128)(2,1)S(1)}, bf16[32,2048]{1,0:T(8,128)(2,1)S(1)}, u32[]{:S(2)}, u32[]{:S(2)}) collective-permute-start(bf16[32,2048]{1,0:T(8,128)(2,1)S(1)} %get-tuple-element.50), channel_id=1, source_target_pairs={{0,1},{1,0},{2,3},{3,2},{4,5},{5,4},{6,7},{7,6},{8,9},{9,8},{10,11... | collective-permute-start | bytes 393224 | tf_op jit(solution)/shard_map/ppermute | solution.py:63
  41.8 0.0 collective-permute-done.7.early_ref.refs_0_
  41.8 4.7 %collective-permute-start.10 = (bf16[144,384]{1,0:T(8,128)(2,1)S(1)}, bf16[144,384]{1,0:T(8,128)(2,1)S(1)}, u32[]{:S(2)}, u32[]{:S(2)}) collective-permute-start(bf16[144,384]{1,0:T(8,128)(2,1)S(1)} %join.1), channel_id=1, source_target_pairs={{0,16},{8,24},{1,17},{9,25},{2,18},{10,26},{3,19},{11,27},{4,20},{... | collective-permute-start | bytes 331784 | tf_op jit(solution)/shard_map/ppermute | solution.py:672
  46.5 2.3 %collective-permute-done.10.refs_1_ = bf16[144,384]{1,0:T(8,128)(2,1)S(1)} collective-permute-done((bf16[144,384]{1,0:T(8,128)(2,1)S(1)}, bf16[144,384]{1,0:T(8,128)(2,1)S(1)}, u32[]{:S(2)}, u32[]{:S(2)}) %collective-permute-start.10) | collective-permute-done | bytes 110624 | tf_op jit(solution)/shard_map/ppermute | solution.py:672
  48.9 1.1 %enter.1.state_ref = bf16[5120,384]{1,0:T(8,128)(2,1)S(1)} custom-call(f32[5120,384]{1,0:T(8,128)S(1)} %get-tuple-element.46.local_ref, f32[40,384]{1,0:T(8,128)S(1)} %get-tuple-element.47.before_ref, bf16[144,384]{1,0:T(8,128)(2,1)S(1)} %collective-permute-done.7.early_ref.refs_0_, bf16[144,384]{1,0:T(8,128)(2,1)S(1)} %collective-permute-done.10.refs_1_), custom_call_target="tpu_custom_call" | custom-call | flops 1000 | bytes 1000 | tf_op jit(solution)/shard_map/enter/pallas_call | solution.py:462
  50.0 0.0 collective-permute-done.11.refs_7_
  50.0 0.0 collective-permute-done.13.refs_11_
  50.0 4.1 %scan.2 = (bf16[5120,384]{1,0:T(8,128)(2,1)S(1)}, f32[40,128]{1,0:T(8,128)S(1)}) custom-call(f32[5120,384]{1,0:T(8,128)S(1)} %get-tuple-element.39.gate_ref, f32[1920,128]{1,0:T(8,128)S(1)} %get-tuple-element.40.factor_ref, f32[3,320,128]{2,1,0:T(8,128)S(1)} %get-tuple-element.41.refs_2_.start_ref, bf16[5120,384]{1,0:T(8,128)(2,1)S(1)} %get-tuple-element.36.refs_3_.xs_ref, ...), custom_call_target="tpu_custom_call" | custom-call | flops 1000 | bytes 1000 | tf_op jit(solution)/shard_map/scan/pallas_call | solution.py:566
  54.1 0.0 collective-permute-done.12.refs_11_
  54.1 0.0 copy-start.3
  54.1 2.7 %scan.3 = (bf16[5120,384]{1,0:T(8,128)(2,1)S(1)}, f32[40,128]{1,0:T(8,128)S(1)}) custom-call(f32[5120,384]{1,0:T(8,128)S(1)} %get-tuple-element.39.gate_ref, f32[1920,128]{1,0:T(8,128)S(1)} %get-tuple-element.40.factor_ref, f32[3,320,128]{2,1,0:T(8,128)S(1)} %get-tuple-element.41.refs_2_.start_ref, ...), custom_call_target="tpu_custom_call", output_to_operand_aliasing={{0}: (17, {}), {1}: (18, {})} | custom-call | flops 1000 | bytes 1000 | tf_op jit(solution)/shard_map/scan/pallas_call | solution.py:566
  56.8 3.3 %collective-permute-start.16 = (f32[40,128]{1,0:T(8,128)S(1)}, f32[40,128]{1,0:T(8,128)S(1)}, u32[]{:S(2)}, u32[]{:S(2)}) collective-permute-start(f32[40,128]{1,0:T(8,128)S(1)} %get-tuple-element.54), channel_id=1, source_target_pairs={{0,6},{1,7},{2,0},{3,1},{4,2},{5,3},{6,4},{7,5},{8,14},{9,15},{10,... | collective-permute-start | bytes 61448 | tf_op jit(solution)/shard_map/ppermute | solution.py:58
  60.1 1.2 %collective-permute-start.14 = (f32[40,128]{1,0:T(8,128)S(1)}, f32[40,128]{1,0:T(8,128)S(1)}, u32[]{:S(2)}, u32[]{:S(2)}) collective-permute-start(f32[40,128]{1,0:T(8,128)S(1)} %get-tuple-element.54), channel_id=1, source_target_pairs={{0,2},{1,3},{2,4},{3,5},{4,6},{5,7},{6,0},{7,1},{8,10},{9,11},{10,... | collective-permute-start | bytes 61448 | tf_op jit(solution)/shard_map/ppermute | solution.py:58
  61.4 1.5 %collective-permute-start.15 = (f32[40,128]{1,0:T(8,128)S(1)}, f32[40,128]{1,0:T(8,128)S(1)}, u32[]{:S(2)}, u32[]{:S(2)}) collective-permute-start(f32[40,128]{1,0:T(8,128)S(1)} %get-tuple-element.54), channel_id=1, source_target_pairs={{0,4},{1,5},{2,6},{3,7},{4,0},{5,1},{6,2},{7,3},{8,12},{9,13},{10,... | collective-permute-start | bytes 61448 | tf_op jit(solution)/shard_map/ppermute | solution.py:58
  62.8 0.3 collective-permute-done.16
  63.1 2.6 %collective-permute-done.14 = f32[40,128]{1,0:T(8,128)S(1)} collective-permute-done((f32[40,128]{1,0:T(8,128)S(1)}, f32[40,128]{1,0:T(8,128)S(1)}, u32[]{:S(2)}, u32[]{:S(2)}) %collective-permute-start.14) | collective-permute-done | bytes 20512 | tf_op jit(solution)/shard_map/ppermute | solution.py:58
  65.7 0.3 collective-permute-done.15
  66.1 2.0 %collective-permute-start.17 = (f32[40,128]{1,0:T(8,128)S(1)}, f32[40,128]{1,0:T(8,128)S(1)}, u32[]{:S(2)}, u32[]{:S(2)}) collective-permute-start(f32[40,128]{1,0:T(8,128)S(1)} %add_add_fusion.refs_0_), channel_id=1, source_target_pairs={{0,1},{1,0},{2,3},{3,2},{4,5},{5,4},{6,7},{7,6},{8,9},{9,8},{10,11... | collective-permute-start | bytes 61448 | tf_op jit(solution)/shard_map/ppermute | solution.py:63
  68.1 0.0 copy-done.3
  68.1 1.8 %collective-permute-done.17.refs_1_ = f32[40,128]{1,0:T(8,128)S(1)} collective-permute-done((f32[40,128]{1,0:T(8,128)S(1)}, f32[40,128]{1,0:T(8,128)S(1)}, u32[]{:S(2)}, u32[]{:S(2)}) %collective-permute-start.17) | collective-permute-done | bytes 20512 | tf_op jit(solution)/shard_map/ppermute | solution.py:63
  69.9 2.3 %norm.1 = bf16[5120,384]{1,0:T(8,128)(2,1)} custom-call(bf16[5120,384]{1,0:T(8,128)(2,1)S(1)} %get-tuple-element.53.gated_ref, f32[1,384]{1,0:T(1,128)S(1)} %broadcast_in_dim.7.gain_ref, f32[40,128]{1,0:T(8,128)S(1)} %add_add_fusion.refs_0_, f32[40,128]{1,0:T(8,128)S(1)} %collective-permute-done.17.refs_1_), custom_call_target="tpu_custom_call" | custom-call | flops 1000 | bytes 1000 | tf_op jit(solution)/shard_map/norm/pallas_call | solution.py:609
  (9 shorter events, 0.1 us)
Async XLA Ops:
  0.0 3.5 %copy-start.4 = (bf16[4,16]{1,0:T(4,128)(2,1)S(1)}, bf16[4,16]{1,0:T(4,128)(2,1)}, u32[]{:S(2)}) copy-start(bf16[4,16]{1,0:T(4,128)(2,1)} %param.16) | copy-start | bytes 388
  0.0 3.6 %copy-start.5 = (bf16[4,16]{1,0:T(4,128)(2,1)S(1)}, bf16[4,16]{1,0:T(4,128)(2,1)}, u32[]{:S(2)}) copy-start(bf16[4,16]{1,0:T(4,128)(2,1)} %param.17) | copy-start | bytes 388
  0.0 12.9 %copy-start.6 = (f32[6]{0:T(128)S(1)}, f32[6]{0:T(128)}, u32[]{:S(2)}) copy-start(f32[6]{0:T(128)} %param.18) | copy-start | bytes 76
  0.0 13.0 %copy-start.1 = (f32[5120,6]{0,1:T(8,128)S(1)}, f32[5120,6]{0,1:T(8,128)}, u32[]{:S(2)}) copy-start(f32[5120,6]{0,1:T(8,128)} %param.14) | copy-start | bytes 368644
  0.0 14.3 %copy-start.2 = (bf16[4,384]{1,0:T(4,128)(2,1)S(1)}, bf16[4,384]{1,0:T(4,128)(2,1)}, u32[]{:S(2)}) copy-start(bf16[4,384]{1,0:T(4,128)(2,1)} %param.15) | copy-start | bytes 9220
  1.1 3.2 %collective-permute-start = (bf16[48,384]{1,0:T(8,128)(2,1)S(1)}, bf16[48,384]{1,0:T(8,128)(2,1)S(1)}, u32[]{:S(2)}, u32[]{:S(2)}) collective-permute-start(bf16[48,384]{1,0:T(8,128)(2,1)S(1)} %get-tuple-element.32), channel_id=1, source_target_pairs={{0,8},{8,16},{16,24},{1,9},{9,17},{17,25},{2,10},{10,18},{18,26},{... | collective-permute-start | bytes 110600 | tf_op jit(solution)/shard_map/ppermute | solution.py:631
  5.0 16.2 %collective-permute-start.1 = (bf16[16,5120]{1,0:T(8,128)(2,1)S(1)}, bf16[16,5120]{1,0:T(8,128)(2,1)S(1)}, u32[]{:S(2)}, u32[]{:S(2)}) collective-permute-start(bf16[16,5120]{1,0:T(8,128)(2,1)S(1)} %get-tuple-element.35.refs_0_), channel_id=1, source_target_pairs={{0,2},{1,3},{2,4},{3,5},{4,6},{5,7},{6,0},{7,1},{8,10},{9,11},{10,... | collective-permute-start | bytes 491528 | tf_op jit(solution)/shard_map/ppermute | solution.py:58
  7.4 14.1 %collective-permute-start.2 = (bf16[16,5120]{1,0:T(8,128)(2,1)S(1)}, bf16[16,5120]{1,0:T(8,128)(2,1)S(1)}, u32[]{:S(2)}, u32[]{:S(2)}) collective-permute-start(bf16[16,5120]{1,0:T(8,128)(2,1)S(1)} %get-tuple-element.35.refs_0_), channel_id=1, source_target_pairs={{0,4},{1,5},{2,6},{3,7},{4,0},{5,1},{6,2},{7,3},{8,12},{9,13},{10,... | collective-permute-start | bytes 491528 | tf_op jit(solution)/shard_map/ppermute | solution.py:58
  10.0 11.5 %collective-permute-start.3 = (bf16[16,5120]{1,0:T(8,128)(2,1)S(1)}, bf16[16,5120]{1,0:T(8,128)(2,1)S(1)}, u32[]{:S(2)}, u32[]{:S(2)}) collective-permute-start(bf16[16,5120]{1,0:T(8,128)(2,1)S(1)} %get-tuple-element.35.refs_0_), channel_id=1, source_target_pairs={{0,6},{1,7},{2,0},{3,1},{4,2},{5,3},{6,4},{7,5},{8,14},{9,15},{10,... | collective-permute-start | bytes 491528 | tf_op jit(solution)/shard_map/ppermute | solution.py:58
  11.4 10.2 %collective-permute-start.4 = (bf16[16,5120]{1,0:T(8,128)(2,1)S(1)}, bf16[16,5120]{1,0:T(8,128)(2,1)S(1)}, u32[]{:S(2)}, u32[]{:S(2)}) collective-permute-start(bf16[16,5120]{1,0:T(8,128)(2,1)S(1)} %get-tuple-element.35.refs_0_), channel_id=1, source_target_pairs={{0,1},{1,0},{2,3},{3,2},{4,5},{5,4},{6,7},{7,6},{8,9},{9,8},{10,11... | collective-permute-start | bytes 491528 | tf_op jit(solution)/shard_map/ppermute | solution.py:63
  21.1 8.6 %copy-start = (bf16[5120,384]{1,0:T(8,128)(2,1)S(1)}, bf16[5120,384]{1,0:T(8,128)(2,1)}, u32[]{:S(2)}) copy-start(bf16[5120,384]{1,0:T(8,128)(2,1)} %z_ref.1) | copy-start | bytes 11796484
  21.6 13.7 %collective-permute-start.6 = (bf16[48,5120]{1,0:T(8,128)(2,1)S(1)}, bf16[48,5120]{1,0:T(8,128)(2,1)S(1)}, u32[]{:S(2)}, u32[]{:S(2)}) collective-permute-start(bf16[48,5120]{1,0:T(8,128)(2,1)S(1)} %pack.3.refs_2_), channel_id=1, source_target_pairs={{0,1},{1,0},{2,3},{3,2},{4,5},{5,4},{6,7},{7,6},{8,9},{9,8},{10,11... | collective-permute-start | bytes 1474568 | tf_op jit(solution)/shard_map/ppermute | solution.py:63
  23.3 9.6 %collective-permute-start.5 = (bf16[16,5120]{1,0:T(8,128)(2,1)S(1)}, bf16[16,5120]{1,0:T(8,128)(2,1)S(1)}, u32[]{:S(2)}, u32[]{:S(2)}) collective-permute-start(bf16[16,5120]{1,0:T(8,128)(2,1)S(1)} %get-tuple-element.45), channel_id=1, source_target_pairs={{0,2},{1,3},{2,4},{3,5},{4,6},{5,7},{6,0},{7,1},{8,10},{9,11},{10,... | collective-permute-start | bytes 491528 | tf_op jit(solution)/shard_map/ppermute | solution.py:58
  27.4 12.2 %collective-permute-start.8 = (bf16[16,5120]{1,0:T(8,128)(2,1)S(1)}, bf16[16,5120]{1,0:T(8,128)(2,1)S(1)}, u32[]{:S(2)}, u32[]{:S(2)}) collective-permute-start(bf16[16,5120]{1,0:T(8,128)(2,1)S(1)} %get-tuple-element.45), channel_id=1, source_target_pairs={{0,4},{1,5},{2,6},{3,7},{4,0},{5,1},{6,2},{7,3},{8,12},{9,13},{10,... | collective-permute-start | bytes 491528 | tf_op jit(solution)/shard_map/ppermute | solution.py:58
  28.1 11.5 %collective-permute-start.9 = (bf16[16,5120]{1,0:T(8,128)(2,1)S(1)}, bf16[16,5120]{1,0:T(8,128)(2,1)S(1)}, u32[]{:S(2)}, u32[]{:S(2)}) collective-permute-start(bf16[16,5120]{1,0:T(8,128)(2,1)S(1)} %get-tuple-element.45), channel_id=1, source_target_pairs={{0,6},{1,7},{2,0},{3,1},{4,2},{5,3},{6,4},{7,5},{8,14},{9,15},{10,... | collective-permute-start | bytes 491528 | tf_op jit(solution)/shard_map/ppermute | solution.py:58
  32.9 17.0 %collective-permute-start.11 = (bf16[32,5120]{1,0:T(8,128)(2,1)S(1)}, bf16[32,5120]{1,0:T(8,128)(2,1)S(1)}, u32[]{:S(2)}, u32[]{:S(2)}) collective-permute-start(bf16[32,5120]{1,0:T(8,128)(2,1)S(1)} %pack.4.refs_1_), channel_id=1, source_target_pairs={{0,1},{1,0},{2,3},{3,2},{4,5},{5,4},{6,7},{7,6},{8,9},{9,8},{10,11... | collective-permute-start | bytes 983048 | tf_op jit(solution)/shard_map/ppermute | solution.py:63
  37.2 4.5 %collective-permute-start.7 = (bf16[144,384]{1,0:T(8,128)(2,1)S(1)}, bf16[144,384]{1,0:T(8,128)(2,1)S(1)}, u32[]{:S(2)}, u32[]{:S(2)}) collective-permute-start(bf16[144,384]{1,0:T(8,128)(2,1)S(1)} %get-tuple-element.48.refs_2_.late_ref), channel_id=1, source_target_pairs={{0,8},{8,16},{16,24},{1,9},{9,17},{17,25},{2,10},{10,18},{18,26},{... | collective-permute-start | bytes 331784 | tf_op jit(solution)/shard_map/ppermute | solution.py:672
  39.7 10.3 %collective-permute-start.13 = (bf16[32,3072]{1,0:T(8,128)(2,1)S(1)}, bf16[32,3072]{1,0:T(8,128)(2,1)S(1)}, u32[]{:S(2)}, u32[]{:S(2)}) collective-permute-start(bf16[32,3072]{1,0:T(8,128)(2,1)S(1)} %get-tuple-element.49.token_ref), channel_id=1, source_target_pairs={{0,1},{1,0},{2,3},{3,2},{4,5},{5,4},{6,7},{7,6},{8,9},{9,8},{10,11... | collective-permute-start | bytes 589832 | tf_op jit(solution)/shard_map/ppermute | solution.py:63
  40.7 13.3 %collective-permute-start.12 = (bf16[32,2048]{1,0:T(8,128)(2,1)S(1)}, bf16[32,2048]{1,0:T(8,128)(2,1)S(1)}, u32[]{:S(2)}, u32[]{:S(2)}) collective-permute-start(bf16[32,2048]{1,0:T(8,128)(2,1)S(1)} %get-tuple-element.50), channel_id=1, source_target_pairs={{0,1},{1,0},{2,3},{3,2},{4,5},{5,4},{6,7},{7,6},{8,9},{9,8},{10,11... | collective-permute-start | bytes 393224 | tf_op jit(solution)/shard_map/ppermute | solution.py:63
  41.8 7.1 %collective-permute-start.10 = (bf16[144,384]{1,0:T(8,128)(2,1)S(1)}, bf16[144,384]{1,0:T(8,128)(2,1)S(1)}, u32[]{:S(2)}, u32[]{:S(2)}) collective-permute-start(bf16[144,384]{1,0:T(8,128)(2,1)S(1)} %join.1), channel_id=1, source_target_pairs={{0,16},{8,24},{1,17},{9,25},{2,18},{10,26},{3,19},{11,27},{4,20},{... | collective-permute-start | bytes 331784 | tf_op jit(solution)/shard_map/ppermute | solution.py:672
  54.1 14.0 %copy-start.3 = (f32[384]{0:T(512)S(1)}, f32[384]{0:T(512)}, u32[]{:S(2)}) copy-start(f32[384]{0:T(512)} %param.19) | copy-start | bytes 4612
  56.8 6.3 %collective-permute-start.16 = (f32[40,128]{1,0:T(8,128)S(1)}, f32[40,128]{1,0:T(8,128)S(1)}, u32[]{:S(2)}, u32[]{:S(2)}) collective-permute-start(f32[40,128]{1,0:T(8,128)S(1)} %get-tuple-element.54), channel_id=1, source_target_pairs={{0,6},{1,7},{2,0},{3,1},{4,2},{5,3},{6,4},{7,5},{8,14},{9,15},{10,... | collective-permute-start | bytes 61448 | tf_op jit(solution)/shard_map/ppermute | solution.py:58
  60.1 5.6 %collective-permute-start.14 = (f32[40,128]{1,0:T(8,128)S(1)}, f32[40,128]{1,0:T(8,128)S(1)}, u32[]{:S(2)}, u32[]{:S(2)}) collective-permute-start(f32[40,128]{1,0:T(8,128)S(1)} %get-tuple-element.54), channel_id=1, source_target_pairs={{0,2},{1,3},{2,4},{3,5},{4,6},{5,7},{6,0},{7,1},{8,10},{9,11},{10,... | collective-permute-start | bytes 61448 | tf_op jit(solution)/shard_map/ppermute | solution.py:58
  61.4 4.7 %collective-permute-start.15 = (f32[40,128]{1,0:T(8,128)S(1)}, f32[40,128]{1,0:T(8,128)S(1)}, u32[]{:S(2)}, u32[]{:S(2)}) collective-permute-start(f32[40,128]{1,0:T(8,128)S(1)} %get-tuple-element.54), channel_id=1, source_target_pairs={{0,4},{1,5},{2,6},{3,7},{4,0},{5,1},{6,2},{7,3},{8,12},{9,13},{10,... | collective-permute-start | bytes 61448 | tf_op jit(solution)/shard_map/ppermute | solution.py:58
  66.1 3.8 %collective-permute-start.17 = (f32[40,128]{1,0:T(8,128)S(1)}, f32[40,128]{1,0:T(8,128)S(1)}, u32[]{:S(2)}, u32[]{:S(2)}) collective-permute-start(f32[40,128]{1,0:T(8,128)S(1)} %add_add_fusion.refs_0_), channel_id=1, source_target_pairs={{0,1},{1,0},{2,3},{3,2},{4,5},{5,4},{6,7},{7,6},{8,9},{9,8},{10,11... | collective-permute-start | bytes 61448 | tf_op jit(solution)/shard_map/ppermute | solution.py:63

commit v2 on v1

--- a/solution.py
+++ b/solution.py
@@ -414,32 +414,35 @@
     )(*in_vmem([weighted, decays, *pieces]))
 
 
-def join_kernel(early_ref, late_ref, token_ref, out_ref):
-    size = late_ref.shape[0] - 16
-    early, late = early_ref[...].astype(F32), late_ref[...].astype(F32)
+def join_kernel(bit, mine_ref, other_ref, token_ref, out_ref):
+    size = mine_ref.shape[0] - 16
+    upper = jnp.bitwise_and(lax.axis_index("seq"), bit) != 0
+    mine, other = mine_ref[...].astype(F32), other_ref[...].astype(F32)
+    early, late = jnp.where(upper, other, mine), jnp.where(upper, mine, other)
     decay = late[size : size + 1]
     out_ref[:size] = (early[:size] * decay + late[:size]).astype(BF16)
     out_ref[size:] = (early[size:] * decay).astype(BF16)
 
 
-def join(early, late, token):
-    return pl.pallas_call(
-        join_kernel,
-        in_specs=[IN_VMEM] * 2 + [ANYWHERE],
+def join(bit, mine, other, token):
+    return pl.pallas_call(
+        functools.partial(join_kernel, bit),
+        in_specs=[IN_VMEM, IN_VMEM, ANYWHERE],
         out_specs=IN_VMEM,
-        out_shape=jax.ShapeDtypeStruct(late.shape, BF16),
+        out_shape=jax.ShapeDtypeStruct(mine.shape, BF16),
         compiler_params=params(),
         cost_estimate=BRIEF,
         name="join",
-    )(*in_vmem([early, late]), token)
+    )(*in_vmem([mine, other]), token)
 
 
 def enter_kernel(local_ref, before_ref, *refs):
-    earlier, (out_ref, state) = refs[:-2], refs[-2:]
+    others, out_ref, state = refs[:-2], refs[-2], refs[-1]
     size = state.shape[0]
     carry = jnp.zeros(state.shape, F32)
-    for ref in reversed(earlier):
-        carry = carry * ref[size : size + 1].astype(F32) + ref[:size].astype(F32)
+    for k in reversed(range(len(others))):
+        longer = carry * others[k][size : size + 1].astype(F32) + others[k][:size].astype(F32)
+        carry = jnp.where(jnp.bitwise_and(lax.axis_index("seq"), 1 << k) != 0, longer, carry)
     state[...] = carry
     some = 8
 
@@ -455,10 +458,10 @@
     lax.fori_loop(0, before_ref.shape[0] // some, group, 0)
 
 
-def enter(local, before, earlier):
+def enter(local, before, others):
     rows, width = local.shape
     size = rows // before.shape[0]
-    operands = [local, before, *earlier]
+    operands = [local, before, *others]
     return pl.pallas_call(
         enter_kernel,
         in_specs=[IN_VMEM] * len(operands),
@@ -626,9 +629,8 @@
     local_heads = decay_rate.shape[0]
     seq, heads = lax.axis_size("seq"), lax.axis_size("head")
     b_cols, c_cols = b_rows.T, c_rows.T
-    ahead = lambda d: [(s, s + d) for s in range(seq - d)]
     ends, b_cols, c_cols = tails(x_rows, b_cols, c_cols)
-    halo = lax.ppermute(ends, "seq", ahead(1))
+    halo = lax.ppermute(ends, "seq", [(i, i + 1) for i in range(seq - 1)])
     bs, cs, cs_sent = shared_conv(b_cols, c_cols, halo, conv_b.T.astype(F32), conv_c.T.astype(F32))
     cols = bs.shape[0]
     outer, _ = factors(heads)
@@ -667,14 +669,15 @@
         c_rows = [one] * 5 + [(cols, 2 * cols)]
         token, tail = c_rest[0], [two]
         runs = [((0, cut // TILE), c_ends[0], 0), ((cut // TILE, tiles), c_ends[1], cut)]
-    earlier, reach, ends = [], 1, mine
-    while True:
-        earlier.append(lax.ppermute(ends, "seq", ahead(reach)))
-        reach *= 2
-        if reach >= seq:
-            break
-        ends = join(earlier[-1], ends, token)
-    states = enter(local, before, earlier)
+    others, bit = [], 1
+    while bit < seq:
+        last = 2 * bit == seq
+        pairs = [(i, i ^ bit) for i in range(seq) if not (last and i & bit)]
+        others.append(lax.ppermute(mine, "seq", pairs))
+        if not last:
+            mine = join(bit, mine, others[-1], token)
+        bit *= 2
+    states = enter(local, before, others)
     filled = ()
     for span, piece, begin in runs:
         filled = scan(

time: 72.5 us -> 72 us (level)
  starting transfers between devices: 35.3 us -> 30 us
  waiting for transfers between devices: 11.2 us -> 16 us
    ppermute x3, starting transfers between devices: 8.7 us -> 4.84 us  [the longest x2 2.46 us: body(): others.append(lax.ppermute(mine, 'seq', pairs))]
    ppermute x9, waiting for transfers between devices: 4.46 us -> 7.76 us  [along_outer(): lax.ppermute(piece, 'head', outer_pairs(d))]
    ppermute x6, waiting for transfers between devices: 3.8 us -> 5.24 us  [along_inner(): lax.ppermute(p, 'head', inner_pairs(e))]
    ppermute x6, starting transfers between devices: 7.72 us -> 6.28 us  [along_inner(): lax.ppermute(p, 'head', inner_pairs(e))]
  transfers between devices with their start and end apart: 18 -> 18, of which waited for: 9 -> 8; matrix products, arithmetic and copies ran while one was open for 0% -> 0% of each run, Pallas kernels for 26% -> 26%
where the time goes in v2:
time: 72 us; the launch traced here: 71.7 us
  starting transfers between devices  30 us (42%)
  Pallas kernels  25.3 us (35%)
  waiting for transfers between devices  16 us (22%)
    ppermute x9, starting transfers between devices, along_outer(): lax.ppermute(piece, 'head', outer_pairs(d))  18.9 us
    ppermute x9, waiting for transfers between devices, along_outer(): lax.ppermute(piece, 'head', outer_pairs(d))  7.76 us
    pallas_call x1, Pallas kernels, head_conv(): pl.pallas_call(functools.partial(head_conv_kernel, first, heads), grid=(c...  6.83 us
    pallas_call x2, Pallas kernels, scan(): pl.pallas_call(functools.partial(scan_kernel, span, b_rows, picks(b_piece...  6.82 us
    ppermute x6, starting transfers between devices, along_inner(): lax.ppermute(p, 'head', inner_pairs(e))  6.28 us
    ppermute x6, waiting for transfers between devices, along_inner(): lax.ppermute(p, 'head', inner_pairs(e))  5.24 us
    pallas_call x1, Pallas kernels, gates(): pl.pallas_call(gates_kernel, grid=(length // TILE,), in_specs=[wide, pl.B...  3.14 us
    ppermute x2, starting transfers between devices, body(): others.append(lax.ppermute(mine, 'seq', pairs))  2.46 us
  transfers between devices with their start and end apart: 18, of which 8 were waited for; matrix products, arithmetic and copies ran while one was open for 0% of the time, Pallas kernels for 26%

profile of v2, /device:TPU:0, one launch (start us, length us, event | category | flops | bytes accessed | tf_op | source)
XLA Modules:
  0.0 71.7 jit_solution(10300468907726018872)
XLA Ops:
  0.0 0.0 copy-start.4
  0.0 0.0 copy-start.5
  0.0 0.0 copy-start.6
  0.0 0.0 copy-start.1
  0.0 0.0 copy-start.2
  0.0 1.1 %tails.1 = (bf16[48,384]{1,0:T(8,128)(2,1)S(1)}, bf16[16,5120]{1,0:T(8,128)(2,1)S(1)}, bf16[16,5120]{1,0:T(8,128)(2,1)S(1)}) custom-call(bf16[5120,384]{1,0:T(8,128)(2,1)} %before_ref.1, bf16[16,5120]{1,0:T(8,128)(2,1)} %bitcast.9, bf16[16,5120]{1,0:T(8,128)(2,1)} %bitcast.10), custom_call_target="tpu_custom_call" | custom-call | flops 1000 | bytes 1000 | tf_op jit(solution)/shard_map/tails/pallas_call | solution.py:124
  1.1 2.4 %collective-permute-start = (bf16[48,384]{1,0:T(8,128)(2,1)S(1)}, bf16[48,384]{1,0:T(8,128)(2,1)S(1)}, u32[]{:S(2)}, u32[]{:S(2)}) collective-permute-start(bf16[48,384]{1,0:T(8,128)(2,1)S(1)} %get-tuple-element.32), channel_id=1, source_target_pairs={{0,8},{8,16},{16,24},{1,9},{9,17},{17,25},{2,10},{10,18},{18,26},{... | collective-permute-start | bytes 110600 | tf_op jit(solution)/shard_map/ppermute | solution.py:633
  3.5 0.0 copy-done.4
  3.5 0.1 copy.19
  3.6 0.0 copy-done.5
  3.6 0.1 copy.20
  3.7 0.7 collective-permute-done.halo_ref
  4.4 0.6 shared_conv.1
  5.0 2.5 %collective-permute-start.1 = (bf16[16,5120]{1,0:T(8,128)(2,1)S(1)}, bf16[16,5120]{1,0:T(8,128)(2,1)S(1)}, u32[]{:S(2)}, u32[]{:S(2)}) collective-permute-start(bf16[16,5120]{1,0:T(8,128)(2,1)S(1)} %get-tuple-element.35.refs_0_), channel_id=1, source_target_pairs={{0,2},{1,3},{2,4},{3,5},{4,6},{5,7},{6,0},{7,1},{8,10},{9,11},{10,... | collective-permute-start | bytes 491528 | tf_op jit(solution)/shard_map/ppermute | solution.py:58
  7.4 2.6 %collective-permute-start.2 = (bf16[16,5120]{1,0:T(8,128)(2,1)S(1)}, bf16[16,5120]{1,0:T(8,128)(2,1)S(1)}, u32[]{:S(2)}, u32[]{:S(2)}) collective-permute-start(bf16[16,5120]{1,0:T(8,128)(2,1)S(1)} %get-tuple-element.35.refs_0_), channel_id=1, source_target_pairs={{0,4},{1,5},{2,6},{3,7},{4,0},{5,1},{6,2},{7,3},{8,12},{9,13},{10,... | collective-permute-start | bytes 491528 | tf_op jit(solution)/shard_map/ppermute | solution.py:58
  10.0 1.3 %collective-permute-start.3 = (bf16[16,5120]{1,0:T(8,128)(2,1)S(1)}, bf16[16,5120]{1,0:T(8,128)(2,1)S(1)}, u32[]{:S(2)}, u32[]{:S(2)}) collective-permute-start(bf16[16,5120]{1,0:T(8,128)(2,1)S(1)} %get-tuple-element.35.refs_0_), channel_id=1, source_target_pairs={{0,6},{1,7},{2,0},{3,1},{4,2},{5,3},{6,4},{7,5},{8,14},{9,15},{10,... | collective-permute-start | bytes 491528 | tf_op jit(solution)/shard_map/ppermute | solution.py:58
  11.4 1.5 %collective-permute-start.4 = (bf16[16,5120]{1,0:T(8,128)(2,1)S(1)}, bf16[16,5120]{1,0:T(8,128)(2,1)S(1)}, u32[]{:S(2)}, u32[]{:S(2)}) collective-permute-start(bf16[16,5120]{1,0:T(8,128)(2,1)S(1)} %get-tuple-element.35.refs_0_), channel_id=1, source_target_pairs={{0,1},{1,0},{2,3},{3,2},{4,5},{5,4},{6,7},{7,6},{8,9},{9,8},{10,11... | collective-permute-start | bytes 491528 | tf_op jit(solution)/shard_map/ppermute | solution.py:63
  12.9 0.0 copy-done.6
  12.9 0.1 copy.21.rate_ref
  13.0 0.0 copy-done.1
  13.0 1.3 %rows.1 = (f32[8,5120]{1,0:T(8,128)S(1)}, bf16[5120,40]{1,0:T(8,128)(2,1)S(1)}, f32[40,384]{1,0:T(8,128)S(1)}) custom-call(f32[6,5120]{1,0:T(8,128)S(1)} %bitcast.6, f32[6,1]{1,0:T(8,128)S(1)} %copy.21.rate_ref), custom_call_target="tpu_custom_call" | custom-call | flops 1000 | bytes 1000 | tf_op jit(solution)/shard_map/rows/pallas_call | solution.py:219
  14.3 0.0 copy-done.2
  14.3 6.8 %head_conv.1 = (bf16[5120,384]{1,0:T(8,128)(2,1)S(1)}, bf16[5120,384]{1,0:T(8,128)(2,1)S(1)}) custom-call(bf16[5120,384]{1,0:T(8,128)(2,1)} %before_ref.1, bf16[5120,384]{1,0:T(8,128)(2,1)} %before_ref.1, bf16[48,384]{1,0:T(8,128)(2,1)S(1)} %collective-permute-done.halo_ref, f32[4,384]{1,0:T(4,128)S(1)} %convert_element_type.17.taps_ref, ...), custom_call_target="tpu_custom_call" | custom-call | flops 1000 | bytes 1000 | tf_op jit(solution)/shard_map/head_conv/pallas_call | solution.py:275
  21.1 0.0 copy-start
  21.1 0.0 collective-permute-done.1.refs_0_.refs_2_
  21.2 0.4 collective-permute-done.2.refs_1_.refs_3_
  21.6 0.0 collective-permute-done.3.refs_2_.refs_4_
  21.6 0.0 collective-permute-done.4.refs_4_.refs_1_
  21.6 1.7 %collective-permute-start.6 = (bf16[48,5120]{1,0:T(8,128)(2,1)S(1)}, bf16[48,5120]{1,0:T(8,128)(2,1)S(1)}, u32[]{:S(2)}, u32[]{:S(2)}) collective-permute-start(bf16[48,5120]{1,0:T(8,128)(2,1)S(1)} %pack.3.refs_2_), channel_id=1, source_target_pairs={{0,1},{1,0},{2,3},{3,2},{4,5},{5,4},{6,7},{7,6},{8,9},{9,8},{10,11... | collective-permute-start | bytes 1474568 | tf_op jit(solution)/shard_map/ppermute | solution.py:63
  23.3 4.1 %collective-permute-start.5 = (bf16[16,5120]{1,0:T(8,128)(2,1)S(1)}, bf16[16,5120]{1,0:T(8,128)(2,1)S(1)}, u32[]{:S(2)}, u32[]{:S(2)}) collective-permute-start(bf16[16,5120]{1,0:T(8,128)(2,1)S(1)} %get-tuple-element.45), channel_id=1, source_target_pairs={{0,2},{1,3},{2,4},{3,5},{4,6},{5,7},{6,0},{7,1},{8,10},{9,11},{10,... | collective-permute-start | bytes 491528 | tf_op jit(solution)/shard_map/ppermute | solution.py:58
  27.4 0.8 %collective-permute-start.8 = (bf16[16,5120]{1,0:T(8,128)(2,1)S(1)}, bf16[16,5120]{1,0:T(8,128)(2,1)S(1)}, u32[]{:S(2)}, u32[]{:S(2)}) collective-permute-start(bf16[16,5120]{1,0:T(8,128)(2,1)S(1)} %get-tuple-element.45), channel_id=1, source_target_pairs={{0,4},{1,5},{2,6},{3,7},{4,0},{5,1},{6,2},{7,3},{8,12},{9,13},{10,... | collective-permute-start | bytes 491528 | tf_op jit(solution)/shard_map/ppermute | solution.py:58
  28.1 1.6 %collective-permute-start.9 = (bf16[16,5120]{1,0:T(8,128)(2,1)S(1)}, bf16[16,5120]{1,0:T(8,128)(2,1)S(1)}, u32[]{:S(2)}, u32[]{:S(2)}) collective-permute-start(bf16[16,5120]{1,0:T(8,128)(2,1)S(1)} %get-tuple-element.45), channel_id=1, source_target_pairs={{0,6},{1,7},{2,0},{3,1},{4,2},{5,3},{6,4},{7,5},{8,14},{9,15},{10,... | collective-permute-start | bytes 491528 | tf_op jit(solution)/shard_map/ppermute | solution.py:58
  29.7 0.0 copy-done
  29.8 3.1 %gates.1 = (f32[5120,384]{1,0:T(8,128)S(1)}, f32[1920,128]{1,0:T(8,128)S(1)}, f32[3,320,128]{2,1,0:T(8,128)S(1)}) custom-call(bf16[5120,384]{1,0:T(8,128)(2,1)S(1)} %copy-done, bf16[5120,40]{1,0:T(8,128)(2,1)S(1)} %get-tuple-element.37.column_ref, f32[8,5120]{1,0:T(8,128)S(1)} %get-tuple-element.38.q_ref), custom_call_target="tpu_custom_call" | custom-call | flops 1000 | bytes 1000 | tf_op jit(solution)/shard_map/gates/pallas_call | solution.py:334
  32.9 0.0 collective-permute-done.5.refs_1_.refs_8_
  32.9 0.4 collective-permute-start.11
  33.4 1.9 %collective-permute-done.6.refs_5_ = bf16[48,5120]{1,0:T(8,128)(2,1)S(1)} collective-permute-done((bf16[48,5120]{1,0:T(8,128)(2,1)S(1)}, bf16[48,5120]{1,0:T(8,128)(2,1)S(1)}, u32[]{:S(2)}, u32[]{:S(2)}) %collective-permute-start.6) | collective-permute-done | bytes 491552 | tf_op jit(solution)/shard_map/ppermute | solution.py:63
  35.3 1.9 %last_state.1 = (bf16[144,384]{1,0:T(8,128)(2,1)S(1)}, f32[5120,384]{1,0:T(8,128)S(1)}, f32[40,384]{1,0:T(8,128)S(1)}) custom-call(bf16[5120,384]{1,0:T(8,128)(2,1)S(1)} %get-tuple-element.42.wt_ref, f32[40,384]{1,0:T(8,128)S(1)} %tie.3.decay_ref, bf16[16,5120]{1,0:T(8,128)(2,1)S(1)} %get-tuple-element.35.refs_0_, ...), custom_call_target="tpu_custom_call" | custom-call | flops 1000 | bytes 1000 | tf_op jit(solution)/shard_map/last_state/pallas_call | solution.py:401
  37.2 0.1 collective-permute-start.7
  37.3 2.3 %collective-permute-done.8.refs_0_.refs_9_ = bf16[16,5120]{1,0:T(8,128)(2,1)S(1)} collective-permute-done((bf16[16,5120]{1,0:T(8,128)(2,1)S(1)}, bf16[16,5120]{1,0:T(8,128)(2,1)S(1)}, u32[]{:S(2)}, u32[]{:S(2)}) %collective-permute-start.8) | collective-permute-done | bytes 163872 | tf_op jit(solution)/shard_map/ppermute | solution.py:58
  39.6 0.0 collective-permute-done.9.refs_1_.refs_10_
  39.7 0.6 collective-permute-start.13
  40.2 1.5 %collective-permute-start.12 = (bf16[32,2048]{1,0:T(8,128)(2,1)S(1)}, bf16[32,2048]{1,0:T(8,128)(2,1)S(1)}, u32[]{:S(2)}, u32[]{:S(2)}) collective-permute-start(bf16[32,2048]{1,0:T(8,128)(2,1)S(1)} %get-tuple-element.50), channel_id=1, source_target_pairs={{0,1},{1,0},{2,3},{3,2},{4,5},{5,4},{6,7},{7,6},{8,9},{9,8},{10,11... | collective-permute-start | bytes 393224 | tf_op jit(solution)/shard_map/ppermute | solution.py:63
  41.8 0.0 collective-permute-done.7.other_ref.refs_0_
  41.8 0.1 join.1
  41.8 2.4 %collective-permute-start.10 = (bf16[144,384]{1,0:T(8,128)(2,1)S(1)}, bf16[144,384]{1,0:T(8,128)(2,1)S(1)}, u32[]{:S(2)}, u32[]{:S(2)}) collective-permute-start(bf16[144,384]{1,0:T(8,128)(2,1)S(1)} %join.1), channel_id=1, source_target_pairs={{0,16},{8,24},{1,17},{9,25},{2,18},{10,26},{3,19},{11,27},{4,20},{... | collective-permute-start | bytes 331784 | tf_op jit(solution)/shard_map/ppermute | solution.py:676
  44.2 2.3 %collective-permute-done.10.refs_1_ = bf16[144,384]{1,0:T(8,128)(2,1)S(1)} collective-permute-done((bf16[144,384]{1,0:T(8,128)(2,1)S(1)}, bf16[144,384]{1,0:T(8,128)(2,1)S(1)}, u32[]{:S(2)}, u32[]{:S(2)}) %collective-permute-start.10) | collective-permute-done | bytes 110624 | tf_op jit(solution)/shard_map/ppermute | solution.py:676
  46.5 1.1 %enter.1.state_ref = bf16[5120,384]{1,0:T(8,128)(2,1)S(1)} custom-call(f32[5120,384]{1,0:T(8,128)S(1)} %get-tuple-element.46.local_ref, f32[40,384]{1,0:T(8,128)S(1)} %get-tuple-element.47.before_ref, bf16[144,384]{1,0:T(8,128)(2,1)S(1)} %collective-permute-done.7.other_ref.refs_0_, bf16[144,384]{1,0:T(8,128)(2,1)S(1)} %collective-permute-done.10.refs_1_), custom_call_target="tpu_custom_call" | custom-call | flops 1000 | bytes 1000 | tf_op jit(solution)/shard_map/enter/pallas_call | solution.py:465
  47.7 0.0 collective-permute-done.11.refs_7_
  47.7 0.0 collective-permute-done.13.refs_11_
  47.7 4.1 %scan.2 = (bf16[5120,384]{1,0:T(8,128)(2,1)S(1)}, f32[40,128]{1,0:T(8,128)S(1)}) custom-call(f32[5120,384]{1,0:T(8,128)S(1)} %get-tuple-element.39.gate_ref, f32[1920,128]{1,0:T(8,128)S(1)} %get-tuple-element.40.factor_ref, f32[3,320,128]{2,1,0:T(8,128)S(1)} %get-tuple-element.41.refs_2_.start_ref, bf16[5120,384]{1,0:T(8,128)(2,1)S(1)} %get-tuple-element.36.refs_3_.xs_ref, ...), custom_call_target="tpu_custom_call" | custom-call | flops 1000 | bytes 1000 | tf_op jit(solution)/shard_map/scan/pallas_call | solution.py:569
  51.8 0.0 collective-permute-done.12.refs_11_
  51.8 0.0 copy-start.3
  51.8 2.7 %scan.3 = (bf16[5120,384]{1,0:T(8,128)(2,1)S(1)}, f32[40,128]{1,0:T(8,128)S(1)}) custom-call(f32[5120,384]{1,0:T(8,128)S(1)} %get-tuple-element.39.gate_ref, f32[1920,128]{1,0:T(8,128)S(1)} %get-tuple-element.40.factor_ref, f32[3,320,128]{2,1,0:T(8,128)S(1)} %get-tuple-element.41.refs_2_.start_ref, ...), custom_call_target="tpu_custom_call", output_to_operand_aliasing={{0}: (17, {}), {1}: (18, {})} | custom-call | flops 1000 | bytes 1000 | tf_op jit(solution)/shard_map/scan/pallas_call | solution.py:569
  54.5 5.5 %collective-permute-start.16 = (f32[40,128]{1,0:T(8,128)S(1)}, f32[40,128]{1,0:T(8,128)S(1)}, u32[]{:S(2)}, u32[]{:S(2)}) collective-permute-start(f32[40,128]{1,0:T(8,128)S(1)} %get-tuple-element.54), channel_id=1, source_target_pairs={{0,6},{1,7},{2,0},{3,1},{4,2},{5,3},{6,4},{7,5},{8,14},{9,15},{10,... | collective-permute-start | bytes 61448 | tf_op jit(solution)/shard_map/ppermute | solution.py:58
  60.0 0.0 collective-permute-start.14
  60.0 0.6 collective-permute-start.15
  60.5 0.9 %collective-permute-done.16 = f32[40,128]{1,0:T(8,128)S(1)} collective-permute-done((f32[40,128]{1,0:T(8,128)S(1)}, f32[40,128]{1,0:T(8,128)S(1)}, u32[]{:S(2)}, u32[]{:S(2)}) %collective-permute-start.16) | collective-permute-done | bytes 20512 | tf_op jit(solution)/shard_map/ppermute | solution.py:58
  61.5 4.1 %collective-permute-done.14 = f32[40,128]{1,0:T(8,128)S(1)} collective-permute-done((f32[40,128]{1,0:T(8,128)S(1)}, f32[40,128]{1,0:T(8,128)S(1)}, u32[]{:S(2)}, u32[]{:S(2)}) %collective-permute-start.14) | collective-permute-done | bytes 20512 | tf_op jit(solution)/shard_map/ppermute | solution.py:58
  65.6 0.0 collective-permute-done.15
  65.6 0.6 collective-permute-start.17
  66.1 0.0 copy-done.3
  66.1 3.3 %collective-permute-done.17.refs_1_ = f32[40,128]{1,0:T(8,128)S(1)} collective-permute-done((f32[40,128]{1,0:T(8,128)S(1)}, f32[40,128]{1,0:T(8,128)S(1)}, u32[]{:S(2)}, u32[]{:S(2)}) %collective-permute-start.17) | collective-permute-done | bytes 20512 | tf_op jit(solution)/shard_map/ppermute | solution.py:63
  69.4 2.3 %norm.1 = bf16[5120,384]{1,0:T(8,128)(2,1)} custom-call(bf16[5120,384]{1,0:T(8,128)(2,1)S(1)} %get-tuple-element.53.gated_ref, f32[1,384]{1,0:T(1,128)S(1)} %broadcast_in_dim.7.gain_ref, f32[40,128]{1,0:T(8,128)S(1)} %add_add_fusion.refs_0_, f32[40,128]{1,0:T(8,128)S(1)} %collective-permute-done.17.refs_1_), custom_call_target="tpu_custom_call" | custom-call | flops 1000 | bytes 1000 | tf_op jit(solution)/shard_map/norm/pallas_call | solution.py:612
  (8 shorter events, 0.1 us)
Async XLA Ops:
  0.0 3.5 %copy-start.4 = (bf16[4,16]{1,0:T(4,128)(2,1)S(1)}, bf16[4,16]{1,0:T(4,128)(2,1)}, u32[]{:S(2)}) copy-start(bf16[4,16]{1,0:T(4,128)(2,1)} %param.16) | copy-start | bytes 388
  0.0 3.6 %copy-start.5 = (bf16[4,16]{1,0:T(4,128)(2,1)S(1)}, bf16[4,16]{1,0:T(4,128)(2,1)}, u32[]{:S(2)}) copy-start(bf16[4,16]{1,0:T(4,128)(2,1)} %param.17) | copy-start | bytes 388
  0.0 12.9 %copy-start.6 = (f32[6]{0:T(128)S(1)}, f32[6]{0:T(128)}, u32[]{:S(2)}) copy-start(f32[6]{0:T(128)} %param.18) | copy-start | bytes 76
  0.0 13.0 %copy-start.1 = (f32[5120,6]{0,1:T(8,128)S(1)}, f32[5120,6]{0,1:T(8,128)}, u32[]{:S(2)}) copy-start(f32[5120,6]{0,1:T(8,128)} %param.14) | copy-start | bytes 368644
  0.0 14.3 %copy-start.2 = (bf16[4,384]{1,0:T(4,128)(2,1)S(1)}, bf16[4,384]{1,0:T(4,128)(2,1)}, u32[]{:S(2)}) copy-start(bf16[4,384]{1,0:T(4,128)(2,1)} %param.15) | copy-start | bytes 9220
  1.1 3.2 %collective-permute-start = (bf16[48,384]{1,0:T(8,128)(2,1)S(1)}, bf16[48,384]{1,0:T(8,128)(2,1)S(1)}, u32[]{:S(2)}, u32[]{:S(2)}) collective-permute-start(bf16[48,384]{1,0:T(8,128)(2,1)S(1)} %get-tuple-element.32), channel_id=1, source_target_pairs={{0,8},{8,16},{16,24},{1,9},{9,17},{17,25},{2,10},{10,18},{18,26},{... | collective-permute-start | bytes 110600 | tf_op jit(solution)/shard_map/ppermute | solution.py:633
  5.0 16.2 %collective-permute-start.1 = (bf16[16,5120]{1,0:T(8,128)(2,1)S(1)}, bf16[16,5120]{1,0:T(8,128)(2,1)S(1)}, u32[]{:S(2)}, u32[]{:S(2)}) collective-permute-start(bf16[16,5120]{1,0:T(8,128)(2,1)S(1)} %get-tuple-element.35.refs_0_), channel_id=1, source_target_pairs={{0,2},{1,3},{2,4},{3,5},{4,6},{5,7},{6,0},{7,1},{8,10},{9,11},{10,... | collective-permute-start | bytes 491528 | tf_op jit(solution)/shard_map/ppermute | solution.py:58
  7.4 14.1 %collective-permute-start.2 = (bf16[16,5120]{1,0:T(8,128)(2,1)S(1)}, bf16[16,5120]{1,0:T(8,128)(2,1)S(1)}, u32[]{:S(2)}, u32[]{:S(2)}) collective-permute-start(bf16[16,5120]{1,0:T(8,128)(2,1)S(1)} %get-tuple-element.35.refs_0_), channel_id=1, source_target_pairs={{0,4},{1,5},{2,6},{3,7},{4,0},{5,1},{6,2},{7,3},{8,12},{9,13},{10,... | collective-permute-start | bytes 491528 | tf_op jit(solution)/shard_map/ppermute | solution.py:58
  10.0 11.5 %collective-permute-start.3 = (bf16[16,5120]{1,0:T(8,128)(2,1)S(1)}, bf16[16,5120]{1,0:T(8,128)(2,1)S(1)}, u32[]{:S(2)}, u32[]{:S(2)}) collective-permute-start(bf16[16,5120]{1,0:T(8,128)(2,1)S(1)} %get-tuple-element.35.refs_0_), channel_id=1, source_target_pairs={{0,6},{1,7},{2,0},{3,1},{4,2},{5,3},{6,4},{7,5},{8,14},{9,15},{10,... | collective-permute-start | bytes 491528 | tf_op jit(solution)/shard_map/ppermute | solution.py:58
  11.4 10.2 %collective-permute-start.4 = (bf16[16,5120]{1,0:T(8,128)(2,1)S(1)}, bf16[16,5120]{1,0:T(8,128)(2,1)S(1)}, u32[]{:S(2)}, u32[]{:S(2)}) collective-permute-start(bf16[16,5120]{1,0:T(8,128)(2,1)S(1)} %get-tuple-element.35.refs_0_), channel_id=1, source_target_pairs={{0,1},{1,0},{2,3},{3,2},{4,5},{5,4},{6,7},{7,6},{8,9},{9,8},{10,11... | collective-permute-start | bytes 491528 | tf_op jit(solution)/shard_map/ppermute | solution.py:63
  21.1 8.6 %copy-start = (bf16[5120,384]{1,0:T(8,128)(2,1)S(1)}, bf16[5120,384]{1,0:T(8,128)(2,1)}, u32[]{:S(2)}) copy-start(bf16[5120,384]{1,0:T(8,128)(2,1)} %z_ref.1) | copy-start | bytes 11796484
  21.6 13.7 %collective-permute-start.6 = (bf16[48,5120]{1,0:T(8,128)(2,1)S(1)}, bf16[48,5120]{1,0:T(8,128)(2,1)S(1)}, u32[]{:S(2)}, u32[]{:S(2)}) collective-permute-start(bf16[48,5120]{1,0:T(8,128)(2,1)S(1)} %pack.3.refs_2_), channel_id=1, source_target_pairs={{0,1},{1,0},{2,3},{3,2},{4,5},{5,4},{6,7},{7,6},{8,9},{9,8},{10,11... | collective-permute-start | bytes 1474568 | tf_op jit(solution)/shard_map/ppermute | solution.py:63
  23.3 9.6 %collective-permute-start.5 = (bf16[16,5120]{1,0:T(8,128)(2,1)S(1)}, bf16[16,5120]{1,0:T(8,128)(2,1)S(1)}, u32[]{:S(2)}, u32[]{:S(2)}) collective-permute-start(bf16[16,5120]{1,0:T(8,128)(2,1)S(1)} %get-tuple-element.45), channel_id=1, source_target_pairs={{0,2},{1,3},{2,4},{3,5},{4,6},{5,7},{6,0},{7,1},{8,10},{9,11},{10,... | collective-permute-start | bytes 491528 | tf_op jit(solution)/shard_map/ppermute | solution.py:58
  27.4 12.2 %collective-permute-start.8 = (bf16[16,5120]{1,0:T(8,128)(2,1)S(1)}, bf16[16,5120]{1,0:T(8,128)(2,1)S(1)}, u32[]{:S(2)}, u32[]{:S(2)}) collective-permute-start(bf16[16,5120]{1,0:T(8,128)(2,1)S(1)} %get-tuple-element.45), channel_id=1, source_target_pairs={{0,4},{1,5},{2,6},{3,7},{4,0},{5,1},{6,2},{7,3},{8,12},{9,13},{10,... | collective-permute-start | bytes 491528 | tf_op jit(solution)/shard_map/ppermute | solution.py:58
  28.1 11.5 %collective-permute-start.9 = (bf16[16,5120]{1,0:T(8,128)(2,1)S(1)}, bf16[16,5120]{1,0:T(8,128)(2,1)S(1)}, u32[]{:S(2)}, u32[]{:S(2)}) collective-permute-start(bf16[16,5120]{1,0:T(8,128)(2,1)S(1)} %get-tuple-element.45), channel_id=1, source_target_pairs={{0,6},{1,7},{2,0},{3,1},{4,2},{5,3},{6,4},{7,5},{8,14},{9,15},{10,... | collective-permute-start | bytes 491528 | tf_op jit(solution)/shard_map/ppermute | solution.py:58
  32.9 14.7 %collective-permute-start.11 = (bf16[32,5120]{1,0:T(8,128)(2,1)S(1)}, bf16[32,5120]{1,0:T(8,128)(2,1)S(1)}, u32[]{:S(2)}, u32[]{:S(2)}) collective-permute-start(bf16[32,5120]{1,0:T(8,128)(2,1)S(1)} %pack.4.refs_1_), channel_id=1, source_target_pairs={{0,1},{1,0},{2,3},{3,2},{4,5},{5,4},{6,7},{7,6},{8,9},{9,8},{10,11... | collective-permute-start | bytes 983048 | tf_op jit(solution)/shard_map/ppermute | solution.py:63
  37.2 4.5 %collective-permute-start.7 = (bf16[144,384]{1,0:T(8,128)(2,1)S(1)}, bf16[144,384]{1,0:T(8,128)(2,1)S(1)}, u32[]{:S(2)}, u32[]{:S(2)}) collective-permute-start(bf16[144,384]{1,0:T(8,128)(2,1)S(1)} %get-tuple-element.48.refs_2_.mine_ref), channel_id=1, source_target_pairs={{0,8},{8,0},{16,24},{24,16},{1,9},{9,1},{17,25},{25,17},{2,10},{10... | collective-permute-start | bytes 331784 | tf_op jit(solution)/shard_map/ppermute | solution.py:676
  39.7 8.0 %collective-permute-start.13 = (bf16[32,3072]{1,0:T(8,128)(2,1)S(1)}, bf16[32,3072]{1,0:T(8,128)(2,1)S(1)}, u32[]{:S(2)}, u32[]{:S(2)}) collective-permute-start(bf16[32,3072]{1,0:T(8,128)(2,1)S(1)} %get-tuple-element.49.token_ref), channel_id=1, source_target_pairs={{0,1},{1,0},{2,3},{3,2},{4,5},{5,4},{6,7},{7,6},{8,9},{9,8},{10,11... | collective-permute-start | bytes 589832 | tf_op jit(solution)/shard_map/ppermute | solution.py:63
  40.2 11.5 %collective-permute-start.12 = (bf16[32,2048]{1,0:T(8,128)(2,1)S(1)}, bf16[32,2048]{1,0:T(8,128)(2,1)S(1)}, u32[]{:S(2)}, u32[]{:S(2)}) collective-permute-start(bf16[32,2048]{1,0:T(8,128)(2,1)S(1)} %get-tuple-element.50), channel_id=1, source_target_pairs={{0,1},{1,0},{2,3},{3,2},{4,5},{5,4},{6,7},{7,6},{8,9},{9,8},{10,11... | collective-permute-start | bytes 393224 | tf_op jit(solution)/shard_map/ppermute | solution.py:63
  41.8 4.7 %collective-permute-start.10 = (bf16[144,384]{1,0:T(8,128)(2,1)S(1)}, bf16[144,384]{1,0:T(8,128)(2,1)S(1)}, u32[]{:S(2)}, u32[]{:S(2)}) collective-permute-start(bf16[144,384]{1,0:T(8,128)(2,1)S(1)} %join.1), channel_id=1, source_target_pairs={{0,16},{8,24},{1,17},{9,25},{2,18},{10,26},{3,19},{11,27},{4,20},{... | collective-permute-start | bytes 331784 | tf_op jit(solution)/shard_map/ppermute | solution.py:676
  51.8 14.4 %copy-start.3 = (f32[384]{0:T(512)S(1)}, f32[384]{0:T(512)}, u32[]{:S(2)}) copy-start(f32[384]{0:T(512)} %param.19) | copy-start | bytes 4612
  54.5 7.0 %collective-permute-start.16 = (f32[40,128]{1,0:T(8,128)S(1)}, f32[40,128]{1,0:T(8,128)S(1)}, u32[]{:S(2)}, u32[]{:S(2)}) collective-permute-start(f32[40,128]{1,0:T(8,128)S(1)} %get-tuple-element.54), channel_id=1, source_target_pairs={{0,6},{1,7},{2,0},{3,1},{4,2},{5,3},{6,4},{7,5},{8,14},{9,15},{10,... | collective-permute-start | bytes 61448 | tf_op jit(solution)/shard_map/ppermute | solution.py:58
  60.0 5.6 %collective-permute-start.14 = (f32[40,128]{1,0:T(8,128)S(1)}, f32[40,128]{1,0:T(8,128)S(1)}, u32[]{:S(2)}, u32[]{:S(2)}) collective-permute-start(f32[40,128]{1,0:T(8,128)S(1)} %get-tuple-element.54), channel_id=1, source_target_pairs={{0,2},{1,3},{2,4},{3,5},{4,6},{5,7},{6,0},{7,1},{8,10},{9,11},{10,... | collective-permute-start | bytes 61448 | tf_op jit(solution)/shard_map/ppermute | solution.py:58
  60.0 5.6 %collective-permute-start.15 = (f32[40,128]{1,0:T(8,128)S(1)}, f32[40,128]{1,0:T(8,128)S(1)}, u32[]{:S(2)}, u32[]{:S(2)}) collective-permute-start(f32[40,128]{1,0:T(8,128)S(1)} %get-tuple-element.54), channel_id=1, source_target_pairs={{0,4},{1,5},{2,6},{3,7},{4,0},{5,1},{6,2},{7,3},{8,12},{9,13},{10,... | collective-permute-start | bytes 61448 | tf_op jit(solution)/shard_map/ppermute | solution.py:58
  65.6 3.8 %collective-permute-start.17 = (f32[40,128]{1,0:T(8,128)S(1)}, f32[40,128]{1,0:T(8,128)S(1)}, u32[]{:S(2)}, u32[]{:S(2)}) collective-permute-start(f32[40,128]{1,0:T(8,128)S(1)} %add_add_fusion.refs_0_), channel_id=1, source_target_pairs={{0,1},{1,0},{2,3},{3,2},{4,5},{5,4},{6,7},{7,6},{8,9},{9,8},{10,11... | collective-permute-start | bytes 61448 | tf_op jit(solution)/shard_map/ppermute | solution.py:63

commit v3 on v2

--- a/solution.py
+++ b/solution.py
@@ -436,53 +436,23 @@
     )(*in_vmem([mine, other]), token)
 
 
-def enter_kernel(local_ref, before_ref, *refs):
-    others, out_ref, state = refs[:-2], refs[-2], refs[-1]
-    size = state.shape[0]
-    carry = jnp.zeros(state.shape, F32)
-    for k in reversed(range(len(others))):
-        longer = carry * others[k][size : size + 1].astype(F32) + others[k][:size].astype(F32)
-        carry = jnp.where(jnp.bitwise_and(lax.axis_index("seq"), 1 << k) != 0, longer, carry)
-    state[...] = carry
-    some = 8
-
-    def group(t, _):
-        row = pl.multiple_of(t * some, some)
-        decays = before_ref[pl.ds(row, some)]
-        held = state[...]
-        for s in range(some):
-            at = pl.ds(pl.multiple_of((t * some + s) * size, size), size)
-            out_ref[at] = (local_ref[at] + held * decays[s : s + 1]).astype(BF16)
-        return 0
-
-    lax.fori_loop(0, before_ref.shape[0] // some, group, 0)
-
-
-def enter(local, before, others):
-    rows, width = local.shape
-    size = rows // before.shape[0]
-    operands = [local, before, *others]
-    return pl.pallas_call(
-        enter_kernel,
-        in_specs=[IN_VMEM] * len(operands),
-        out_specs=IN_VMEM,
-        out_shape=pltpu.VMEM((rows, width), BF16),
-        scratch_shapes=[pltpu.VMEM((size, width), F32)],
-        compiler_params=params(),
-        cost_estimate=BRIEF,
-        name="enter",
-    )(*in_vmem(operands))
-
-
 def scan_kernel(
-    span, b_rows, b_picks, c_rows_of, c_picks, c_begins, gate_ref, factor_ref, start_ref, xs_ref, state_ref, *refs
+    span, count, b_rows, b_picks, c_rows_of, c_picks, c_begins, gate_ref, factor_ref, start_ref, xs_ref,
+    local_ref, before_ref, *refs
 ):
+    others, refs = refs[:count], refs[count:]
     b_refs, c_refs = [refs[i] for i in b_picks], [refs[i] for i in c_picks]
-    gated_ref, square_ref, c_rows, scores, carried, squares = refs[-6:]
+    gated_ref, square_ref, carry, c_rows, scores, carried, squares = refs[-7:]
     length, width = gate_ref.shape
     heads = factor_ref.shape[0] // (length // ROWS)
     groups, subs, pairs = SUB // ROWS, TILE // SUB, width // SUB
-    size = state_ref.shape[0] // square_ref.shape[0]
+    size = carry.shape[0]
+    entering = jnp.zeros(carry.shape, F32)
+    for k in reversed(range(count)):
+        end = others[k][...].astype(F32)
+        longer = entering * end[size : size + 1] + end[:size]
+        entering = jnp.where(jnp.bitwise_and(lax.axis_index("seq"), 1 << k) != 0, longer, entering)
+    carry[...] = entering
     i = lax.broadcasted_iota(jnp.int32, (SUB, SUB), 0)
     j = lax.broadcasted_iota(jnp.int32, (SUB, SUB), 1)
     causal = i >= j
@@ -504,15 +474,18 @@
         factors = pl.multiple_of(t * (subs * heads * groups), subs * heads * groups)
         starts = pl.multiple_of(t * (subs * groups), subs * groups)
 
+        decays = before_ref[pl.ds(row, subs)]
+
         def turn(s):
             c_rows[local[s]] = columns_from(c_refs, c_rows_of, c_begins, t * TILE + s * SUB).T
 
         def products(s):
             b_cols = columns_of(b_refs, b_rows, whole[s])
             held = pl.ds(pl.multiple_of((t * subs + s) * size, size), size)
+            state = local_ref[held] + carry[...] * decays[s : s + 1]
             both = jnp.dot(
                 c_rows[local[s]],
-                jnp.concatenate([b_cols, state_ref[held]], axis=1),
+                jnp.concatenate([b_cols, state.astype(BF16)], axis=1),
                 preferred_element_type=F32,
             )
             scores[local[s]] = jnp.where(causal, both[:, :SUB], 0.0)
@@ -556,7 +529,7 @@
     lax.fori_loop(*span, tile, 0)
 
 
-def scan(span, gate, factor, start, xs, states, b_pieces, b_rows, c_pieces, c_rows, c_begins, filled=()):
+def scan(span, gate, factor, start, xs, local, before, others, b_pieces, b_rows, c_pieces, c_rows, c_begins, filled=()):
     length, width = xs.shape
     size = sum(last - first for first, last in b_rows)
     pieces = []
@@ -564,16 +537,17 @@
         if not any(piece is other for other in pieces):
             pieces.append(piece)
     picks = lambda some: [next(i for i, q in enumerate(pieces) if q is p) for p in some]
-    operands = [gate, factor, start, xs, states, *pieces, *filled]
+    operands = [gate, factor, start, xs, local, before, *others, *pieces, *filled]
     first = len(operands) - len(filled)
     return pl.pallas_call(
         functools.partial(
-            scan_kernel, span, b_rows, picks(b_pieces), c_rows, picks(c_pieces), c_begins
+            scan_kernel, span, len(others), b_rows, picks(b_pieces), c_rows, picks(c_pieces), c_begins
         ),
         in_specs=[IN_VMEM] * len(operands),
         out_specs=[IN_VMEM, IN_VMEM],
         out_shape=[pltpu.VMEM((length, width), BF16), pltpu.VMEM((length // SUB, SUB), F32)],
         scratch_shapes=[
+            pltpu.VMEM((size, width), F32),
             pltpu.VMEM((TILE, size), BF16),
             pltpu.VMEM((TILE, SUB), F32),
             pltpu.VMEM((TILE, width), F32),
@@ -677,11 +651,10 @@
         if not last:
             mine = join(bit, mine, others[-1], token)
         bit *= 2
-    states = enter(local, before, others)
     filled = ()
     for span, piece, begin in runs:
         filled = scan(
-            span, gate, factor, start, xs, states, b_pieces, b_rows,
+            span, gate, factor, start, xs, local, before, others, b_pieces, b_rows,
             c_pieces + [piece] * len(tail), c_rows + tail, [0] * len(c_pieces) + [begin], filled,
         )
     gated, square = filled

time: 72 us -> 70.9 us (0.985)
  waiting for transfers between devices: 16 us -> 14.6 us
    ppermute x6, waiting for transfers between devices: 5.24 us -> 8.23 us  [along_inner(): lax.ppermute(p, 'head', inner_pairs(e))]
    ppermute x2, waiting for transfers between devices: 2.31 us -> 0.01 us  [body(): others.append(lax.ppermute(mine, 'seq', pairs))]
    ppermute x9, waiting for transfers between devices: 7.76 us -> 5.7 us  [along_outer(): lax.ppermute(piece, 'head', outer_pairs(d))]
    pallas_call x3 -> x2, Pallas kernels: 7.95 us -> 7.68 us  [scan(): pl.pallas_call(functools.partial(scan_kernel, span, len(others), b_rows,...]
  transfers between devices with their start and end apart: 18 -> 18, of which waited for: 8 -> 9; matrix products, arithmetic and copies ran while one was open for 0% -> 0% of each run, Pallas kernels for 26% -> 25%
where the time goes in v3:
time: 70.9 us; the launch traced here: 70.6 us
  starting transfers between devices  30.5 us (43%)
  Pallas kernels  25 us (35%)
  waiting for transfers between devices  14.6 us (21%)
    ppermute x9, starting transfers between devices, along_outer(): lax.ppermute(piece, 'head', outer_pairs(d))  19.2 us
    ppermute x6, waiting for transfers between devices, along_inner(): lax.ppermute(p, 'head', inner_pairs(e))  8.23 us
    pallas_call x2, Pallas kernels, scan(): pl.pallas_call(functools.partial(scan_kernel, span, len(others), b_rows,...  7.68 us
    pallas_call x1, Pallas kernels, head_conv(): pl.pallas_call(functools.partial(head_conv_kernel, first, heads), grid=(c...  6.81 us
    ppermute x6, starting transfers between devices, along_inner(): lax.ppermute(p, 'head', inner_pairs(e))  6.47 us
    ppermute x9, waiting for transfers between devices, along_outer(): lax.ppermute(piece, 'head', outer_pairs(d))  5.7 us
    pallas_call x1, Pallas kernels, gates(): pl.pallas_call(gates_kernel, grid=(length // TILE,), in_specs=[wide, pl.B...  3.18 us
    ppermute x2, starting transfers between devices, body(): others.append(lax.ppermute(mine, 'seq', pairs))  2.46 us
  transfers between devices with their start and end apart: 18, of which 9 were waited for; matrix products, arithmetic and copies ran while one was open for 0% of the time, Pallas kernels for 25%

profile of v3, /device:TPU:0, one launch (start us, length us, event | category | flops | bytes accessed | tf_op | source)
XLA Modules:
  0.0 70.6 jit_solution(8930149040386217460)
XLA Ops:
  0.0 0.0 copy-start.4
  0.0 0.0 copy-start.5
  0.0 0.0 copy-start.6
  0.0 0.0 copy-start.1
  0.0 0.0 copy-start.2
  0.0 1.1 %tails.1 = (bf16[48,384]{1,0:T(8,128)(2,1)S(1)}, bf16[16,5120]{1,0:T(8,128)(2,1)S(1)}, bf16[16,5120]{1,0:T(8,128)(2,1)S(1)}) custom-call(bf16[5120,384]{1,0:T(8,128)(2,1)} %before_ref.1, bf16[16,5120]{1,0:T(8,128)(2,1)} %bitcast.9, bf16[16,5120]{1,0:T(8,128)(2,1)} %bitcast.10), custom_call_target="tpu_custom_call" | custom-call | flops 1000 | bytes 1000 | tf_op jit(solution)/shard_map/tails/pallas_call | solution.py:124
  1.1 2.4 %collective-permute-start = (bf16[48,384]{1,0:T(8,128)(2,1)S(1)}, bf16[48,384]{1,0:T(8,128)(2,1)S(1)}, u32[]{:S(2)}, u32[]{:S(2)}) collective-permute-start(bf16[48,384]{1,0:T(8,128)(2,1)S(1)} %get-tuple-element.32), channel_id=1, source_target_pairs={{0,8},{8,16},{16,24},{1,9},{9,17},{17,25},{2,10},{10,18},{18,26},{... | collective-permute-start | bytes 110600 | tf_op jit(solution)/shard_map/ppermute | solution.py:607
  3.5 0.0 copy-done.4
  3.5 0.1 copy.19
  3.6 0.0 copy-done.5
  3.6 0.1 copy.20
  3.7 0.7 collective-permute-done.halo_ref
  4.4 0.6 shared_conv.1
  5.0 2.5 %collective-permute-start.1 = (bf16[16,5120]{1,0:T(8,128)(2,1)S(1)}, bf16[16,5120]{1,0:T(8,128)(2,1)S(1)}, u32[]{:S(2)}, u32[]{:S(2)}) collective-permute-start(bf16[16,5120]{1,0:T(8,128)(2,1)S(1)} %get-tuple-element.35.refs_0_.refs_2_), channel_id=1, source_target_pairs={{0,2},{1,3},{2,4},{3,5},{4,6},{5,7},{6,0},{7,1},{8,10},{9,11},{10,... | collective-permute-start | bytes 491528 | tf_op jit(solution)/shard_map/ppermute | solution.py:58
  7.4 2.6 %collective-permute-start.2 = (bf16[16,5120]{1,0:T(8,128)(2,1)S(1)}, bf16[16,5120]{1,0:T(8,128)(2,1)S(1)}, u32[]{:S(2)}, u32[]{:S(2)}) collective-permute-start(bf16[16,5120]{1,0:T(8,128)(2,1)S(1)} %get-tuple-element.35.refs_0_.refs_2_), channel_id=1, source_target_pairs={{0,4},{1,5},{2,6},{3,7},{4,0},{5,1},{6,2},{7,3},{8,12},{9,13},{10,... | collective-permute-start | bytes 491528 | tf_op jit(solution)/shard_map/ppermute | solution.py:58
  10.0 1.3 %collective-permute-start.3 = (bf16[16,5120]{1,0:T(8,128)(2,1)S(1)}, bf16[16,5120]{1,0:T(8,128)(2,1)S(1)}, u32[]{:S(2)}, u32[]{:S(2)}) collective-permute-start(bf16[16,5120]{1,0:T(8,128)(2,1)S(1)} %get-tuple-element.35.refs_0_.refs_2_), channel_id=1, source_target_pairs={{0,6},{1,7},{2,0},{3,1},{4,2},{5,3},{6,4},{7,5},{8,14},{9,15},{10,... | collective-permute-start | bytes 491528 | tf_op jit(solution)/shard_map/ppermute | solution.py:58
  11.4 1.5 %collective-permute-start.4 = (bf16[16,5120]{1,0:T(8,128)(2,1)S(1)}, bf16[16,5120]{1,0:T(8,128)(2,1)S(1)}, u32[]{:S(2)}, u32[]{:S(2)}) collective-permute-start(bf16[16,5120]{1,0:T(8,128)(2,1)S(1)} %get-tuple-element.35.refs_0_.refs_2_), channel_id=1, source_target_pairs={{0,1},{1,0},{2,3},{3,2},{4,5},{5,4},{6,7},{7,6},{8,9},{9,8},{10,11... | collective-permute-start | bytes 491528 | tf_op jit(solution)/shard_map/ppermute | solution.py:63
  12.9 0.0 copy-done.6
  12.9 0.1 copy.21.rate_ref
  13.0 0.0 copy-done.1
  13.0 1.3 %rows.1 = (f32[8,5120]{1,0:T(8,128)S(1)}, bf16[5120,40]{1,0:T(8,128)(2,1)S(1)}, f32[40,384]{1,0:T(8,128)S(1)}) custom-call(f32[6,5120]{1,0:T(8,128)S(1)} %bitcast.6, f32[6,1]{1,0:T(8,128)S(1)} %copy.21.rate_ref), custom_call_target="tpu_custom_call" | custom-call | flops 1000 | bytes 1000 | tf_op jit(solution)/shard_map/rows/pallas_call | solution.py:219
  14.3 0.0 copy-done.2
  14.3 6.8 %head_conv.1 = (bf16[5120,384]{1,0:T(8,128)(2,1)S(1)}, bf16[5120,384]{1,0:T(8,128)(2,1)S(1)}) custom-call(bf16[5120,384]{1,0:T(8,128)(2,1)} %before_ref.1, bf16[5120,384]{1,0:T(8,128)(2,1)} %before_ref.1, bf16[48,384]{1,0:T(8,128)(2,1)S(1)} %collective-permute-done.halo_ref, f32[4,384]{1,0:T(4,128)S(1)} %convert_element_type.17.taps_ref, ...), custom_call_target="tpu_custom_call" | custom-call | flops 1000 | bytes 1000 | tf_op jit(solution)/shard_map/head_conv/pallas_call | solution.py:275
  21.1 0.0 copy-start
  21.1 0.0 collective-permute-done.1.refs_0_.refs_2_.refs_4_
  21.1 0.4 collective-permute-done.2.refs_1_.refs_3_.refs_5_
  21.6 0.0 collective-permute-done.3.refs_2_.refs_4_.refs_6_
  21.6 0.0 collective-permute-done.4.refs_4_.refs_1_.refs_3_
  21.6 1.7 %collective-permute-start.6 = (bf16[48,5120]{1,0:T(8,128)(2,1)S(1)}, bf16[48,5120]{1,0:T(8,128)(2,1)S(1)}, u32[]{:S(2)}, u32[]{:S(2)}) collective-permute-start(bf16[48,5120]{1,0:T(8,128)(2,1)S(1)} %pack.3.refs_2_), channel_id=1, source_target_pairs={{0,1},{1,0},{2,3},{3,2},{4,5},{5,4},{6,7},{7,6},{8,9},{9,8},{10,11... | collective-permute-start | bytes 1474568 | tf_op jit(solution)/shard_map/ppermute | solution.py:63
  23.3 4.1 %collective-permute-start.5 = (bf16[16,5120]{1,0:T(8,128)(2,1)S(1)}, bf16[16,5120]{1,0:T(8,128)(2,1)S(1)}, u32[]{:S(2)}, u32[]{:S(2)}) collective-permute-start(bf16[16,5120]{1,0:T(8,128)(2,1)S(1)} %get-tuple-element.45), channel_id=1, source_target_pairs={{0,2},{1,3},{2,4},{3,5},{4,6},{5,7},{6,0},{7,1},{8,10},{9,11},{10,... | collective-permute-start | bytes 491528 | tf_op jit(solution)/shard_map/ppermute | solution.py:58
  27.4 0.8 %collective-permute-start.8 = (bf16[16,5120]{1,0:T(8,128)(2,1)S(1)}, bf16[16,5120]{1,0:T(8,128)(2,1)S(1)}, u32[]{:S(2)}, u32[]{:S(2)}) collective-permute-start(bf16[16,5120]{1,0:T(8,128)(2,1)S(1)} %get-tuple-element.45), channel_id=1, source_target_pairs={{0,4},{1,5},{2,6},{3,7},{4,0},{5,1},{6,2},{7,3},{8,12},{9,13},{10,... | collective-permute-start | bytes 491528 | tf_op jit(solution)/shard_map/ppermute | solution.py:58
  28.1 1.6 %collective-permute-start.9 = (bf16[16,5120]{1,0:T(8,128)(2,1)S(1)}, bf16[16,5120]{1,0:T(8,128)(2,1)S(1)}, u32[]{:S(2)}, u32[]{:S(2)}) collective-permute-start(bf16[16,5120]{1,0:T(8,128)(2,1)S(1)} %get-tuple-element.45), channel_id=1, source_target_pairs={{0,6},{1,7},{2,0},{3,1},{4,2},{5,3},{6,4},{7,5},{8,14},{9,15},{10,... | collective-permute-start | bytes 491528 | tf_op jit(solution)/shard_map/ppermute | solution.py:58
  29.7 0.0 copy-done
  29.8 3.2 %gates.1 = (f32[5120,384]{1,0:T(8,128)S(1)}, f32[1920,128]{1,0:T(8,128)S(1)}, f32[3,320,128]{2,1,0:T(8,128)S(1)}) custom-call(bf16[5120,384]{1,0:T(8,128)(2,1)S(1)} %copy-done, bf16[5120,40]{1,0:T(8,128)(2,1)S(1)} %get-tuple-element.37.column_ref, f32[8,5120]{1,0:T(8,128)S(1)} %get-tuple-element.38.q_ref), custom_call_target="tpu_custom_call" | custom-call | flops 1000 | bytes 1000 | tf_op jit(solution)/shard_map/gates/pallas_call | solution.py:334
  32.9 0.0 collective-permute-done.5.refs_1_.refs_10_
  33.0 0.4 collective-permute-start.11
  33.4 1.9 %collective-permute-done.6.refs_5_.refs_7_ = bf16[48,5120]{1,0:T(8,128)(2,1)S(1)} collective-permute-done((bf16[48,5120]{1,0:T(8,128)(2,1)S(1)}, bf16[48,5120]{1,0:T(8,128)(2,1)S(1)}, u32[]{:S(2)}, u32[]{:S(2)}) %collective-permute-start.6) | collective-permute-done | bytes 491552 | tf_op jit(solution)/shard_map/ppermute | solution.py:63
  35.2 2.0 %last_state.1 = (bf16[144,384]{1,0:T(8,128)(2,1)S(1)}, f32[5120,384]{1,0:T(8,128)S(1)}, f32[40,384]{1,0:T(8,128)S(1)}) custom-call(bf16[5120,384]{1,0:T(8,128)(2,1)S(1)} %get-tuple-element.42.wt_ref, f32[40,384]{1,0:T(8,128)S(1)} %tie.3.decay_ref, bf16[16,5120]{1,0:T(8,128)(2,1)S(1)} %get-tuple-element.35.refs_0_.refs_2_, ...), custom_call_target="tpu_custom_call" | custom-call | flops 1000 | bytes 1000 | tf_op jit(solution)/shard_map/last_state/pallas_call | solution.py:401
  37.2 0.1 collective-permute-start.7
  37.3 2.3 %collective-permute-done.8.refs_0_.refs_11_ = bf16[16,5120]{1,0:T(8,128)(2,1)S(1)} collective-permute-done((bf16[16,5120]{1,0:T(8,128)(2,1)S(1)}, bf16[16,5120]{1,0:T(8,128)(2,1)S(1)}, u32[]{:S(2)}, u32[]{:S(2)}) %collective-permute-start.8) | collective-permute-done | bytes 163872 | tf_op jit(solution)/shard_map/ppermute | solution.py:58
  39.6 0.0 collective-permute-done.9.refs_1_.refs_12_
  39.7 0.6 collective-permute-start.13
  40.2 1.5 %collective-permute-start.12 = (bf16[32,2048]{1,0:T(8,128)(2,1)S(1)}, bf16[32,2048]{1,0:T(8,128)(2,1)S(1)}, u32[]{:S(2)}, u32[]{:S(2)}) collective-permute-start(bf16[32,2048]{1,0:T(8,128)(2,1)S(1)} %get-tuple-element.50), channel_id=1, source_target_pairs={{0,1},{1,0},{2,3},{3,2},{4,5},{5,4},{6,7},{7,6},{8,9},{9,8},{10,11... | collective-permute-start | bytes 393224 | tf_op jit(solution)/shard_map/ppermute | solution.py:63
  41.8 0.0 collective-permute-done.7.other_ref.refs_0_
  41.8 0.1 join.1
  41.8 2.4 %collective-permute-start.10 = (bf16[144,384]{1,0:T(8,128)(2,1)S(1)}, bf16[144,384]{1,0:T(8,128)(2,1)S(1)}, u32[]{:S(2)}, u32[]{:S(2)}) collective-permute-start(bf16[144,384]{1,0:T(8,128)(2,1)S(1)} %join.1), channel_id=1, source_target_pairs={{0,16},{8,24},{1,17},{9,25},{2,18},{10,26},{3,19},{11,27},{4,20},{... | collective-permute-start | bytes 331784 | tf_op jit(solution)/shard_map/ppermute | solution.py:650
  44.2 0.0 collective-permute-done.11.refs_9_
  44.2 3.3 %collective-permute-done.13.refs_13_ = bf16[32,3072]{1,0:T(8,128)(2,1)S(1)} collective-permute-done((bf16[32,3072]{1,0:T(8,128)(2,1)S(1)}, bf16[32,3072]{1,0:T(8,128)(2,1)S(1)}, u32[]{:S(2)}, u32[]{:S(2)}) %collective-permute-start.13) | collective-permute-done | bytes 196640 | tf_op jit(solution)/shard_map/ppermute | solution.py:63
  47.5 0.0 collective-permute-done.10.refs_1_
  47.5 4.6 %scan.2 = (bf16[5120,384]{1,0:T(8,128)(2,1)S(1)}, f32[40,128]{1,0:T(8,128)S(1)}) custom-call(f32[5120,384]{1,0:T(8,128)S(1)} %get-tuple-element.39.gate_ref, f32[1920,128]{1,0:T(8,128)S(1)} %get-tuple-element.40.factor_ref, f32[3,320,128]{2,1,0:T(8,128)S(1)} %get-tuple-element.41.refs_2_.start_ref, bf16[5120,384]{1,0:T(8,128)(2,1)S(1)} %get-tuple-element.36.refs_3_.xs_ref, ...), custom_call_target="tpu_custom_call" | custom-call | flops 1000 | bytes 1000 | tf_op jit(solution)/shard_map/scan/pallas_call | solution.py:542
  52.1 0.0 collective-permute-done.12.refs_13_
  52.1 0.0 copy-start.3
  52.1 3.1 %scan.3 = (bf16[5120,384]{1,0:T(8,128)(2,1)S(1)}, f32[40,128]{1,0:T(8,128)S(1)}) custom-call(f32[5120,384]{1,0:T(8,128)S(1)} %get-tuple-element.39.gate_ref, f32[1920,128]{1,0:T(8,128)S(1)} %get-tuple-element.40.factor_ref, f32[3,320,128]{2,1,0:T(8,128)S(1)} %get-tuple-element.41.refs_2_.start_ref, ...), custom_call_target="tpu_custom_call", output_to_operand_aliasing={{0}: (20, {}), {1}: (21, {})} | custom-call | flops 1000 | bytes 1000 | tf_op jit(solution)/shard_map/scan/pallas_call | solution.py:542
  55.2 4.0 %collective-permute-start.14 = (f32[40,128]{1,0:T(8,128)S(1)}, f32[40,128]{1,0:T(8,128)S(1)}, u32[]{:S(2)}, u32[]{:S(2)}) collective-permute-start(f32[40,128]{1,0:T(8,128)S(1)} %get-tuple-element.54), channel_id=1, source_target_pairs={{0,2},{1,3},{2,4},{3,5},{4,6},{5,7},{6,0},{7,1},{8,10},{9,11},{10,... | collective-permute-start | bytes 61448 | tf_op jit(solution)/shard_map/ppermute | solution.py:58
  59.2 1.5 %collective-permute-start.15 = (f32[40,128]{1,0:T(8,128)S(1)}, f32[40,128]{1,0:T(8,128)S(1)}, u32[]{:S(2)}, u32[]{:S(2)}) collective-permute-start(f32[40,128]{1,0:T(8,128)S(1)} %get-tuple-element.54), channel_id=1, source_target_pairs={{0,4},{1,5},{2,6},{3,7},{4,0},{5,1},{6,2},{7,3},{8,12},{9,13},{10,... | collective-permute-start | bytes 61448 | tf_op jit(solution)/shard_map/ppermute | solution.py:58
  60.7 0.9 %collective-permute-start.16 = (f32[40,128]{1,0:T(8,128)S(1)}, f32[40,128]{1,0:T(8,128)S(1)}, u32[]{:S(2)}, u32[]{:S(2)}) collective-permute-start(f32[40,128]{1,0:T(8,128)S(1)} %get-tuple-element.54), channel_id=1, source_target_pairs={{0,6},{1,7},{2,0},{3,1},{4,2},{5,3},{6,4},{7,5},{8,14},{9,15},{10,... | collective-permute-start | bytes 61448 | tf_op jit(solution)/shard_map/ppermute | solution.py:58
  61.5 0.4 collective-permute-done.14
  61.9 1.9 %collective-permute-done.15 = f32[40,128]{1,0:T(8,128)S(1)} collective-permute-done((f32[40,128]{1,0:T(8,128)S(1)}, f32[40,128]{1,0:T(8,128)S(1)}, u32[]{:S(2)}, u32[]{:S(2)}) %collective-permute-start.15) | collective-permute-done | bytes 20512 | tf_op jit(solution)/shard_map/ppermute | solution.py:58
  63.8 0.6 collective-permute-done.16
  64.5 0.8 %collective-permute-start.17 = (f32[40,128]{1,0:T(8,128)S(1)}, f32[40,128]{1,0:T(8,128)S(1)}, u32[]{:S(2)}, u32[]{:S(2)}) collective-permute-start(f32[40,128]{1,0:T(8,128)S(1)} %add_add_fusion.refs_0_), channel_id=1, source_target_pairs={{0,1},{1,0},{2,3},{3,2},{4,5},{5,4},{6,7},{7,6},{8,9},{9,8},{10,11... | collective-permute-start | bytes 61448 | tf_op jit(solution)/shard_map/ppermute | solution.py:63
  65.2 0.0 copy-done.3
  65.3 3.1 %collective-permute-done.17.refs_1_ = f32[40,128]{1,0:T(8,128)S(1)} collective-permute-done((f32[40,128]{1,0:T(8,128)S(1)}, f32[40,128]{1,0:T(8,128)S(1)}, u32[]{:S(2)}, u32[]{:S(2)}) %collective-permute-start.17) | collective-permute-done | bytes 20512 | tf_op jit(solution)/shard_map/ppermute | solution.py:63
  68.3 2.3 %norm.1 = bf16[5120,384]{1,0:T(8,128)(2,1)} custom-call(bf16[5120,384]{1,0:T(8,128)(2,1)S(1)} %get-tuple-element.53.gated_ref, f32[1,384]{1,0:T(1,128)S(1)} %broadcast_in_dim.7.gain_ref, f32[40,128]{1,0:T(8,128)S(1)} %add_add_fusion.refs_0_, f32[40,128]{1,0:T(8,128)S(1)} %collective-permute-done.17.refs_1_), custom_call_target="tpu_custom_call" | custom-call | flops 1000 | bytes 1000 | tf_op jit(solution)/shard_map/norm/pallas_call | solution.py:586
  (8 shorter events, 0.1 us)
Async XLA Ops:
  0.0 3.5 %copy-start.4 = (bf16[4,16]{1,0:T(4,128)(2,1)S(1)}, bf16[4,16]{1,0:T(4,128)(2,1)}, u32[]{:S(2)}) copy-start(bf16[4,16]{1,0:T(4,128)(2,1)} %param.16) | copy-start | bytes 388
  0.0 3.6 %copy-start.5 = (bf16[4,16]{1,0:T(4,128)(2,1)S(1)}, bf16[4,16]{1,0:T(4,128)(2,1)}, u32[]{:S(2)}) copy-start(bf16[4,16]{1,0:T(4,128)(2,1)} %param.17) | copy-start | bytes 388
  0.0 12.9 %copy-start.6 = (f32[6]{0:T(128)S(1)}, f32[6]{0:T(128)}, u32[]{:S(2)}) copy-start(f32[6]{0:T(128)} %param.18) | copy-start | bytes 76
  0.0 13.0 %copy-start.1 = (f32[5120,6]{0,1:T(8,128)S(1)}, f32[5120,6]{0,1:T(8,128)}, u32[]{:S(2)}) copy-start(f32[5120,6]{0,1:T(8,128)} %param.14) | copy-start | bytes 368644
  0.0 14.3 %copy-start.2 = (bf16[4,384]{1,0:T(4,128)(2,1)S(1)}, bf16[4,384]{1,0:T(4,128)(2,1)}, u32[]{:S(2)}) copy-start(bf16[4,384]{1,0:T(4,128)(2,1)} %param.15) | copy-start | bytes 9220
  1.1 3.2 %collective-permute-start = (bf16[48,384]{1,0:T(8,128)(2,1)S(1)}, bf16[48,384]{1,0:T(8,128)(2,1)S(1)}, u32[]{:S(2)}, u32[]{:S(2)}) collective-permute-start(bf16[48,384]{1,0:T(8,128)(2,1)S(1)} %get-tuple-element.32), channel_id=1, source_target_pairs={{0,8},{8,16},{16,24},{1,9},{9,17},{17,25},{2,10},{10,18},{18,26},{... | collective-permute-start | bytes 110600 | tf_op jit(solution)/shard_map/ppermute | solution.py:607
  5.0 16.1 %collective-permute-start.1 = (bf16[16,5120]{1,0:T(8,128)(2,1)S(1)}, bf16[16,5120]{1,0:T(8,128)(2,1)S(1)}, u32[]{:S(2)}, u32[]{:S(2)}) collective-permute-start(bf16[16,5120]{1,0:T(8,128)(2,1)S(1)} %get-tuple-element.35.refs_0_.refs_2_), channel_id=1, source_target_pairs={{0,2},{1,3},{2,4},{3,5},{4,6},{5,7},{6,0},{7,1},{8,10},{9,11},{10,... | collective-permute-start | bytes 491528 | tf_op jit(solution)/shard_map/ppermute | solution.py:58
  7.4 14.1 %collective-permute-start.2 = (bf16[16,5120]{1,0:T(8,128)(2,1)S(1)}, bf16[16,5120]{1,0:T(8,128)(2,1)S(1)}, u32[]{:S(2)}, u32[]{:S(2)}) collective-permute-start(bf16[16,5120]{1,0:T(8,128)(2,1)S(1)} %get-tuple-element.35.refs_0_.refs_2_), channel_id=1, source_target_pairs={{0,4},{1,5},{2,6},{3,7},{4,0},{5,1},{6,2},{7,3},{8,12},{9,13},{10,... | collective-permute-start | bytes 491528 | tf_op jit(solution)/shard_map/ppermute | solution.py:58
  10.0 11.5 %collective-permute-start.3 = (bf16[16,5120]{1,0:T(8,128)(2,1)S(1)}, bf16[16,5120]{1,0:T(8,128)(2,1)S(1)}, u32[]{:S(2)}, u32[]{:S(2)}) collective-permute-start(bf16[16,5120]{1,0:T(8,128)(2,1)S(1)} %get-tuple-element.35.refs_0_.refs_2_), channel_id=1, source_target_pairs={{0,6},{1,7},{2,0},{3,1},{4,2},{5,3},{6,4},{7,5},{8,14},{9,15},{10,... | collective-permute-start | bytes 491528 | tf_op jit(solution)/shard_map/ppermute | solution.py:58
  11.4 10.2 %collective-permute-start.4 = (bf16[16,5120]{1,0:T(8,128)(2,1)S(1)}, bf16[16,5120]{1,0:T(8,128)(2,1)S(1)}, u32[]{:S(2)}, u32[]{:S(2)}) collective-permute-start(bf16[16,5120]{1,0:T(8,128)(2,1)S(1)} %get-tuple-element.35.refs_0_.refs_2_), channel_id=1, source_target_pairs={{0,1},{1,0},{2,3},{3,2},{4,5},{5,4},{6,7},{7,6},{8,9},{9,8},{10,11... | collective-permute-start | bytes 491528 | tf_op jit(solution)/shard_map/ppermute | solution.py:63
  21.1 8.6 %copy-start = (bf16[5120,384]{1,0:T(8,128)(2,1)S(1)}, bf16[5120,384]{1,0:T(8,128)(2,1)}, u32[]{:S(2)}) copy-start(bf16[5120,384]{1,0:T(8,128)(2,1)} %z_ref.1) | copy-start | bytes 11796484
  21.6 13.6 %collective-permute-start.6 = (bf16[48,5120]{1,0:T(8,128)(2,1)S(1)}, bf16[48,5120]{1,0:T(8,128)(2,1)S(1)}, u32[]{:S(2)}, u32[]{:S(2)}) collective-permute-start(bf16[48,5120]{1,0:T(8,128)(2,1)S(1)} %pack.3.refs_2_), channel_id=1, source_target_pairs={{0,1},{1,0},{2,3},{3,2},{4,5},{5,4},{6,7},{7,6},{8,9},{9,8},{10,11... | collective-permute-start | bytes 1474568 | tf_op jit(solution)/shard_map/ppermute | solution.py:63
  23.3 9.6 %collective-permute-start.5 = (bf16[16,5120]{1,0:T(8,128)(2,1)S(1)}, bf16[16,5120]{1,0:T(8,128)(2,1)S(1)}, u32[]{:S(2)}, u32[]{:S(2)}) collective-permute-start(bf16[16,5120]{1,0:T(8,128)(2,1)S(1)} %get-tuple-element.45), channel_id=1, source_target_pairs={{0,2},{1,3},{2,4},{3,5},{4,6},{5,7},{6,0},{7,1},{8,10},{9,11},{10,... | collective-permute-start | bytes 491528 | tf_op jit(solution)/shard_map/ppermute | solution.py:58
  27.4 12.2 %collective-permute-start.8 = (bf16[16,5120]{1,0:T(8,128)(2,1)S(1)}, bf16[16,5120]{1,0:T(8,128)(2,1)S(1)}, u32[]{:S(2)}, u32[]{:S(2)}) collective-permute-start(bf16[16,5120]{1,0:T(8,128)(2,1)S(1)} %get-tuple-element.45), channel_id=1, source_target_pairs={{0,4},{1,5},{2,6},{3,7},{4,0},{5,1},{6,2},{7,3},{8,12},{9,13},{10,... | collective-permute-start | bytes 491528 | tf_op jit(solution)/shard_map/ppermute | solution.py:58
  28.1 11.5 %collective-permute-start.9 = (bf16[16,5120]{1,0:T(8,128)(2,1)S(1)}, bf16[16,5120]{1,0:T(8,128)(2,1)S(1)}, u32[]{:S(2)}, u32[]{:S(2)}) collective-permute-start(bf16[16,5120]{1,0:T(8,128)(2,1)S(1)} %get-tuple-element.45), channel_id=1, source_target_pairs={{0,6},{1,7},{2,0},{3,1},{4,2},{5,3},{6,4},{7,5},{8,14},{9,15},{10,... | collective-permute-start | bytes 491528 | tf_op jit(solution)/shard_map/ppermute | solution.py:58
  33.0 11.2 %collective-permute-start.11 = (bf16[32,5120]{1,0:T(8,128)(2,1)S(1)}, bf16[32,5120]{1,0:T(8,128)(2,1)S(1)}, u32[]{:S(2)}, u32[]{:S(2)}) collective-permute-start(bf16[32,5120]{1,0:T(8,128)(2,1)S(1)} %pack.4.refs_1_), channel_id=1, source_target_pairs={{0,1},{1,0},{2,3},{3,2},{4,5},{5,4},{6,7},{7,6},{8,9},{9,8},{10,11... | collective-permute-start | bytes 983048 | tf_op jit(solution)/shard_map/ppermute | solution.py:63
  37.2 4.5 %collective-permute-start.7 = (bf16[144,384]{1,0:T(8,128)(2,1)S(1)}, bf16[144,384]{1,0:T(8,128)(2,1)S(1)}, u32[]{:S(2)}, u32[]{:S(2)}) collective-permute-start(bf16[144,384]{1,0:T(8,128)(2,1)S(1)} %get-tuple-element.48.refs_2_.mine_ref), channel_id=1, source_target_pairs={{0,8},{8,0},{16,24},{24,16},{1,9},{9,1},{17,25},{25,17},{2,10},{10... | collective-permute-start | bytes 331784 | tf_op jit(solution)/shard_map/ppermute | solution.py:650
  39.7 7.8 %collective-permute-start.13 = (bf16[32,3072]{1,0:T(8,128)(2,1)S(1)}, bf16[32,3072]{1,0:T(8,128)(2,1)S(1)}, u32[]{:S(2)}, u32[]{:S(2)}) collective-permute-start(bf16[32,3072]{1,0:T(8,128)(2,1)S(1)} %get-tuple-element.49.token_ref), channel_id=1, source_target_pairs={{0,1},{1,0},{2,3},{3,2},{4,5},{5,4},{6,7},{7,6},{8,9},{9,8},{10,11... | collective-permute-start | bytes 589832 | tf_op jit(solution)/shard_map/ppermute | solution.py:63
  40.2 11.9 %collective-permute-start.12 = (bf16[32,2048]{1,0:T(8,128)(2,1)S(1)}, bf16[32,2048]{1,0:T(8,128)(2,1)S(1)}, u32[]{:S(2)}, u32[]{:S(2)}) collective-permute-start(bf16[32,2048]{1,0:T(8,128)(2,1)S(1)} %get-tuple-element.50), channel_id=1, source_target_pairs={{0,1},{1,0},{2,3},{3,2},{4,5},{5,4},{6,7},{7,6},{8,9},{9,8},{10,11... | collective-permute-start | bytes 393224 | tf_op jit(solution)/shard_map/ppermute | solution.py:63
  41.8 5.7 %collective-permute-start.10 = (bf16[144,384]{1,0:T(8,128)(2,1)S(1)}, bf16[144,384]{1,0:T(8,128)(2,1)S(1)}, u32[]{:S(2)}, u32[]{:S(2)}) collective-permute-start(bf16[144,384]{1,0:T(8,128)(2,1)S(1)} %join.1), channel_id=1, source_target_pairs={{0,16},{8,24},{1,17},{9,25},{2,18},{10,26},{3,19},{11,27},{4,20},{... | collective-permute-start | bytes 331784 | tf_op jit(solution)/shard_map/ppermute | solution.py:650
  52.1 13.1 %copy-start.3 = (f32[384]{0:T(512)S(1)}, f32[384]{0:T(512)}, u32[]{:S(2)}) copy-start(f32[384]{0:T(512)} %param.19) | copy-start | bytes 4612
  55.2 6.8 %collective-permute-start.14 = (f32[40,128]{1,0:T(8,128)S(1)}, f32[40,128]{1,0:T(8,128)S(1)}, u32[]{:S(2)}, u32[]{:S(2)}) collective-permute-start(f32[40,128]{1,0:T(8,128)S(1)} %get-tuple-element.54), channel_id=1, source_target_pairs={{0,2},{1,3},{2,4},{3,5},{4,6},{5,7},{6,0},{7,1},{8,10},{9,11},{10,... | collective-permute-start | bytes 61448 | tf_op jit(solution)/shard_map/ppermute | solution.py:58
  59.2 4.7 %collective-permute-start.15 = (f32[40,128]{1,0:T(8,128)S(1)}, f32[40,128]{1,0:T(8,128)S(1)}, u32[]{:S(2)}, u32[]{:S(2)}) collective-permute-start(f32[40,128]{1,0:T(8,128)S(1)} %get-tuple-element.54), channel_id=1, source_target_pairs={{0,4},{1,5},{2,6},{3,7},{4,0},{5,1},{6,2},{7,3},{8,12},{9,13},{10,... | collective-permute-start | bytes 61448 | tf_op jit(solution)/shard_map/ppermute | solution.py:58
  60.7 3.8 %collective-permute-start.16 = (f32[40,128]{1,0:T(8,128)S(1)}, f32[40,128]{1,0:T(8,128)S(1)}, u32[]{:S(2)}, u32[]{:S(2)}) collective-permute-start(f32[40,128]{1,0:T(8,128)S(1)} %get-tuple-element.54), channel_id=1, source_target_pairs={{0,6},{1,7},{2,0},{3,1},{4,2},{5,3},{6,4},{7,5},{8,14},{9,15},{10,... | collective-permute-start | bytes 61448 | tf_op jit(solution)/shard_map/ppermute | solution.py:58
  64.5 3.8 %collective-permute-start.17 = (f32[40,128]{1,0:T(8,128)S(1)}, f32[40,128]{1,0:T(8,128)S(1)}, u32[]{:S(2)}, u32[]{:S(2)}) collective-permute-start(f32[40,128]{1,0:T(8,128)S(1)} %add_add_fusion.refs_0_), channel_id=1, source_target_pairs={{0,1},{1,0},{2,3},{3,2},{4,5},{5,4},{6,7},{7,6},{8,9},{9,8},{10,11... | collective-permute-start | bytes 61448 | tf_op jit(solution)/shard_map/ppermute | solution.py:63

commit v4 on v3

--- a/solution.py
+++ b/solution.py
@@ -623,24 +623,24 @@
         token, tail, runs = mine, [], [((0, tiles), None, None)]
     else:
         one, two = (0, cols), (0, 2 * cols)
-        b_outer, own = along_outer(bs), along_inner([bs])
+        b_outer, own, c_own = along_outer(bs), along_inner([bs]), along_inner([cs])
         xs, weighted = conv(0, tiles)
-        (b_packed,) = pack(b_outer, [one] * 3, xs, *own)
+        (b_packed,) = pack(b_outer, [one] * 3, xs, *own, *c_own)
         b_passed = along_inner([b_packed])
         cs_sent, columns = after([cs_sent, columns], b_packed)
         c_outer = along_outer(cs_sent)
         gate, factor, start = gates(z_rows, columns, q, local_heads)
-        (c_first,) = pack([cs, c_outer[0]], [one] * 2, start)
-        c_passed = along_inner([c_first])
-        (decays,) = after([decays], c_first)
+        c_outer[:1] = after(c_outer[:1], start)
+        c_passed = c_own + along_inner(c_outer[:1])
+        (decays,) = after([decays], c_outer[0])
         b_pieces = [bs, *own, *b_outer, *b_passed]
         b_rows = [one] * 5 + [(0, 3 * cols)]
         mine, local, before = last_state(weighted, decays, b_pieces, b_rows)
         cut = -(-tiles // 2) * TILE
-        c_rest = pack(c_outer[1:], [one] * 2, mine, cuts=[0, cut, length])
+        c_rest = pack(c_outer[1:], [one] * 2, mine, c_passed[1], cuts=[0, cut, length])
         c_ends = along_inner(c_rest)
-        c_pieces = [cs, *c_passed, *c_outer, *c_passed]
-        c_rows = [one] * 5 + [(cols, 2 * cols)]
+        c_pieces = [cs, *c_own, *c_outer, c_passed[1]]
+        c_rows = [one] * 6
         token, tail = c_rest[0], [two]
         runs = [((0, cut // TILE), c_ends[0], 0), ((cut // TILE, tiles), c_ends[1], cut)]
     others, bit = [], 1

time: 70.9 us -> 71.2 us (level)
  waiting for transfers between devices: 14.6 us -> 18.9 us
  starting transfers between devices: 30.5 us -> 26.5 us
    ppermute x9, starting transfers between devices: 19.2 us -> 15.7 us  [along_outer(): lax.ppermute(piece, 'head', outer_pairs(d))]
    ppermute x9, waiting for transfers between devices: 5.7 us -> 8.13 us  [along_outer(): lax.ppermute(piece, 'head', outer_pairs(d))]
    ppermute x6 -> x7, waiting for transfers between devices: 8.23 us -> 10.1 us  [along_inner(): lax.ppermute(p, 'head', inner_pairs(e))]
    ppermute x2, starting transfers between devices: 2.46 us -> 1.63 us  [body(): others.append(lax.ppermute(mine, 'seq', pairs))]
    ppermute x6 -> x7, starting transfers between devices: 6.47 us -> 6.78 us  [along_inner(): lax.ppermute(p, 'head', inner_pairs(e))]
  transfers between devices with their start and end apart: 18 -> 19, of which waited for: 9 -> 9; matrix products, arithmetic and copies ran while one was open for 0% -> 0% of each run, Pallas kernels for 25% -> 25%
where the time goes in v4:
time: 71.2 us; the launch traced here: 70.9 us
  starting transfers between devices  26.5 us (37%)
  Pallas kernels  25 us (35%)
  waiting for transfers between devices  18.9 us (27%)
    ppermute x9, starting transfers between devices, along_outer(): lax.ppermute(piece, 'head', outer_pairs(d))  15.7 us
    ppermute x7, waiting for transfers between devices, along_inner(): lax.ppermute(p, 'head', inner_pairs(e))  10.1 us
    ppermute x9, waiting for transfers between devices, along_outer(): lax.ppermute(piece, 'head', outer_pairs(d))  8.13 us
    pallas_call x2, Pallas kernels, scan(): pl.pallas_call(functools.partial(scan_kernel, span, len(others), b_rows,...  7.68 us
    pallas_call x1, Pallas kernels, head_conv(): pl.pallas_call(functools.partial(head_conv_kernel, first, heads), grid=(c...  6.84 us
    ppermute x7, starting transfers between devices, along_inner(): lax.ppermute(p, 'head', inner_pairs(e))  6.78 us
    pallas_call x1, Pallas kernels, gates(): pl.pallas_call(gates_kernel, grid=(length // TILE,), in_specs=[wide, pl.B...  3.16 us
    ppermute x1, starting transfers between devices, body(): halo = lax.ppermute(ends, 'seq', [(i, i + 1) for i in range(seq - 1)])  2.39 us
  transfers between devices with their start and end apart: 19, of which 9 were waited for; matrix products, arithmetic and copies ran while one was open for 0% of the time, Pallas kernels for 25%

profile of v4, /device:TPU:0, one launch (start us, length us, event | category | flops | bytes accessed | tf_op | source)
XLA Modules:
  0.0 70.9 jit_solution(1202213686547656694)
XLA Ops:
  0.0 0.0 copy-start.4
  0.0 0.0 copy-start.5
  0.0 0.0 copy-start.6
  0.0 0.0 copy-start.1
  0.0 0.0 copy-start.2
  0.0 1.1 %tails.1 = (bf16[48,384]{1,0:T(8,128)(2,1)S(1)}, bf16[16,5120]{1,0:T(8,128)(2,1)S(1)}, bf16[16,5120]{1,0:T(8,128)(2,1)S(1)}) custom-call(bf16[5120,384]{1,0:T(8,128)(2,1)} %before_ref.1, bf16[16,5120]{1,0:T(8,128)(2,1)} %bitcast.9, bf16[16,5120]{1,0:T(8,128)(2,1)} %bitcast.10), custom_call_target="tpu_custom_call" | custom-call | flops 1000 | bytes 1000 | tf_op jit(solution)/shard_map/tails/pallas_call | solution.py:124
  1.1 2.4 %collective-permute-start = (bf16[48,384]{1,0:T(8,128)(2,1)S(1)}, bf16[48,384]{1,0:T(8,128)(2,1)S(1)}, u32[]{:S(2)}, u32[]{:S(2)}) collective-permute-start(bf16[48,384]{1,0:T(8,128)(2,1)S(1)} %get-tuple-element.32), channel_id=1, source_target_pairs={{0,8},{8,16},{16,24},{1,9},{9,17},{17,25},{2,10},{10,18},{18,26},{... | collective-permute-start | bytes 110600 | tf_op jit(solution)/shard_map/ppermute | solution.py:607
  3.5 0.0 copy-done.4
  3.5 0.1 copy.20
  3.6 0.0 copy-done.5
  3.6 0.1 copy.21
  3.7 0.7 collective-permute-done.halo_ref
  4.4 0.6 shared_conv.1
  5.0 2.5 %collective-permute-start.1 = (bf16[16,5120]{1,0:T(8,128)(2,1)S(1)}, bf16[16,5120]{1,0:T(8,128)(2,1)S(1)}, u32[]{:S(2)}, u32[]{:S(2)}) collective-permute-start(bf16[16,5120]{1,0:T(8,128)(2,1)S(1)} %get-tuple-element.35.refs_0_.refs_2_), channel_id=1, source_target_pairs={{0,2},{1,3},{2,4},{3,5},{4,6},{5,7},{6,0},{7,1},{8,10},{9,11},{10,... | collective-permute-start | bytes 491528 | tf_op jit(solution)/shard_map/ppermute | solution.py:58
  7.4 2.6 %collective-permute-start.2 = (bf16[16,5120]{1,0:T(8,128)(2,1)S(1)}, bf16[16,5120]{1,0:T(8,128)(2,1)S(1)}, u32[]{:S(2)}, u32[]{:S(2)}) collective-permute-start(bf16[16,5120]{1,0:T(8,128)(2,1)S(1)} %get-tuple-element.35.refs_0_.refs_2_), channel_id=1, source_target_pairs={{0,4},{1,5},{2,6},{3,7},{4,0},{5,1},{6,2},{7,3},{8,12},{9,13},{10,... | collective-permute-start | bytes 491528 | tf_op jit(solution)/shard_map/ppermute | solution.py:58
  10.0 1.3 %collective-permute-start.3 = (bf16[16,5120]{1,0:T(8,128)(2,1)S(1)}, bf16[16,5120]{1,0:T(8,128)(2,1)S(1)}, u32[]{:S(2)}, u32[]{:S(2)}) collective-permute-start(bf16[16,5120]{1,0:T(8,128)(2,1)S(1)} %get-tuple-element.35.refs_0_.refs_2_), channel_id=1, source_target_pairs={{0,6},{1,7},{2,0},{3,1},{4,2},{5,3},{6,4},{7,5},{8,14},{9,15},{10,... | collective-permute-start | bytes 491528 | tf_op jit(solution)/shard_map/ppermute | solution.py:58
  11.4 1.5 %collective-permute-start.4 = (bf16[16,5120]{1,0:T(8,128)(2,1)S(1)}, bf16[16,5120]{1,0:T(8,128)(2,1)S(1)}, u32[]{:S(2)}, u32[]{:S(2)}) collective-permute-start(bf16[16,5120]{1,0:T(8,128)(2,1)S(1)} %get-tuple-element.35.refs_0_.refs_2_), channel_id=1, source_target_pairs={{0,1},{1,0},{2,3},{3,2},{4,5},{5,4},{6,7},{7,6},{8,9},{9,8},{10,11... | collective-permute-start | bytes 491528 | tf_op jit(solution)/shard_map/ppermute | solution.py:63
  12.9 0.5 collective-permute-start.5
  13.4 0.0 copy-done.6
  13.4 0.1 copy.22.rate_ref
  13.5 0.0 copy-done.1
  13.5 1.3 %rows.1 = (f32[8,5120]{1,0:T(8,128)S(1)}, bf16[5120,40]{1,0:T(8,128)(2,1)S(1)}, f32[40,384]{1,0:T(8,128)S(1)}) custom-call(f32[6,5120]{1,0:T(8,128)S(1)} %bitcast.6, f32[6,1]{1,0:T(8,128)S(1)} %copy.22.rate_ref), custom_call_target="tpu_custom_call" | custom-call | flops 1000 | bytes 1000 | tf_op jit(solution)/shard_map/rows/pallas_call | solution.py:219
  14.8 0.0 copy-done.2
  14.8 6.8 %head_conv.1 = (bf16[5120,384]{1,0:T(8,128)(2,1)S(1)}, bf16[5120,384]{1,0:T(8,128)(2,1)S(1)}) custom-call(bf16[5120,384]{1,0:T(8,128)(2,1)} %before_ref.1, bf16[5120,384]{1,0:T(8,128)(2,1)} %before_ref.1, bf16[48,384]{1,0:T(8,128)(2,1)S(1)} %collective-permute-done.halo_ref, f32[4,384]{1,0:T(4,128)S(1)} %convert_element_type.17.taps_ref, ...), custom_call_target="tpu_custom_call" | custom-call | flops 1000 | bytes 1000 | tf_op jit(solution)/shard_map/head_conv/pallas_call | solution.py:275
  21.6 0.0 copy-start
  21.7 0.0 collective-permute-done.1.refs_0_.refs_2_.refs_4_
  21.7 0.0 collective-permute-done.2.refs_1_.refs_3_.refs_5_
  21.7 0.0 collective-permute-done.3.refs_2_.refs_4_.refs_6_
  21.7 0.0 collective-permute-done.4.refs_4_.refs_1_.refs_3_
  21.7 0.1 collective-permute-done.5.refs_5_.refs_9_
  21.8 1.6 %collective-permute-start.7 = (bf16[48,5120]{1,0:T(8,128)(2,1)S(1)}, bf16[48,5120]{1,0:T(8,128)(2,1)S(1)}, u32[]{:S(2)}, u32[]{:S(2)}) collective-permute-start(bf16[48,5120]{1,0:T(8,128)(2,1)S(1)} %pack.2.refs_2_), channel_id=1, source_target_pairs={{0,1},{1,0},{2,3},{3,2},{4,5},{5,4},{6,7},{7,6},{8,9},{9,8},{10,11... | collective-permute-start | bytes 1474568 | tf_op jit(solution)/shard_map/ppermute | solution.py:63
  23.4 4.0 %collective-permute-start.6 = (bf16[16,5120]{1,0:T(8,128)(2,1)S(1)}, bf16[16,5120]{1,0:T(8,128)(2,1)S(1)}, u32[]{:S(2)}, u32[]{:S(2)}) collective-permute-start(bf16[16,5120]{1,0:T(8,128)(2,1)S(1)} %get-tuple-element.45), channel_id=1, source_target_pairs={{0,2},{1,3},{2,4},{3,5},{4,6},{5,7},{6,0},{7,1},{8,10},{9,11},{10,... | collective-permute-start | bytes 491528 | tf_op jit(solution)/shard_map/ppermute | solution.py:58
  27.4 0.2 collective-permute-start.10
  27.6 1.3 %collective-permute-start.9 = (bf16[16,5120]{1,0:T(8,128)(2,1)S(1)}, bf16[16,5120]{1,0:T(8,128)(2,1)S(1)}, u32[]{:S(2)}, u32[]{:S(2)}) collective-permute-start(bf16[16,5120]{1,0:T(8,128)(2,1)S(1)} %get-tuple-element.45), channel_id=1, source_target_pairs={{0,4},{1,5},{2,6},{3,7},{4,0},{5,1},{6,2},{7,3},{8,12},{9,13},{10,... | collective-permute-start | bytes 491528 | tf_op jit(solution)/shard_map/ppermute | solution.py:58
  28.9 0.0 copy-done
  28.9 3.2 %gates.1 = (f32[5120,384]{1,0:T(8,128)S(1)}, f32[1920,128]{1,0:T(8,128)S(1)}, f32[3,320,128]{2,1,0:T(8,128)S(1)}) custom-call(bf16[5120,384]{1,0:T(8,128)(2,1)S(1)} %copy-done, bf16[5120,40]{1,0:T(8,128)(2,1)S(1)} %get-tuple-element.38.column_ref, f32[8,5120]{1,0:T(8,128)S(1)} %get-tuple-element.39.q_ref), custom_call_target="tpu_custom_call" | custom-call | flops 1000 | bytes 1000 | tf_op jit(solution)/shard_map/gates/pallas_call | solution.py:334
  32.0 0.7 collective-permute-done.6.refs_0_
  32.7 0.5 collective-permute-start.11
  33.2 2.7 %collective-permute-done.7.refs_5_.refs_7_ = bf16[48,5120]{1,0:T(8,128)(2,1)S(1)} collective-permute-done((bf16[48,5120]{1,0:T(8,128)(2,1)S(1)}, bf16[48,5120]{1,0:T(8,128)(2,1)S(1)}, u32[]{:S(2)}, u32[]{:S(2)}) %collective-permute-start.7) | collective-permute-done | bytes 491552 | tf_op jit(solution)/shard_map/ppermute | solution.py:63
  35.9 1.9 %last_state.1 = (bf16[144,384]{1,0:T(8,128)(2,1)S(1)}, f32[5120,384]{1,0:T(8,128)S(1)}, f32[40,384]{1,0:T(8,128)S(1)}) custom-call(bf16[5120,384]{1,0:T(8,128)(2,1)S(1)} %get-tuple-element.43.wt_ref, f32[40,384]{1,0:T(8,128)S(1)} %tie.5.decay_ref, bf16[16,5120]{1,0:T(8,128)(2,1)S(1)} %get-tuple-element.35.refs_0_.refs_2_, ...), custom_call_target="tpu_custom_call" | custom-call | flops 1000 | bytes 1000 | tf_op jit(solution)/shard_map/last_state/pallas_call | solution.py:401
  37.8 0.1 collective-permute-start.8
  37.9 0.0 collective-permute-done.10.refs_1_.refs_12_
  37.9 5.1 %collective-permute-done.9.refs_0_.refs_11_ = bf16[16,5120]{1,0:T(8,128)(2,1)S(1)} collective-permute-done((bf16[16,5120]{1,0:T(8,128)(2,1)S(1)}, bf16[16,5120]{1,0:T(8,128)(2,1)S(1)}, u32[]{:S(2)}, u32[]{:S(2)}) %collective-permute-start.9) | collective-permute-done | bytes 163872 | tf_op jit(solution)/shard_map/ppermute | solution.py:58
  43.0 0.0 collective-permute-done.11.refs_3_.refs_13_
  43.1 0.6 collective-permute-start.14
  43.6 1.5 %collective-permute-start.13 = (bf16[32,2048]{1,0:T(8,128)(2,1)S(1)}, bf16[32,2048]{1,0:T(8,128)(2,1)S(1)}, u32[]{:S(2)}, u32[]{:S(2)}) collective-permute-start(bf16[32,2048]{1,0:T(8,128)(2,1)S(1)} %get-tuple-element.50), channel_id=1, source_target_pairs={{0,1},{1,0},{2,3},{3,2},{4,5},{5,4},{6,7},{7,6},{8,9},{9,8},{10,11... | collective-permute-start | bytes 393224 | tf_op jit(solution)/shard_map/ppermute | solution.py:63
  45.2 0.0 collective-permute-done.8.other_ref.refs_0_
  45.2 0.1 join.1
  45.2 1.6 %collective-permute-start.12 = (bf16[144,384]{1,0:T(8,128)(2,1)S(1)}, bf16[144,384]{1,0:T(8,128)(2,1)S(1)}, u32[]{:S(2)}, u32[]{:S(2)}) collective-permute-start(bf16[144,384]{1,0:T(8,128)(2,1)S(1)} %join.1), channel_id=1, source_target_pairs={{0,16},{8,24},{1,17},{9,25},{2,18},{10,26},{3,19},{11,27},{4,20},{... | collective-permute-start | bytes 331784 | tf_op jit(solution)/shard_map/ppermute | solution.py:650
  46.8 4.1 %collective-permute-done.14.refs_14_ = bf16[32,3072]{1,0:T(8,128)(2,1)S(1)} collective-permute-done((bf16[32,3072]{1,0:T(8,128)(2,1)S(1)}, bf16[32,3072]{1,0:T(8,128)(2,1)S(1)}, u32[]{:S(2)}, u32[]{:S(2)}) %collective-permute-start.14) | collective-permute-done | bytes 196640 | tf_op jit(solution)/shard_map/ppermute | solution.py:63
  50.9 0.0 collective-permute-done.12.refs_1_
  50.9 4.6 %scan.2 = (bf16[5120,384]{1,0:T(8,128)(2,1)S(1)}, f32[40,128]{1,0:T(8,128)S(1)}) custom-call(f32[5120,384]{1,0:T(8,128)S(1)} %get-tuple-element.40.gate_ref, f32[1920,128]{1,0:T(8,128)S(1)} %get-tuple-element.41.factor_ref, f32[3,320,128]{2,1,0:T(8,128)S(1)} %get-tuple-element.42.refs_1_.start_ref, bf16[5120,384]{1,0:T(8,128)(2,1)S(1)} %get-tuple-element.36.refs_3_.xs_ref, ...), custom_call_target="tpu_custom_call" | custom-call | flops 1000 | bytes 1000 | tf_op jit(solution)/shard_map/scan/pallas_call | solution.py:542
  55.5 0.0 collective-permute-done.13.refs_14_
  55.5 3.1 %scan.3 = (bf16[5120,384]{1,0:T(8,128)(2,1)S(1)}, f32[40,128]{1,0:T(8,128)S(1)}) custom-call(f32[5120,384]{1,0:T(8,128)S(1)} %get-tuple-element.40.gate_ref, f32[1920,128]{1,0:T(8,128)S(1)} %get-tuple-element.41.factor_ref, f32[3,320,128]{2,1,0:T(8,128)S(1)} %get-tuple-element.42.refs_1_.start_ref, ...), custom_call_target="tpu_custom_call", output_to_operand_aliasing={{0}: (21, {}), {1}: (22, {})} | custom-call | flops 1000 | bytes 1000 | tf_op jit(solution)/shard_map/scan/pallas_call | solution.py:542
  58.6 0.0 collective-permute-start.15
  58.6 1.7 %collective-permute-start.16 = (f32[40,128]{1,0:T(8,128)S(1)}, f32[40,128]{1,0:T(8,128)S(1)}, u32[]{:S(2)}, u32[]{:S(2)}) collective-permute-start(f32[40,128]{1,0:T(8,128)S(1)} %get-tuple-element.54), channel_id=1, source_target_pairs={{0,4},{1,5},{2,6},{3,7},{4,0},{5,1},{6,2},{7,3},{8,12},{9,13},{10,... | collective-permute-start | bytes 61448 | tf_op jit(solution)/shard_map/ppermute | solution.py:58
  60.3 2.1 %collective-permute-start.17 = (f32[40,128]{1,0:T(8,128)S(1)}, f32[40,128]{1,0:T(8,128)S(1)}, u32[]{:S(2)}, u32[]{:S(2)}) collective-permute-start(f32[40,128]{1,0:T(8,128)S(1)} %get-tuple-element.54), channel_id=1, source_target_pairs={{0,6},{1,7},{2,0},{3,1},{4,2},{5,3},{6,4},{7,5},{8,14},{9,15},{10,... | collective-permute-start | bytes 61448 | tf_op jit(solution)/shard_map/ppermute | solution.py:58
  62.4 1.8 %collective-permute-done.15 = f32[40,128]{1,0:T(8,128)S(1)} collective-permute-done((f32[40,128]{1,0:T(8,128)S(1)}, f32[40,128]{1,0:T(8,128)S(1)}, u32[]{:S(2)}, u32[]{:S(2)}) %collective-permute-start.15) | collective-permute-done | bytes 20512 | tf_op jit(solution)/shard_map/ppermute | solution.py:58
  64.2 0.0 collective-permute-done.16
  64.2 0.6 collective-permute-done.17
  64.7 0.6 collective-permute-start.18
  65.3 0.0 copy-done.3
  65.3 3.3 %collective-permute-done.18.refs_1_ = f32[40,128]{1,0:T(8,128)S(1)} collective-permute-done((f32[40,128]{1,0:T(8,128)S(1)}, f32[40,128]{1,0:T(8,128)S(1)}, u32[]{:S(2)}, u32[]{:S(2)}) %collective-permute-start.18) | collective-permute-done | bytes 20512 | tf_op jit(solution)/shard_map/ppermute | solution.py:63
  68.6 2.3 %norm.1 = bf16[5120,384]{1,0:T(8,128)(2,1)} custom-call(bf16[5120,384]{1,0:T(8,128)(2,1)S(1)} %get-tuple-element.53.gated_ref, f32[1,384]{1,0:T(1,128)S(1)} %broadcast_in_dim.7.gain_ref, f32[40,128]{1,0:T(8,128)S(1)} %add_add_fusion.refs_0_, f32[40,128]{1,0:T(8,128)S(1)} %collective-permute-done.18.refs_1_), custom_call_target="tpu_custom_call" | custom-call | flops 1000 | bytes 1000 | tf_op jit(solution)/shard_map/norm/pallas_call | solution.py:586
  (9 shorter events, 0.1 us)
Async XLA Ops:
  0.0 3.5 %copy-start.4 = (bf16[4,16]{1,0:T(4,128)(2,1)S(1)}, bf16[4,16]{1,0:T(4,128)(2,1)}, u32[]{:S(2)}) copy-start(bf16[4,16]{1,0:T(4,128)(2,1)} %param.16) | copy-start | bytes 388
  0.0 3.6 %copy-start.5 = (bf16[4,16]{1,0:T(4,128)(2,1)S(1)}, bf16[4,16]{1,0:T(4,128)(2,1)}, u32[]{:S(2)}) copy-start(bf16[4,16]{1,0:T(4,128)(2,1)} %param.17) | copy-start | bytes 388
  0.0 13.4 %copy-start.6 = (f32[6]{0:T(128)S(1)}, f32[6]{0:T(128)}, u32[]{:S(2)}) copy-start(f32[6]{0:T(128)} %param.18) | copy-start | bytes 76
  0.0 13.5 %copy-start.1 = (f32[5120,6]{0,1:T(8,128)S(1)}, f32[5120,6]{0,1:T(8,128)}, u32[]{:S(2)}) copy-start(f32[5120,6]{0,1:T(8,128)} %param.14) | copy-start | bytes 368644
  0.0 14.8 %copy-start.2 = (bf16[4,384]{1,0:T(4,128)(2,1)S(1)}, bf16[4,384]{1,0:T(4,128)(2,1)}, u32[]{:S(2)}) copy-start(bf16[4,384]{1,0:T(4,128)(2,1)} %param.15) | copy-start | bytes 9220
  1.1 3.2 %collective-permute-start = (bf16[48,384]{1,0:T(8,128)(2,1)S(1)}, bf16[48,384]{1,0:T(8,128)(2,1)S(1)}, u32[]{:S(2)}, u32[]{:S(2)}) collective-permute-start(bf16[48,384]{1,0:T(8,128)(2,1)S(1)} %get-tuple-element.32), channel_id=1, source_target_pairs={{0,8},{8,16},{16,24},{1,9},{9,17},{17,25},{2,10},{10,18},{18,26},{... | collective-permute-start | bytes 110600 | tf_op jit(solution)/shard_map/ppermute | solution.py:607
  5.0 16.7 %collective-permute-start.1 = (bf16[16,5120]{1,0:T(8,128)(2,1)S(1)}, bf16[16,5120]{1,0:T(8,128)(2,1)S(1)}, u32[]{:S(2)}, u32[]{:S(2)}) collective-permute-start(bf16[16,5120]{1,0:T(8,128)(2,1)S(1)} %get-tuple-element.35.refs_0_.refs_2_), channel_id=1, source_target_pairs={{0,2},{1,3},{2,4},{3,5},{4,6},{5,7},{6,0},{7,1},{8,10},{9,11},{10,... | collective-permute-start | bytes 491528 | tf_op jit(solution)/shard_map/ppermute | solution.py:58
  7.4 14.2 %collective-permute-start.2 = (bf16[16,5120]{1,0:T(8,128)(2,1)S(1)}, bf16[16,5120]{1,0:T(8,128)(2,1)S(1)}, u32[]{:S(2)}, u32[]{:S(2)}) collective-permute-start(bf16[16,5120]{1,0:T(8,128)(2,1)S(1)} %get-tuple-element.35.refs_0_.refs_2_), channel_id=1, source_target_pairs={{0,4},{1,5},{2,6},{3,7},{4,0},{5,1},{6,2},{7,3},{8,12},{9,13},{10,... | collective-permute-start | bytes 491528 | tf_op jit(solution)/shard_map/ppermute | solution.py:58
  10.0 11.7 %collective-permute-start.3 = (bf16[16,5120]{1,0:T(8,128)(2,1)S(1)}, bf16[16,5120]{1,0:T(8,128)(2,1)S(1)}, u32[]{:S(2)}, u32[]{:S(2)}) collective-permute-start(bf16[16,5120]{1,0:T(8,128)(2,1)S(1)} %get-tuple-element.35.refs_0_.refs_2_), channel_id=1, source_target_pairs={{0,6},{1,7},{2,0},{3,1},{4,2},{5,3},{6,4},{7,5},{8,14},{9,15},{10,... | collective-permute-start | bytes 491528 | tf_op jit(solution)/shard_map/ppermute | solution.py:58
  11.4 10.3 %collective-permute-start.4 = (bf16[16,5120]{1,0:T(8,128)(2,1)S(1)}, bf16[16,5120]{1,0:T(8,128)(2,1)S(1)}, u32[]{:S(2)}, u32[]{:S(2)}) collective-permute-start(bf16[16,5120]{1,0:T(8,128)(2,1)S(1)} %get-tuple-element.35.refs_0_.refs_2_), channel_id=1, source_target_pairs={{0,1},{1,0},{2,3},{3,2},{4,5},{5,4},{6,7},{7,6},{8,9},{9,8},{10,11... | collective-permute-start | bytes 491528 | tf_op jit(solution)/shard_map/ppermute | solution.py:63
  12.9 8.9 %collective-permute-start.5 = (bf16[16,5120]{1,0:T(8,128)(2,1)S(1)}, bf16[16,5120]{1,0:T(8,128)(2,1)S(1)}, u32[]{:S(2)}, u32[]{:S(2)}) collective-permute-start(bf16[16,5120]{1,0:T(8,128)(2,1)S(1)} %get-tuple-element.37.refs_8_), channel_id=1, source_target_pairs={{0,1},{1,0},{2,3},{3,2},{4,5},{5,4},{6,7},{7,6},{8,9},{9,8},{10,11... | collective-permute-start | bytes 491528 | tf_op jit(solution)/shard_map/ppermute | solution.py:63
  21.6 7.2 %copy-start = (bf16[5120,384]{1,0:T(8,128)(2,1)S(1)}, bf16[5120,384]{1,0:T(8,128)(2,1)}, u32[]{:S(2)}) copy-start(bf16[5120,384]{1,0:T(8,128)(2,1)} %z_ref.1) | copy-start | bytes 11796484
  21.8 14.0 %collective-permute-start.7 = (bf16[48,5120]{1,0:T(8,128)(2,1)S(1)}, bf16[48,5120]{1,0:T(8,128)(2,1)S(1)}, u32[]{:S(2)}, u32[]{:S(2)}) collective-permute-start(bf16[48,5120]{1,0:T(8,128)(2,1)S(1)} %pack.2.refs_2_), channel_id=1, source_target_pairs={{0,1},{1,0},{2,3},{3,2},{4,5},{5,4},{6,7},{7,6},{8,9},{9,8},{10,11... | collective-permute-start | bytes 1474568 | tf_op jit(solution)/shard_map/ppermute | solution.py:63
  23.4 9.3 %collective-permute-start.6 = (bf16[16,5120]{1,0:T(8,128)(2,1)S(1)}, bf16[16,5120]{1,0:T(8,128)(2,1)S(1)}, u32[]{:S(2)}, u32[]{:S(2)}) collective-permute-start(bf16[16,5120]{1,0:T(8,128)(2,1)S(1)} %get-tuple-element.45), channel_id=1, source_target_pairs={{0,2},{1,3},{2,4},{3,5},{4,6},{5,7},{6,0},{7,1},{8,10},{9,11},{10,... | collective-permute-start | bytes 491528 | tf_op jit(solution)/shard_map/ppermute | solution.py:58
  27.4 10.5 %collective-permute-start.10 = (bf16[16,5120]{1,0:T(8,128)(2,1)S(1)}, bf16[16,5120]{1,0:T(8,128)(2,1)S(1)}, u32[]{:S(2)}, u32[]{:S(2)}) collective-permute-start(bf16[16,5120]{1,0:T(8,128)(2,1)S(1)} %get-tuple-element.45), channel_id=1, source_target_pairs={{0,6},{1,7},{2,0},{3,1},{4,2},{5,3},{6,4},{7,5},{8,14},{9,15},{10,... | collective-permute-start | bytes 491528 | tf_op jit(solution)/shard_map/ppermute | solution.py:58
  27.6 15.4 %collective-permute-start.9 = (bf16[16,5120]{1,0:T(8,128)(2,1)S(1)}, bf16[16,5120]{1,0:T(8,128)(2,1)S(1)}, u32[]{:S(2)}, u32[]{:S(2)}) collective-permute-start(bf16[16,5120]{1,0:T(8,128)(2,1)S(1)} %get-tuple-element.45), channel_id=1, source_target_pairs={{0,4},{1,5},{2,6},{3,7},{4,0},{5,1},{6,2},{7,3},{8,12},{9,13},{10,... | collective-permute-start | bytes 491528 | tf_op jit(solution)/shard_map/ppermute | solution.py:58
  32.7 10.3 %collective-permute-start.11 = (bf16[16,5120]{1,0:T(8,128)(2,1)S(1)}, bf16[16,5120]{1,0:T(8,128)(2,1)S(1)}, u32[]{:S(2)}, u32[]{:S(2)}) collective-permute-start(bf16[16,5120]{1,0:T(8,128)(2,1)S(1)} %tie.4.refs_1_.refs_10_), channel_id=1, source_target_pairs={{0,1},{1,0},{2,3},{3,2},{4,5},{5,4},{6,7},{7,6},{8,9},{9,8},{10,11... | collective-permute-start | bytes 491528 | tf_op jit(solution)/shard_map/ppermute | solution.py:63
  37.8 7.4 %collective-permute-start.8 = (bf16[144,384]{1,0:T(8,128)(2,1)S(1)}, bf16[144,384]{1,0:T(8,128)(2,1)S(1)}, u32[]{:S(2)}, u32[]{:S(2)}) collective-permute-start(bf16[144,384]{1,0:T(8,128)(2,1)S(1)} %get-tuple-element.48.refs_2_.mine_ref), channel_id=1, source_target_pairs={{0,8},{8,0},{16,24},{24,16},{1,9},{9,1},{17,25},{25,17},{2,10},{10... | collective-permute-start | bytes 331784 | tf_op jit(solution)/shard_map/ppermute | solution.py:650
  43.1 7.8 %collective-permute-start.14 = (bf16[32,3072]{1,0:T(8,128)(2,1)S(1)}, bf16[32,3072]{1,0:T(8,128)(2,1)S(1)}, u32[]{:S(2)}, u32[]{:S(2)}) collective-permute-start(bf16[32,3072]{1,0:T(8,128)(2,1)S(1)} %get-tuple-element.49.token_ref), channel_id=1, source_target_pairs={{0,1},{1,0},{2,3},{3,2},{4,5},{5,4},{6,7},{7,6},{8,9},{9,8},{10,11... | collective-permute-start | bytes 589832 | tf_op jit(solution)/shard_map/ppermute | solution.py:63
  43.6 11.8 %collective-permute-start.13 = (bf16[32,2048]{1,0:T(8,128)(2,1)S(1)}, bf16[32,2048]{1,0:T(8,128)(2,1)S(1)}, u32[]{:S(2)}, u32[]{:S(2)}) collective-permute-start(bf16[32,2048]{1,0:T(8,128)(2,1)S(1)} %get-tuple-element.50), channel_id=1, source_target_pairs={{0,1},{1,0},{2,3},{3,2},{4,5},{5,4},{6,7},{7,6},{8,9},{9,8},{10,11... | collective-permute-start | bytes 393224 | tf_op jit(solution)/shard_map/ppermute | solution.py:63
  45.2 5.7 %collective-permute-start.12 = (bf16[144,384]{1,0:T(8,128)(2,1)S(1)}, bf16[144,384]{1,0:T(8,128)(2,1)S(1)}, u32[]{:S(2)}, u32[]{:S(2)}) collective-permute-start(bf16[144,384]{1,0:T(8,128)(2,1)S(1)} %join.1), channel_id=1, source_target_pairs={{0,16},{8,24},{1,17},{9,25},{2,18},{10,26},{3,19},{11,27},{4,20},{... | collective-permute-start | bytes 331784 | tf_op jit(solution)/shard_map/ppermute | solution.py:650
  55.5 9.8 %copy-start.3 = (f32[384]{0:T(512)S(1)}, f32[384]{0:T(512)}, u32[]{:S(2)}) copy-start(f32[384]{0:T(512)} %param.19) | copy-start | bytes 4612
  58.6 5.6 %collective-permute-start.15 = (f32[40,128]{1,0:T(8,128)S(1)}, f32[40,128]{1,0:T(8,128)S(1)}, u32[]{:S(2)}, u32[]{:S(2)}) collective-permute-start(f32[40,128]{1,0:T(8,128)S(1)} %get-tuple-element.54), channel_id=1, source_target_pairs={{0,2},{1,3},{2,4},{3,5},{4,6},{5,7},{6,0},{7,1},{8,10},{9,11},{10,... | collective-permute-start | bytes 61448 | tf_op jit(solution)/shard_map/ppermute | solution.py:58
  58.6 5.6 %collective-permute-start.16 = (f32[40,128]{1,0:T(8,128)S(1)}, f32[40,128]{1,0:T(8,128)S(1)}, u32[]{:S(2)}, u32[]{:S(2)}) collective-permute-start(f32[40,128]{1,0:T(8,128)S(1)} %get-tuple-element.54), channel_id=1, source_target_pairs={{0,4},{1,5},{2,6},{3,7},{4,0},{5,1},{6,2},{7,3},{8,12},{9,13},{10,... | collective-permute-start | bytes 61448 | tf_op jit(solution)/shard_map/ppermute | solution.py:58
  60.3 4.4 %collective-permute-start.17 = (f32[40,128]{1,0:T(8,128)S(1)}, f32[40,128]{1,0:T(8,128)S(1)}, u32[]{:S(2)}, u32[]{:S(2)}) collective-permute-start(f32[40,128]{1,0:T(8,128)S(1)} %get-tuple-element.54), channel_id=1, source_target_pairs={{0,6},{1,7},{2,0},{3,1},{4,2},{5,3},{6,4},{7,5},{8,14},{9,15},{10,... | collective-permute-start | bytes 61448 | tf_op jit(solution)/shard_map/ppermute | solution.py:58
  64.7 3.8 %collective-permute-start.18 = (f32[40,128]{1,0:T(8,128)S(1)}, f32[40,128]{1,0:T(8,128)S(1)}, u32[]{:S(2)}, u32[]{:S(2)}) collective-permute-start(f32[40,128]{1,0:T(8,128)S(1)} %add_add_fusion.refs_0_), channel_id=1, source_target_pairs={{0,1},{1,0},{2,3},{3,2},{4,5},{5,4},{6,7},{7,6},{8,9},{9,8},{10,11... | collective-permute-start | bytes 61448 | tf_op jit(solution)/shard_map/ppermute | solution.py:63

commit v5 on v4

--- a/solution.py
+++ b/solution.py
@@ -622,7 +622,7 @@
         gate, factor, start = gates(z_rows, columns, q, local_heads)
         token, tail, runs = mine, [], [((0, tiles), None, None)]
     else:
-        one, two = (0, cols), (0, 2 * cols)
+        one = (0, cols)
         b_outer, own, c_own = along_outer(bs), along_inner([bs]), along_inner([cs])
         xs, weighted = conv(0, tiles)
         (b_packed,) = pack(b_outer, [one] * 3, xs, *own, *c_own)
@@ -637,11 +637,11 @@
         b_rows = [one] * 5 + [(0, 3 * cols)]
         mine, local, before = last_state(weighted, decays, b_pieces, b_rows)
         cut = -(-tiles // 2) * TILE
-        c_rest = pack(c_outer[1:], [one] * 2, mine, c_passed[1], cuts=[0, cut, length])
+        c_rest = pack(c_outer[:0:-1], [one] * 2, mine, c_passed[1], cuts=[0, cut, length])
         c_ends = along_inner(c_rest)
         c_pieces = [cs, *c_own, *c_outer, c_passed[1]]
         c_rows = [one] * 6
-        token, tail = c_rest[0], [two]
+        token, tail = c_rest[0], [(cols, 2 * cols), one]
         runs = [((0, cut // TILE), c_ends[0], 0), ((cut // TILE, tiles), c_ends[1], cut)]
     others, bit = [], 1
     while bit < seq:
@@ -655,7 +655,7 @@
     for span, piece, begin in runs:
         filled = scan(
             span, gate, factor, start, xs, local, before, others, b_pieces, b_rows,
-            c_pieces + [piece] * len(tail), c_rows + tail, [0] * len(c_pieces) + [begin], filled,
+            c_pieces + [piece] * len(tail), c_rows + tail, [0] * len(c_pieces) + [begin] * len(tail), filled,
         )
     gated, square = filled
     square = square + sum(along_outer(square))

time: 71.2 us -> 70.6 us (level)
  waiting for transfers between devices: 18.9 us -> 12.8 us
  starting transfers between devices: 26.5 us -> 31.9 us
    ppermute x9, waiting for transfers between devices: 8.13 us -> 4.33 us  [along_outer(): lax.ppermute(piece, 'head', outer_pairs(d))]
    ppermute x7, waiting for transfers between devices: 10.1 us -> 7.13 us  [along_inner(): lax.ppermute(p, 'head', inner_pairs(e))]
    ppermute x9, starting transfers between devices: 15.7 us -> 18.3 us  [along_outer(): lax.ppermute(piece, 'head', outer_pairs(d))]
    ppermute x2, starting transfers between devices: 1.63 us -> 4.16 us  [body(): others.append(lax.ppermute(mine, 'seq', pairs))]
    ppermute x2, waiting for transfers between devices: 0.01 us -> 0.73 us  [body(): others.append(lax.ppermute(mine, 'seq', pairs))]
where the time goes in v5:
time: 70.6 us; the launch traced here: 70.3 us
  starting transfers between devices  31.9 us (45%)
  Pallas kernels  25 us (35%)
  waiting for transfers between devices  12.8 us (18%)
    ppermute x9, starting transfers between devices, along_outer(): lax.ppermute(piece, 'head', outer_pairs(d))  18.3 us
    pallas_call x2, Pallas kernels, scan(): pl.pallas_call(functools.partial(scan_kernel, span, len(others), b_rows,...  7.67 us
    ppermute x7, waiting for transfers between devices, along_inner(): lax.ppermute(p, 'head', inner_pairs(e))  7.13 us
    ppermute x7, starting transfers between devices, along_inner(): lax.ppermute(p, 'head', inner_pairs(e))  7.01 us
    pallas_call x1, Pallas kernels, head_conv(): pl.pallas_call(functools.partial(head_conv_kernel, first, heads), grid=(c...  6.84 us
    ppermute x9, waiting for transfers between devices, along_outer(): lax.ppermute(piece, 'head', outer_pairs(d))  4.33 us
    ppermute x2, starting transfers between devices, body(): others.append(lax.ppermute(mine, 'seq', pairs))  4.16 us
    pallas_call x1, Pallas kernels, gates(): pl.pallas_call(gates_kernel, grid=(length // TILE,), in_specs=[wide, pl.B...  3.16 us
  transfers between devices with their start and end apart: 19, of which 9 were waited for; matrix products, arithmetic and copies ran while one was open for 0% of the time, Pallas kernels for 25%

profile of v5, /device:TPU:0, one launch (start us, length us, event | category | flops | bytes accessed | tf_op | source)
XLA Modules:
  0.0 70.3 jit_solution(8548226144033912020)
XLA Ops:
  0.0 0.0 copy-start.4
  0.0 0.0 copy-start.5
  0.0 0.0 copy-start.6
  0.0 0.0 copy-start.2
  0.0 1.1 %tails.1 = (bf16[48,384]{1,0:T(8,128)(2,1)S(1)}, bf16[16,5120]{1,0:T(8,128)(2,1)S(1)}, bf16[16,5120]{1,0:T(8,128)(2,1)S(1)}) custom-call(bf16[5120,384]{1,0:T(8,128)(2,1)} %before_ref.1, bf16[16,5120]{1,0:T(8,128)(2,1)} %bitcast.9, bf16[16,5120]{1,0:T(8,128)(2,1)} %bitcast.10), custom_call_target="tpu_custom_call" | custom-call | flops 1000 | bytes 1000 | tf_op jit(solution)/shard_map/tails/pallas_call | solution.py:124
  1.1 2.4 %collective-permute-start = (bf16[48,384]{1,0:T(8,128)(2,1)S(1)}, bf16[48,384]{1,0:T(8,128)(2,1)S(1)}, u32[]{:S(2)}, u32[]{:S(2)}) collective-permute-start(bf16[48,384]{1,0:T(8,128)(2,1)S(1)} %get-tuple-element.32), channel_id=1, source_target_pairs={{0,8},{8,16},{16,24},{1,9},{9,17},{17,25},{2,10},{10,18},{18,26},{... | collective-permute-start | bytes 110600 | tf_op jit(solution)/shard_map/ppermute | solution.py:607
  3.5 0.0 copy-done.4
  3.5 0.1 copy.20
  3.6 0.0 copy-done.5
  3.6 0.1 copy.21
  3.7 0.7 collective-permute-done.halo_ref
  4.4 0.6 shared_conv.1
  5.0 2.5 %collective-permute-start.1 = (bf16[16,5120]{1,0:T(8,128)(2,1)S(1)}, bf16[16,5120]{1,0:T(8,128)(2,1)S(1)}, u32[]{:S(2)}, u32[]{:S(2)}) collective-permute-start(bf16[16,5120]{1,0:T(8,128)(2,1)S(1)} %get-tuple-element.35.refs_0_.refs_2_), channel_id=1, source_target_pairs={{0,2},{1,3},{2,4},{3,5},{4,6},{5,7},{6,0},{7,1},{8,10},{9,11},{10,... | collective-permute-start | bytes 491528 | tf_op jit(solution)/shard_map/ppermute | solution.py:58
  7.4 2.6 %collective-permute-start.2 = (bf16[16,5120]{1,0:T(8,128)(2,1)S(1)}, bf16[16,5120]{1,0:T(8,128)(2,1)S(1)}, u32[]{:S(2)}, u32[]{:S(2)}) collective-permute-start(bf16[16,5120]{1,0:T(8,128)(2,1)S(1)} %get-tuple-element.35.refs_0_.refs_2_), channel_id=1, source_target_pairs={{0,4},{1,5},{2,6},{3,7},{4,0},{5,1},{6,2},{7,3},{8,12},{9,13},{10,... | collective-permute-start | bytes 491528 | tf_op jit(solution)/shard_map/ppermute | solution.py:58
  10.0 1.3 %collective-permute-start.3 = (bf16[16,5120]{1,0:T(8,128)(2,1)S(1)}, bf16[16,5120]{1,0:T(8,128)(2,1)S(1)}, u32[]{:S(2)}, u32[]{:S(2)}) collective-permute-start(bf16[16,5120]{1,0:T(8,128)(2,1)S(1)} %get-tuple-element.35.refs_0_.refs_2_), channel_id=1, source_target_pairs={{0,6},{1,7},{2,0},{3,1},{4,2},{5,3},{6,4},{7,5},{8,14},{9,15},{10,... | collective-permute-start | bytes 491528 | tf_op jit(solution)/shard_map/ppermute | solution.py:58
  11.4 1.5 %collective-permute-start.4 = (bf16[16,5120]{1,0:T(8,128)(2,1)S(1)}, bf16[16,5120]{1,0:T(8,128)(2,1)S(1)}, u32[]{:S(2)}, u32[]{:S(2)}) collective-permute-start(bf16[16,5120]{1,0:T(8,128)(2,1)S(1)} %get-tuple-element.35.refs_0_.refs_2_), channel_id=1, source_target_pairs={{0,1},{1,0},{2,3},{3,2},{4,5},{5,4},{6,7},{7,6},{8,9},{9,8},{10,11... | collective-permute-start | bytes 491528 | tf_op jit(solution)/shard_map/ppermute | solution.py:63
  12.9 0.5 collective-permute-start.5
  13.4 0.0 copy-done.6
  13.4 0.1 copy.22.rate_ref
  13.5 0.0 copy-done.1
  13.5 1.3 %rows.1 = (f32[8,5120]{1,0:T(8,128)S(1)}, bf16[5120,40]{1,0:T(8,128)(2,1)S(1)}, f32[40,384]{1,0:T(8,128)S(1)}) custom-call(f32[6,5120]{1,0:T(8,128)S(1)} %bitcast.6, f32[6,1]{1,0:T(8,128)S(1)} %copy.22.rate_ref), custom_call_target="tpu_custom_call" | custom-call | flops 1000 | bytes 1000 | tf_op jit(solution)/shard_map/rows/pallas_call | solution.py:219
  14.8 0.0 copy-done.2
  14.8 6.8 %head_conv.1 = (bf16[5120,384]{1,0:T(8,128)(2,1)S(1)}, bf16[5120,384]{1,0:T(8,128)(2,1)S(1)}) custom-call(bf16[5120,384]{1,0:T(8,128)(2,1)} %before_ref.1, bf16[5120,384]{1,0:T(8,128)(2,1)} %before_ref.1, bf16[48,384]{1,0:T(8,128)(2,1)S(1)} %collective-permute-done.halo_ref, f32[4,384]{1,0:T(4,128)S(1)} %convert_element_type.17.taps_ref, ...), custom_call_target="tpu_custom_call" | custom-call | flops 1000 | bytes 1000 | tf_op jit(solution)/shard_map/head_conv/pallas_call | solution.py:275
  21.6 0.0 copy-start
  21.7 0.0 collective-permute-done.1.refs_0_.refs_2_.refs_4_
  21.7 0.0 collective-permute-done.2.refs_1_.refs_3_.refs_5_
  21.7 0.0 collective-permute-done.3.refs_2_.refs_4_.refs_6_
  21.7 0.0 collective-permute-done.4.refs_4_.refs_1_.refs_3_
  21.7 0.1 collective-permute-done.5.refs_5_.refs_9_
  21.8 1.6 %collective-permute-start.7 = (bf16[48,5120]{1,0:T(8,128)(2,1)S(1)}, bf16[48,5120]{1,0:T(8,128)(2,1)S(1)}, u32[]{:S(2)}, u32[]{:S(2)}) collective-permute-start(bf16[48,5120]{1,0:T(8,128)(2,1)S(1)} %pack.2.refs_2_), channel_id=1, source_target_pairs={{0,1},{1,0},{2,3},{3,2},{4,5},{5,4},{6,7},{7,6},{8,9},{9,8},{10,11... | collective-permute-start | bytes 1474568 | tf_op jit(solution)/shard_map/ppermute | solution.py:63
  23.4 4.0 %collective-permute-start.6 = (bf16[16,5120]{1,0:T(8,128)(2,1)S(1)}, bf16[16,5120]{1,0:T(8,128)(2,1)S(1)}, u32[]{:S(2)}, u32[]{:S(2)}) collective-permute-start(bf16[16,5120]{1,0:T(8,128)(2,1)S(1)} %get-tuple-element.45), channel_id=1, source_target_pairs={{0,2},{1,3},{2,4},{3,5},{4,6},{5,7},{6,0},{7,1},{8,10},{9,11},{10,... | collective-permute-start | bytes 491528 | tf_op jit(solution)/shard_map/ppermute | solution.py:58
  27.4 0.8 %collective-permute-start.10 = (bf16[16,5120]{1,0:T(8,128)(2,1)S(1)}, bf16[16,5120]{1,0:T(8,128)(2,1)S(1)}, u32[]{:S(2)}, u32[]{:S(2)}) collective-permute-start(bf16[16,5120]{1,0:T(8,128)(2,1)S(1)} %get-tuple-element.45), channel_id=1, source_target_pairs={{0,4},{1,5},{2,6},{3,7},{4,0},{5,1},{6,2},{7,3},{8,12},{9,13},{10,... | collective-permute-start | bytes 491528 | tf_op jit(solution)/shard_map/ppermute | solution.py:58
  28.2 1.6 %collective-permute-start.9 = (bf16[16,5120]{1,0:T(8,128)(2,1)S(1)}, bf16[16,5120]{1,0:T(8,128)(2,1)S(1)}, u32[]{:S(2)}, u32[]{:S(2)}) collective-permute-start(bf16[16,5120]{1,0:T(8,128)(2,1)S(1)} %get-tuple-element.45), channel_id=1, source_target_pairs={{0,6},{1,7},{2,0},{3,1},{4,2},{5,3},{6,4},{7,5},{8,14},{9,15},{10,... | collective-permute-start | bytes 491528 | tf_op jit(solution)/shard_map/ppermute | solution.py:58
  29.8 0.0 copy-done
  29.8 3.2 %gates.1 = (f32[5120,384]{1,0:T(8,128)S(1)}, f32[1920,128]{1,0:T(8,128)S(1)}, f32[3,320,128]{2,1,0:T(8,128)S(1)}) custom-call(bf16[5120,384]{1,0:T(8,128)(2,1)S(1)} %copy-done, bf16[5120,40]{1,0:T(8,128)(2,1)S(1)} %get-tuple-element.38.column_ref, f32[8,5120]{1,0:T(8,128)S(1)} %get-tuple-element.39.q_ref), custom_call_target="tpu_custom_call" | custom-call | flops 1000 | bytes 1000 | tf_op jit(solution)/shard_map/gates/pallas_call | solution.py:334
  32.9 0.0 collective-permute-done.6.refs_0_
  32.9 0.4 collective-permute-start.11
  33.3 2.5 %collective-permute-done.7.refs_5_.refs_7_ = bf16[48,5120]{1,0:T(8,128)(2,1)S(1)} collective-permute-done((bf16[48,5120]{1,0:T(8,128)(2,1)S(1)}, bf16[48,5120]{1,0:T(8,128)(2,1)S(1)}, u32[]{:S(2)}, u32[]{:S(2)}) %collective-permute-start.7) | collective-permute-done | bytes 491552 | tf_op jit(solution)/shard_map/ppermute | solution.py:63
  35.9 1.9 %last_state.1 = (bf16[144,384]{1,0:T(8,128)(2,1)S(1)}, f32[5120,384]{1,0:T(8,128)S(1)}, f32[40,384]{1,0:T(8,128)S(1)}) custom-call(bf16[5120,384]{1,0:T(8,128)(2,1)S(1)} %get-tuple-element.43.wt_ref, f32[40,384]{1,0:T(8,128)S(1)} %tie.5.decay_ref, bf16[16,5120]{1,0:T(8,128)(2,1)S(1)} %get-tuple-element.35.refs_0_.refs_2_, ...), custom_call_target="tpu_custom_call" | custom-call | flops 1000 | bytes 1000 | tf_op jit(solution)/shard_map/last_state/pallas_call | solution.py:401
  37.8 0.1 collective-permute-start.8
  37.9 1.8 %collective-permute-done.10.refs_1_.refs_11_ = bf16[16,5120]{1,0:T(8,128)(2,1)S(1)} collective-permute-done((bf16[16,5120]{1,0:T(8,128)(2,1)S(1)}, bf16[16,5120]{1,0:T(8,128)(2,1)S(1)}, u32[]{:S(2)}, u32[]{:S(2)}) %collective-permute-start.10) | collective-permute-done | bytes 163872 | tf_op jit(solution)/shard_map/ppermute | solution.py:58
  39.6 0.0 collective-permute-done.9.refs_0_.refs_12_
  39.6 0.0 collective-permute-done.11.refs_3_.refs_13_
  39.7 1.0 %collective-permute-start.14 = (bf16[32,3072]{1,0:T(8,128)(2,1)S(1)}, bf16[32,3072]{1,0:T(8,128)(2,1)S(1)}, u32[]{:S(2)}, u32[]{:S(2)}) collective-permute-start(bf16[32,3072]{1,0:T(8,128)(2,1)S(1)} %get-tuple-element.49.token_ref), channel_id=1, source_target_pairs={{0,1},{1,0},{2,3},{3,2},{4,5},{5,4},{6,7},{7,6},{8,9},{9,8},{10,11... | collective-permute-start | bytes 589832 | tf_op jit(solution)/shard_map/ppermute | solution.py:63
  40.6 1.1 %collective-permute-start.13 = (bf16[32,2048]{1,0:T(8,128)(2,1)S(1)}, bf16[32,2048]{1,0:T(8,128)(2,1)S(1)}, u32[]{:S(2)}, u32[]{:S(2)}) collective-permute-start(bf16[32,2048]{1,0:T(8,128)(2,1)S(1)} %get-tuple-element.50), channel_id=1, source_target_pairs={{0,1},{1,0},{2,3},{3,2},{4,5},{5,4},{6,7},{7,6},{8,9},{9,8},{10,11... | collective-permute-start | bytes 393224 | tf_op jit(solution)/shard_map/ppermute | solution.py:63
  41.8 0.0 collective-permute-done.8.other_ref.refs_0_
  41.8 0.1 join.1
  41.8 4.1 %collective-permute-start.12 = (bf16[144,384]{1,0:T(8,128)(2,1)S(1)}, bf16[144,384]{1,0:T(8,128)(2,1)S(1)}, u32[]{:S(2)}, u32[]{:S(2)}) collective-permute-start(bf16[144,384]{1,0:T(8,128)(2,1)S(1)} %join.1), channel_id=1, source_target_pairs={{0,16},{8,24},{1,17},{9,25},{2,18},{10,26},{3,19},{11,27},{4,20},{... | collective-permute-start | bytes 331784 | tf_op jit(solution)/shard_map/ppermute | solution.py:650
  45.9 1.6 %collective-permute-done.14.refs_14_ = bf16[32,3072]{1,0:T(8,128)(2,1)S(1)} collective-permute-done((bf16[32,3072]{1,0:T(8,128)(2,1)S(1)}, bf16[32,3072]{1,0:T(8,128)(2,1)S(1)}, u32[]{:S(2)}, u32[]{:S(2)}) %collective-permute-start.14) | collective-permute-done | bytes 196640 | tf_op jit(solution)/shard_map/ppermute | solution.py:63
  47.5 0.7 %collective-permute-done.12.refs_1_ = bf16[144,384]{1,0:T(8,128)(2,1)S(1)} collective-permute-done((bf16[144,384]{1,0:T(8,128)(2,1)S(1)}, bf16[144,384]{1,0:T(8,128)(2,1)S(1)}, u32[]{:S(2)}, u32[]{:S(2)}) %collective-permute-start.12) | collective-permute-done | bytes 110624 | tf_op jit(solution)/shard_map/ppermute | solution.py:650
  48.2 4.6 %scan.2 = (bf16[5120,384]{1,0:T(8,128)(2,1)S(1)}, f32[40,128]{1,0:T(8,128)S(1)}) custom-call(f32[5120,384]{1,0:T(8,128)S(1)} %get-tuple-element.40.gate_ref, f32[1920,128]{1,0:T(8,128)S(1)} %get-tuple-element.41.factor_ref, f32[3,320,128]{2,1,0:T(8,128)S(1)} %get-tuple-element.42.refs_1_.start_ref, bf16[5120,384]{1,0:T(8,128)(2,1)S(1)} %get-tuple-element.36.refs_3_.xs_ref, ...), custom_call_target="tpu_custom_call" | custom-call | flops 1000 | bytes 1000 | tf_op jit(solution)/shard_map/scan/pallas_call | solution.py:542
  52.8 0.0 collective-permute-done.13.refs_14_
  52.8 0.0 copy-start.3
  52.8 3.1 %scan.3 = (bf16[5120,384]{1,0:T(8,128)(2,1)S(1)}, f32[40,128]{1,0:T(8,128)S(1)}) custom-call(f32[5120,384]{1,0:T(8,128)S(1)} %get-tuple-element.40.gate_ref, f32[1920,128]{1,0:T(8,128)S(1)} %get-tuple-element.41.factor_ref, f32[3,320,128]{2,1,0:T(8,128)S(1)} %get-tuple-element.42.refs_1_.start_ref, ...), custom_call_target="tpu_custom_call", output_to_operand_aliasing={{0}: (21, {}), {1}: (22, {})} | custom-call | flops 1000 | bytes 1000 | tf_op jit(solution)/shard_map/scan/pallas_call | solution.py:542
  55.9 3.2 %collective-permute-start.15 = (f32[40,128]{1,0:T(8,128)S(1)}, f32[40,128]{1,0:T(8,128)S(1)}, u32[]{:S(2)}, u32[]{:S(2)}) collective-permute-start(f32[40,128]{1,0:T(8,128)S(1)} %get-tuple-element.54), channel_id=1, source_target_pairs={{0,2},{1,3},{2,4},{3,5},{4,6},{5,7},{6,0},{7,1},{8,10},{9,11},{10,... | collective-permute-start | bytes 61448 | tf_op jit(solution)/shard_map/ppermute | solution.py:58
  59.2 1.2 %collective-permute-start.16 = (f32[40,128]{1,0:T(8,128)S(1)}, f32[40,128]{1,0:T(8,128)S(1)}, u32[]{:S(2)}, u32[]{:S(2)}) collective-permute-start(f32[40,128]{1,0:T(8,128)S(1)} %get-tuple-element.54), channel_id=1, source_target_pairs={{0,4},{1,5},{2,6},{3,7},{4,0},{5,1},{6,2},{7,3},{8,12},{9,13},{10,... | collective-permute-start | bytes 61448 | tf_op jit(solution)/shard_map/ppermute | solution.py:58
  60.3 1.2 %collective-permute-start.17 = (f32[40,128]{1,0:T(8,128)S(1)}, f32[40,128]{1,0:T(8,128)S(1)}, u32[]{:S(2)}, u32[]{:S(2)}) collective-permute-start(f32[40,128]{1,0:T(8,128)S(1)} %get-tuple-element.54), channel_id=1, source_target_pairs={{0,6},{1,7},{2,0},{3,1},{4,2},{5,3},{6,4},{7,5},{8,14},{9,15},{10,... | collective-permute-start | bytes 61448 | tf_op jit(solution)/shard_map/ppermute | solution.py:58
  61.5 0.0 collective-permute-done.15
  61.5 2.3 %collective-permute-done.16 = f32[40,128]{1,0:T(8,128)S(1)} collective-permute-done((f32[40,128]{1,0:T(8,128)S(1)}, f32[40,128]{1,0:T(8,128)S(1)}, u32[]{:S(2)}, u32[]{:S(2)}) %collective-permute-start.16) | collective-permute-done | bytes 20512 | tf_op jit(solution)/shard_map/ppermute | solution.py:58
  63.9 0.3 collective-permute-done.17
  64.1 0.9 %collective-permute-start.18 = (f32[40,128]{1,0:T(8,128)S(1)}, f32[40,128]{1,0:T(8,128)S(1)}, u32[]{:S(2)}, u32[]{:S(2)}) collective-permute-start(f32[40,128]{1,0:T(8,128)S(1)} %add_add_fusion.refs_0_), channel_id=1, source_target_pairs={{0,1},{1,0},{2,3},{3,2},{4,5},{5,4},{6,7},{7,6},{8,9},{9,8},{10,11... | collective-permute-start | bytes 61448 | tf_op jit(solution)/shard_map/ppermute | solution.py:63
  65.0 0.0 copy-done.3
  65.0 2.9 %collective-permute-done.18.refs_1_ = f32[40,128]{1,0:T(8,128)S(1)} collective-permute-done((f32[40,128]{1,0:T(8,128)S(1)}, f32[40,128]{1,0:T(8,128)S(1)}, u32[]{:S(2)}, u32[]{:S(2)}) %collective-permute-start.18) | collective-permute-done | bytes 20512 | tf_op jit(solution)/shard_map/ppermute | solution.py:63
  68.0 2.3 %norm.1 = bf16[5120,384]{1,0:T(8,128)(2,1)} custom-call(bf16[5120,384]{1,0:T(8,128)(2,1)S(1)} %get-tuple-element.53.gated_ref, f32[1,384]{1,0:T(1,128)S(1)} %broadcast_in_dim.7.gain_ref, f32[40,128]{1,0:T(8,128)S(1)} %add_add_fusion.refs_0_, f32[40,128]{1,0:T(8,128)S(1)} %collective-permute-done.18.refs_1_), custom_call_target="tpu_custom_call" | custom-call | flops 1000 | bytes 1000 | tf_op jit(solution)/shard_map/norm/pallas_call | solution.py:586
  (9 shorter events, 0.1 us)
Async XLA Ops:
  0.0 3.5 %copy-start.4 = (bf16[4,16]{1,0:T(4,128)(2,1)S(1)}, bf16[4,16]{1,0:T(4,128)(2,1)}, u32[]{:S(2)}) copy-start(bf16[4,16]{1,0:T(4,128)(2,1)} %param.16) | copy-start | bytes 388
  0.0 3.6 %copy-start.5 = (bf16[4,16]{1,0:T(4,128)(2,1)S(1)}, bf16[4,16]{1,0:T(4,128)(2,1)}, u32[]{:S(2)}) copy-start(bf16[4,16]{1,0:T(4,128)(2,1)} %param.17) | copy-start | bytes 388
  0.0 13.4 %copy-start.6 = (f32[6]{0:T(128)S(1)}, f32[6]{0:T(128)}, u32[]{:S(2)}) copy-start(f32[6]{0:T(128)} %param.18) | copy-start | bytes 76
  0.0 13.5 %copy-start.1 = (f32[5120,6]{0,1:T(8,128)S(1)}, f32[5120,6]{0,1:T(8,128)}, u32[]{:S(2)}) copy-start(f32[5120,6]{0,1:T(8,128)} %param.14) | copy-start | bytes 368644
  0.0 14.8 %copy-start.2 = (bf16[4,384]{1,0:T(4,128)(2,1)S(1)}, bf16[4,384]{1,0:T(4,128)(2,1)}, u32[]{:S(2)}) copy-start(bf16[4,384]{1,0:T(4,128)(2,1)} %param.15) | copy-start | bytes 9220
  1.1 3.2 %collective-permute-start = (bf16[48,384]{1,0:T(8,128)(2,1)S(1)}, bf16[48,384]{1,0:T(8,128)(2,1)S(1)}, u32[]{:S(2)}, u32[]{:S(2)}) collective-permute-start(bf16[48,384]{1,0:T(8,128)(2,1)S(1)} %get-tuple-element.32), channel_id=1, source_target_pairs={{0,8},{8,16},{16,24},{1,9},{9,17},{17,25},{2,10},{10,18},{18,26},{... | collective-permute-start | bytes 110600 | tf_op jit(solution)/shard_map/ppermute | solution.py:607
  5.0 16.7 %collective-permute-start.1 = (bf16[16,5120]{1,0:T(8,128)(2,1)S(1)}, bf16[16,5120]{1,0:T(8,128)(2,1)S(1)}, u32[]{:S(2)}, u32[]{:S(2)}) collective-permute-start(bf16[16,5120]{1,0:T(8,128)(2,1)S(1)} %get-tuple-element.35.refs_0_.refs_2_), channel_id=1, source_target_pairs={{0,2},{1,3},{2,4},{3,5},{4,6},{5,7},{6,0},{7,1},{8,10},{9,11},{10,... | collective-permute-start | bytes 491528 | tf_op jit(solution)/shard_map/ppermute | solution.py:58
  7.4 14.2 %collective-permute-start.2 = (bf16[16,5120]{1,0:T(8,128)(2,1)S(1)}, bf16[16,5120]{1,0:T(8,128)(2,1)S(1)}, u32[]{:S(2)}, u32[]{:S(2)}) collective-permute-start(bf16[16,5120]{1,0:T(8,128)(2,1)S(1)} %get-tuple-element.35.refs_0_.refs_2_), channel_id=1, source_target_pairs={{0,4},{1,5},{2,6},{3,7},{4,0},{5,1},{6,2},{7,3},{8,12},{9,13},{10,... | collective-permute-start | bytes 491528 | tf_op jit(solution)/shard_map/ppermute | solution.py:58
  10.0 11.7 %collective-permute-start.3 = (bf16[16,5120]{1,0:T(8,128)(2,1)S(1)}, bf16[16,5120]{1,0:T(8,128)(2,1)S(1)}, u32[]{:S(2)}, u32[]{:S(2)}) collective-permute-start(bf16[16,5120]{1,0:T(8,128)(2,1)S(1)} %get-tuple-element.35.refs_0_.refs_2_), channel_id=1, source_target_pairs={{0,6},{1,7},{2,0},{3,1},{4,2},{5,3},{6,4},{7,5},{8,14},{9,15},{10,... | collective-permute-start | bytes 491528 | tf_op jit(solution)/shard_map/ppermute | solution.py:58
  11.4 10.3 %collective-permute-start.4 = (bf16[16,5120]{1,0:T(8,128)(2,1)S(1)}, bf16[16,5120]{1,0:T(8,128)(2,1)S(1)}, u32[]{:S(2)}, u32[]{:S(2)}) collective-permute-start(bf16[16,5120]{1,0:T(8,128)(2,1)S(1)} %get-tuple-element.35.refs_0_.refs_2_), channel_id=1, source_target_pairs={{0,1},{1,0},{2,3},{3,2},{4,5},{5,4},{6,7},{7,6},{8,9},{9,8},{10,11... | collective-permute-start | bytes 491528 | tf_op jit(solution)/shard_map/ppermute | solution.py:63
  12.9 8.9 %collective-permute-start.5 = (bf16[16,5120]{1,0:T(8,128)(2,1)S(1)}, bf16[16,5120]{1,0:T(8,128)(2,1)S(1)}, u32[]{:S(2)}, u32[]{:S(2)}) collective-permute-start(bf16[16,5120]{1,0:T(8,128)(2,1)S(1)} %get-tuple-element.37.refs_8_), channel_id=1, source_target_pairs={{0,1},{1,0},{2,3},{3,2},{4,5},{5,4},{6,7},{7,6},{8,9},{9,8},{10,11... | collective-permute-start | bytes 491528 | tf_op jit(solution)/shard_map/ppermute | solution.py:63
  21.6 8.1 %copy-start = (bf16[5120,384]{1,0:T(8,128)(2,1)S(1)}, bf16[5120,384]{1,0:T(8,128)(2,1)}, u32[]{:S(2)}) copy-start(bf16[5120,384]{1,0:T(8,128)(2,1)} %z_ref.1) | copy-start | bytes 11796484
  21.8 14.0 %collective-permute-start.7 = (bf16[48,5120]{1,0:T(8,128)(2,1)S(1)}, bf16[48,5120]{1,0:T(8,128)(2,1)S(1)}, u32[]{:S(2)}, u32[]{:S(2)}) collective-permute-start(bf16[48,5120]{1,0:T(8,128)(2,1)S(1)} %pack.2.refs_2_), channel_id=1, source_target_pairs={{0,1},{1,0},{2,3},{3,2},{4,5},{5,4},{6,7},{7,6},{8,9},{9,8},{10,11... | collective-permute-start | bytes 1474568 | tf_op jit(solution)/shard_map/ppermute | solution.py:63
  23.4 9.5 %collective-permute-start.6 = (bf16[16,5120]{1,0:T(8,128)(2,1)S(1)}, bf16[16,5120]{1,0:T(8,128)(2,1)S(1)}, u32[]{:S(2)}, u32[]{:S(2)}) collective-permute-start(bf16[16,5120]{1,0:T(8,128)(2,1)S(1)} %get-tuple-element.45), channel_id=1, source_target_pairs={{0,2},{1,3},{2,4},{3,5},{4,6},{5,7},{6,0},{7,1},{8,10},{9,11},{10,... | collective-permute-start | bytes 491528 | tf_op jit(solution)/shard_map/ppermute | solution.py:58
  27.4 12.3 %collective-permute-start.10 = (bf16[16,5120]{1,0:T(8,128)(2,1)S(1)}, bf16[16,5120]{1,0:T(8,128)(2,1)S(1)}, u32[]{:S(2)}, u32[]{:S(2)}) collective-permute-start(bf16[16,5120]{1,0:T(8,128)(2,1)S(1)} %get-tuple-element.45), channel_id=1, source_target_pairs={{0,4},{1,5},{2,6},{3,7},{4,0},{5,1},{6,2},{7,3},{8,12},{9,13},{10,... | collective-permute-start | bytes 491528 | tf_op jit(solution)/shard_map/ppermute | solution.py:58
  28.2 11.5 %collective-permute-start.9 = (bf16[16,5120]{1,0:T(8,128)(2,1)S(1)}, bf16[16,5120]{1,0:T(8,128)(2,1)S(1)}, u32[]{:S(2)}, u32[]{:S(2)}) collective-permute-start(bf16[16,5120]{1,0:T(8,128)(2,1)S(1)} %get-tuple-element.45), channel_id=1, source_target_pairs={{0,6},{1,7},{2,0},{3,1},{4,2},{5,3},{6,4},{7,5},{8,14},{9,15},{10,... | collective-permute-start | bytes 491528 | tf_op jit(solution)/shard_map/ppermute | solution.py:58
  32.9 6.7 %collective-permute-start.11 = (bf16[16,5120]{1,0:T(8,128)(2,1)S(1)}, bf16[16,5120]{1,0:T(8,128)(2,1)S(1)}, u32[]{:S(2)}, u32[]{:S(2)}) collective-permute-start(bf16[16,5120]{1,0:T(8,128)(2,1)S(1)} %tie.4.refs_1_.refs_10_), channel_id=1, source_target_pairs={{0,1},{1,0},{2,3},{3,2},{4,5},{5,4},{6,7},{7,6},{8,9},{9,8},{10,11... | collective-permute-start | bytes 491528 | tf_op jit(solution)/shard_map/ppermute | solution.py:63
  37.8 4.0 %collective-permute-start.8 = (bf16[144,384]{1,0:T(8,128)(2,1)S(1)}, bf16[144,384]{1,0:T(8,128)(2,1)S(1)}, u32[]{:S(2)}, u32[]{:S(2)}) collective-permute-start(bf16[144,384]{1,0:T(8,128)(2,1)S(1)} %get-tuple-element.48.refs_2_.mine_ref), channel_id=1, source_target_pairs={{0,8},{8,0},{16,24},{24,16},{1,9},{9,1},{17,25},{25,17},{2,10},{10... | collective-permute-start | bytes 331784 | tf_op jit(solution)/shard_map/ppermute | solution.py:650
  39.7 7.8 %collective-permute-start.14 = (bf16[32,3072]{1,0:T(8,128)(2,1)S(1)}, bf16[32,3072]{1,0:T(8,128)(2,1)S(1)}, u32[]{:S(2)}, u32[]{:S(2)}) collective-permute-start(bf16[32,3072]{1,0:T(8,128)(2,1)S(1)} %get-tuple-element.49.token_ref), channel_id=1, source_target_pairs={{0,1},{1,0},{2,3},{3,2},{4,5},{5,4},{6,7},{7,6},{8,9},{9,8},{10,11... | collective-permute-start | bytes 589832 | tf_op jit(solution)/shard_map/ppermute | solution.py:63
  40.6 12.2 %collective-permute-start.13 = (bf16[32,2048]{1,0:T(8,128)(2,1)S(1)}, bf16[32,2048]{1,0:T(8,128)(2,1)S(1)}, u32[]{:S(2)}, u32[]{:S(2)}) collective-permute-start(bf16[32,2048]{1,0:T(8,128)(2,1)S(1)} %get-tuple-element.50), channel_id=1, source_target_pairs={{0,1},{1,0},{2,3},{3,2},{4,5},{5,4},{6,7},{7,6},{8,9},{9,8},{10,11... | collective-permute-start | bytes 393224 | tf_op jit(solution)/shard_map/ppermute | solution.py:63
  41.8 6.4 %collective-permute-start.12 = (bf16[144,384]{1,0:T(8,128)(2,1)S(1)}, bf16[144,384]{1,0:T(8,128)(2,1)S(1)}, u32[]{:S(2)}, u32[]{:S(2)}) collective-permute-start(bf16[144,384]{1,0:T(8,128)(2,1)S(1)} %join.1), channel_id=1, source_target_pairs={{0,16},{8,24},{1,17},{9,25},{2,18},{10,26},{3,19},{11,27},{4,20},{... | collective-permute-start | bytes 331784 | tf_op jit(solution)/shard_map/ppermute | solution.py:650
  52.8 12.2 %copy-start.3 = (f32[384]{0:T(512)S(1)}, f32[384]{0:T(512)}, u32[]{:S(2)}) copy-start(f32[384]{0:T(512)} %param.19) | copy-start | bytes 4612
  55.9 5.6 %collective-permute-start.15 = (f32[40,128]{1,0:T(8,128)S(1)}, f32[40,128]{1,0:T(8,128)S(1)}, u32[]{:S(2)}, u32[]{:S(2)}) collective-permute-start(f32[40,128]{1,0:T(8,128)S(1)} %get-tuple-element.54), channel_id=1, source_target_pairs={{0,2},{1,3},{2,4},{3,5},{4,6},{5,7},{6,0},{7,1},{8,10},{9,11},{10,... | collective-permute-start | bytes 61448 | tf_op jit(solution)/shard_map/ppermute | solution.py:58
  59.2 4.7 %collective-permute-start.16 = (f32[40,128]{1,0:T(8,128)S(1)}, f32[40,128]{1,0:T(8,128)S(1)}, u32[]{:S(2)}, u32[]{:S(2)}) collective-permute-start(f32[40,128]{1,0:T(8,128)S(1)} %get-tuple-element.54), channel_id=1, source_target_pairs={{0,4},{1,5},{2,6},{3,7},{4,0},{5,1},{6,2},{7,3},{8,12},{9,13},{10,... | collective-permute-start | bytes 61448 | tf_op jit(solution)/shard_map/ppermute | solution.py:58
  60.3 3.8 %collective-permute-start.17 = (f32[40,128]{1,0:T(8,128)S(1)}, f32[40,128]{1,0:T(8,128)S(1)}, u32[]{:S(2)}, u32[]{:S(2)}) collective-permute-start(f32[40,128]{1,0:T(8,128)S(1)} %get-tuple-element.54), channel_id=1, source_target_pairs={{0,6},{1,7},{2,0},{3,1},{4,2},{5,3},{6,4},{7,5},{8,14},{9,15},{10,... | collective-permute-start | bytes 61448 | tf_op jit(solution)/shard_map/ppermute | solution.py:58
  64.1 3.8 %collective-permute-start.18 = (f32[40,128]{1,0:T(8,128)S(1)}, f32[40,128]{1,0:T(8,128)S(1)}, u32[]{:S(2)}, u32[]{:S(2)}) collective-permute-start(f32[40,128]{1,0:T(8,128)S(1)} %add_add_fusion.refs_0_), channel_id=1, source_target_pairs={{0,1},{1,0},{2,3},{3,2},{4,5},{5,4},{6,7},{7,6},{8,9},{9,8},{10,11... | collective-permute-start | bytes 61448 | tf_op jit(solution)/shard_map/ppermute | solution.py:63

commit v6 on v5

--- a/solution.py
+++ b/solution.py
@@ -442,7 +442,7 @@
 ):
     others, refs = refs[:count], refs[count:]
     b_refs, c_refs = [refs[i] for i in b_picks], [refs[i] for i in c_picks]
-    gated_ref, square_ref, carry, c_rows, scores, carried, squares = refs[-7:]
+    gated_ref, square_ref, carry, c_rows, scores, carried = refs[-6:]
     length, width = gate_ref.shape
     heads = factor_ref.shape[0] // (length // ROWS)
     groups, subs, pairs = SUB // ROWS, TILE // SUB, width // SUB
@@ -491,6 +491,7 @@
             scores[local[s]] = jnp.where(causal, both[:, :SUB], 0.0)
             carried[local[s]] = both[:, SUB:]
 
+        sums = []
         turn(0)
         turn(1)
         products(0)
@@ -519,11 +520,9 @@
                 gated_ref[at, cols] = gated.astype(BF16)
                 square = gated * gated
                 total = square if total is None else total + square
-            squares[local[s]] = total.astype(BF16)
-        sums = lax.dot_general(
-            jnp.ones((8, SUB), BF16), squares[...], (((1,), (1,)), ((), ())), preferred_element_type=F32
-        )
-        square_ref[pl.ds(row, subs)] = jnp.concatenate([sums[:1, at] for at in local], axis=0)
+            column = jnp.sum(total, axis=1, keepdims=True)
+            sums.append(jnp.sum(jnp.where(i == j, column, 0.0), axis=0, keepdims=True))
+        square_ref[pl.ds(row, subs)] = jnp.concatenate(sums, axis=0)
         return 0
 
     lax.fori_loop(*span, tile, 0)
@@ -551,7 +550,6 @@
             pltpu.VMEM((TILE, size), BF16),
             pltpu.VMEM((TILE, SUB), F32),
             pltpu.VMEM((TILE, width), F32),
-            pltpu.VMEM((TILE, SUB), BF16),
         ],
         input_output_aliases={first + i: i for i in range(len(filled))},
         compiler_params=params(),

time: 70.6 us -> 70.6 us (level)
  no operation moved by 1% of the time
where the time goes in v6:
time: 70.6 us; the launch traced here: 70.3 us
  starting transfers between devices  32 us (45%)
  Pallas kernels  25 us (35%)
  waiting for transfers between devices  12.8 us (18%)
    ppermute x9, starting transfers between devices, along_outer(): lax.ppermute(piece, 'head', outer_pairs(d))  18.5 us
    pallas_call x2, Pallas kernels, scan(): pl.pallas_call(functools.partial(scan_kernel, span, len(others), b_rows,...  7.68 us
    ppermute x7, waiting for transfers between devices, along_inner(): lax.ppermute(p, 'head', inner_pairs(e))  7.12 us
    ppermute x7, starting transfers between devices, along_inner(): lax.ppermute(p, 'head', inner_pairs(e))  7.02 us
    pallas_call x1, Pallas kernels, head_conv(): pl.pallas_call(functools.partial(head_conv_kernel, first, heads), grid=(c...  6.84 us
    ppermute x9, waiting for transfers between devices, along_outer(): lax.ppermute(piece, 'head', outer_pairs(d))  4.27 us
    ppermute x2, starting transfers between devices, body(): others.append(lax.ppermute(mine, 'seq', pairs))  4.16 us
    pallas_call x1, Pallas kernels, gates(): pl.pallas_call(gates_kernel, grid=(length // TILE,), in_specs=[wide, pl.B...  3.16 us
  transfers between devices with their start and end apart: 19, of which 9 were waited for; matrix products, arithmetic and copies ran while one was open for 0% of the time, Pallas kernels for 25%

profile of v6, /device:TPU:0, one launch (start us, length us, event | category | flops | bytes accessed | tf_op | source)
XLA Modules:
  0.0 70.3 jit_solution(16690059798517409674)
XLA Ops:
  0.0 0.0 copy-start.4
  0.0 0.0 copy-start.5
  0.0 0.0 copy-start.1
  0.0 0.0 copy-start.2
  0.0 1.1 %tails.1 = (bf16[48,384]{1,0:T(8,128)(2,1)S(1)}, bf16[16,5120]{1,0:T(8,128)(2,1)S(1)}, bf16[16,5120]{1,0:T(8,128)(2,1)S(1)}) custom-call(bf16[5120,384]{1,0:T(8,128)(2,1)} %before_ref.1, bf16[16,5120]{1,0:T(8,128)(2,1)} %bitcast.9, bf16[16,5120]{1,0:T(8,128)(2,1)} %bitcast.10), custom_call_target="tpu_custom_call" | custom-call | flops 1000 | bytes 1000 | tf_op jit(solution)/shard_map/tails/pallas_call | solution.py:124
  1.1 2.4 %collective-permute-start = (bf16[48,384]{1,0:T(8,128)(2,1)S(1)}, bf16[48,384]{1,0:T(8,128)(2,1)S(1)}, u32[]{:S(2)}, u32[]{:S(2)}) collective-permute-start(bf16[48,384]{1,0:T(8,128)(2,1)S(1)} %get-tuple-element.32), channel_id=1, source_target_pairs={{0,8},{8,16},{16,24},{1,9},{9,17},{17,25},{2,10},{10,18},{18,26},{... | collective-permute-start | bytes 110600 | tf_op jit(solution)/shard_map/ppermute | solution.py:605
  3.5 0.0 copy-done.4
  3.5 0.1 copy.20
  3.6 0.0 copy-done.5
  3.6 0.1 copy.21
  3.7 0.7 collective-permute-done.halo_ref
  4.4 0.6 shared_conv.1
  5.0 2.5 %collective-permute-start.1 = (bf16[16,5120]{1,0:T(8,128)(2,1)S(1)}, bf16[16,5120]{1,0:T(8,128)(2,1)S(1)}, u32[]{:S(2)}, u32[]{:S(2)}) collective-permute-start(bf16[16,5120]{1,0:T(8,128)(2,1)S(1)} %get-tuple-element.35.refs_0_.refs_2_), channel_id=1, source_target_pairs={{0,2},{1,3},{2,4},{3,5},{4,6},{5,7},{6,0},{7,1},{8,10},{9,11},{10,... | collective-permute-start | bytes 491528 | tf_op jit(solution)/shard_map/ppermute | solution.py:58
  7.4 2.6 %collective-permute-start.2 = (bf16[16,5120]{1,0:T(8,128)(2,1)S(1)}, bf16[16,5120]{1,0:T(8,128)(2,1)S(1)}, u32[]{:S(2)}, u32[]{:S(2)}) collective-permute-start(bf16[16,5120]{1,0:T(8,128)(2,1)S(1)} %get-tuple-element.35.refs_0_.refs_2_), channel_id=1, source_target_pairs={{0,4},{1,5},{2,6},{3,7},{4,0},{5,1},{6,2},{7,3},{8,12},{9,13},{10,... | collective-permute-start | bytes 491528 | tf_op jit(solution)/shard_map/ppermute | solution.py:58
  10.0 1.3 %collective-permute-start.3 = (bf16[16,5120]{1,0:T(8,128)(2,1)S(1)}, bf16[16,5120]{1,0:T(8,128)(2,1)S(1)}, u32[]{:S(2)}, u32[]{:S(2)}) collective-permute-start(bf16[16,5120]{1,0:T(8,128)(2,1)S(1)} %get-tuple-element.35.refs_0_.refs_2_), channel_id=1, source_target_pairs={{0,6},{1,7},{2,0},{3,1},{4,2},{5,3},{6,4},{7,5},{8,14},{9,15},{10,... | collective-permute-start | bytes 491528 | tf_op jit(solution)/shard_map/ppermute | solution.py:58
  11.4 1.5 %collective-permute-start.4 = (bf16[16,5120]{1,0:T(8,128)(2,1)S(1)}, bf16[16,5120]{1,0:T(8,128)(2,1)S(1)}, u32[]{:S(2)}, u32[]{:S(2)}) collective-permute-start(bf16[16,5120]{1,0:T(8,128)(2,1)S(1)} %get-tuple-element.35.refs_0_.refs_2_), channel_id=1, source_target_pairs={{0,1},{1,0},{2,3},{3,2},{4,5},{5,4},{6,7},{7,6},{8,9},{9,8},{10,11... | collective-permute-start | bytes 491528 | tf_op jit(solution)/shard_map/ppermute | solution.py:63
  12.9 0.5 collective-permute-start.5
  13.4 0.0 copy-done.6
  13.4 0.1 copy.22.rate_ref
  13.5 0.0 copy-done.1
  13.5 1.3 %rows.1 = (f32[8,5120]{1,0:T(8,128)S(1)}, bf16[5120,40]{1,0:T(8,128)(2,1)S(1)}, f32[40,384]{1,0:T(8,128)S(1)}) custom-call(f32[6,5120]{1,0:T(8,128)S(1)} %bitcast.6, f32[6,1]{1,0:T(8,128)S(1)} %copy.22.rate_ref), custom_call_target="tpu_custom_call" | custom-call | flops 1000 | bytes 1000 | tf_op jit(solution)/shard_map/rows/pallas_call | solution.py:219
  14.8 0.0 copy-done.2
  14.8 6.8 %head_conv.1 = (bf16[5120,384]{1,0:T(8,128)(2,1)S(1)}, bf16[5120,384]{1,0:T(8,128)(2,1)S(1)}) custom-call(bf16[5120,384]{1,0:T(8,128)(2,1)} %before_ref.1, bf16[5120,384]{1,0:T(8,128)(2,1)} %before_ref.1, bf16[48,384]{1,0:T(8,128)(2,1)S(1)} %collective-permute-done.halo_ref, f32[4,384]{1,0:T(4,128)S(1)} %convert_element_type.17.taps_ref, ...), custom_call_target="tpu_custom_call" | custom-call | flops 1000 | bytes 1000 | tf_op jit(solution)/shard_map/head_conv/pallas_call | solution.py:275
  21.6 0.0 copy-start
  21.7 0.0 collective-permute-done.1.refs_0_.refs_2_.refs_4_
  21.7 0.0 collective-permute-done.2.refs_1_.refs_3_.refs_5_
  21.7 0.0 collective-permute-done.3.refs_2_.refs_4_.refs_6_
  21.7 0.0 collective-permute-done.4.refs_4_.refs_1_.refs_3_
  21.7 0.1 collective-permute-done.5.refs_5_.refs_9_
  21.8 1.6 %collective-permute-start.7 = (bf16[48,5120]{1,0:T(8,128)(2,1)S(1)}, bf16[48,5120]{1,0:T(8,128)(2,1)S(1)}, u32[]{:S(2)}, u32[]{:S(2)}) collective-permute-start(bf16[48,5120]{1,0:T(8,128)(2,1)S(1)} %pack.2.refs_2_), channel_id=1, source_target_pairs={{0,1},{1,0},{2,3},{3,2},{4,5},{5,4},{6,7},{7,6},{8,9},{9,8},{10,11... | collective-permute-start | bytes 1474568 | tf_op jit(solution)/shard_map/ppermute | solution.py:63
  23.4 4.0 %collective-permute-start.6 = (bf16[16,5120]{1,0:T(8,128)(2,1)S(1)}, bf16[16,5120]{1,0:T(8,128)(2,1)S(1)}, u32[]{:S(2)}, u32[]{:S(2)}) collective-permute-start(bf16[16,5120]{1,0:T(8,128)(2,1)S(1)} %get-tuple-element.45), channel_id=1, source_target_pairs={{0,2},{1,3},{2,4},{3,5},{4,6},{5,7},{6,0},{7,1},{8,10},{9,11},{10,... | collective-permute-start | bytes 491528 | tf_op jit(solution)/shard_map/ppermute | solution.py:58
  27.4 0.8 %collective-permute-start.10 = (bf16[16,5120]{1,0:T(8,128)(2,1)S(1)}, bf16[16,5120]{1,0:T(8,128)(2,1)S(1)}, u32[]{:S(2)}, u32[]{:S(2)}) collective-permute-start(bf16[16,5120]{1,0:T(8,128)(2,1)S(1)} %get-tuple-element.45), channel_id=1, source_target_pairs={{0,4},{1,5},{2,6},{3,7},{4,0},{5,1},{6,2},{7,3},{8,12},{9,13},{10,... | collective-permute-start | bytes 491528 | tf_op jit(solution)/shard_map/ppermute | solution.py:58
  28.2 1.6 %collective-permute-start.9 = (bf16[16,5120]{1,0:T(8,128)(2,1)S(1)}, bf16[16,5120]{1,0:T(8,128)(2,1)S(1)}, u32[]{:S(2)}, u32[]{:S(2)}) collective-permute-start(bf16[16,5120]{1,0:T(8,128)(2,1)S(1)} %get-tuple-element.45), channel_id=1, source_target_pairs={{0,6},{1,7},{2,0},{3,1},{4,2},{5,3},{6,4},{7,5},{8,14},{9,15},{10,... | collective-permute-start | bytes 491528 | tf_op jit(solution)/shard_map/ppermute | solution.py:58
  29.8 0.0 copy-done
  29.8 3.2 %gates.1 = (f32[5120,384]{1,0:T(8,128)S(1)}, f32[1920,128]{1,0:T(8,128)S(1)}, f32[3,320,128]{2,1,0:T(8,128)S(1)}) custom-call(bf16[5120,384]{1,0:T(8,128)(2,1)S(1)} %copy-done, bf16[5120,40]{1,0:T(8,128)(2,1)S(1)} %get-tuple-element.38.column_ref, f32[8,5120]{1,0:T(8,128)S(1)} %get-tuple-element.39.q_ref), custom_call_target="tpu_custom_call" | custom-call | flops 1000 | bytes 1000 | tf_op jit(solution)/shard_map/gates/pallas_call | solution.py:334
  32.9 0.0 collective-permute-done.6.refs_0_
  32.9 0.4 collective-permute-start.11
  33.3 2.5 %collective-permute-done.7.refs_5_.refs_7_ = bf16[48,5120]{1,0:T(8,128)(2,1)S(1)} collective-permute-done((bf16[48,5120]{1,0:T(8,128)(2,1)S(1)}, bf16[48,5120]{1,0:T(8,128)(2,1)S(1)}, u32[]{:S(2)}, u32[]{:S(2)}) %collective-permute-start.7) | collective-permute-done | bytes 491552 | tf_op jit(solution)/shard_map/ppermute | solution.py:63
  35.9 1.9 %last_state.1 = (bf16[144,384]{1,0:T(8,128)(2,1)S(1)}, f32[5120,384]{1,0:T(8,128)S(1)}, f32[40,384]{1,0:T(8,128)S(1)}) custom-call(bf16[5120,384]{1,0:T(8,128)(2,1)S(1)} %get-tuple-element.43.wt_ref, f32[40,384]{1,0:T(8,128)S(1)} %tie.5.decay_ref, bf16[16,5120]{1,0:T(8,128)(2,1)S(1)} %get-tuple-element.35.refs_0_.refs_2_, ...), custom_call_target="tpu_custom_call" | custom-call | flops 1000 | bytes 1000 | tf_op jit(solution)/shard_map/last_state/pallas_call | solution.py:401
  37.8 0.1 collective-permute-start.8
  37.9 1.8 %collective-permute-done.10.refs_1_.refs_11_ = bf16[16,5120]{1,0:T(8,128)(2,1)S(1)} collective-permute-done((bf16[16,5120]{1,0:T(8,128)(2,1)S(1)}, bf16[16,5120]{1,0:T(8,128)(2,1)S(1)}, u32[]{:S(2)}, u32[]{:S(2)}) %collective-permute-start.10) | collective-permute-done | bytes 163872 | tf_op jit(solution)/shard_map/ppermute | solution.py:58
  39.6 0.0 collective-permute-done.9.refs_0_.refs_12_
  39.6 0.0 collective-permute-done.11.refs_3_.refs_13_
  39.7 1.0 %collective-permute-start.14 = (bf16[32,3072]{1,0:T(8,128)(2,1)S(1)}, bf16[32,3072]{1,0:T(8,128)(2,1)S(1)}, u32[]{:S(2)}, u32[]{:S(2)}) collective-permute-start(bf16[32,3072]{1,0:T(8,128)(2,1)S(1)} %get-tuple-element.49.token_ref), channel_id=1, source_target_pairs={{0,1},{1,0},{2,3},{3,2},{4,5},{5,4},{6,7},{7,6},{8,9},{9,8},{10,11... | collective-permute-start | bytes 589832 | tf_op jit(solution)/shard_map/ppermute | solution.py:63
  40.6 1.1 %collective-permute-start.13 = (bf16[32,2048]{1,0:T(8,128)(2,1)S(1)}, bf16[32,2048]{1,0:T(8,128)(2,1)S(1)}, u32[]{:S(2)}, u32[]{:S(2)}) collective-permute-start(bf16[32,2048]{1,0:T(8,128)(2,1)S(1)} %get-tuple-element.50), channel_id=1, source_target_pairs={{0,1},{1,0},{2,3},{3,2},{4,5},{5,4},{6,7},{7,6},{8,9},{9,8},{10,11... | collective-permute-start | bytes 393224 | tf_op jit(solution)/shard_map/ppermute | solution.py:63
  41.8 0.0 collective-permute-done.8.other_ref.refs_0_
  41.8 0.1 join.1
  41.8 4.1 %collective-permute-start.12 = (bf16[144,384]{1,0:T(8,128)(2,1)S(1)}, bf16[144,384]{1,0:T(8,128)(2,1)S(1)}, u32[]{:S(2)}, u32[]{:S(2)}) collective-permute-start(bf16[144,384]{1,0:T(8,128)(2,1)S(1)} %join.1), channel_id=1, source_target_pairs={{0,16},{8,24},{1,17},{9,25},{2,18},{10,26},{3,19},{11,27},{4,20},{... | collective-permute-start | bytes 331784 | tf_op jit(solution)/shard_map/ppermute | solution.py:648
  45.9 1.6 %collective-permute-done.14.refs_14_ = bf16[32,3072]{1,0:T(8,128)(2,1)S(1)} collective-permute-done((bf16[32,3072]{1,0:T(8,128)(2,1)S(1)}, bf16[32,3072]{1,0:T(8,128)(2,1)S(1)}, u32[]{:S(2)}, u32[]{:S(2)}) %collective-permute-start.14) | collective-permute-done | bytes 196640 | tf_op jit(solution)/shard_map/ppermute | solution.py:63
  47.5 0.7 %collective-permute-done.12.refs_1_ = bf16[144,384]{1,0:T(8,128)(2,1)S(1)} collective-permute-done((bf16[144,384]{1,0:T(8,128)(2,1)S(1)}, bf16[144,384]{1,0:T(8,128)(2,1)S(1)}, u32[]{:S(2)}, u32[]{:S(2)}) %collective-permute-start.12) | collective-permute-done | bytes 110624 | tf_op jit(solution)/shard_map/ppermute | solution.py:648
  48.2 4.6 %scan.2 = (bf16[5120,384]{1,0:T(8,128)(2,1)S(1)}, f32[40,128]{1,0:T(8,128)S(1)}) custom-call(f32[5120,384]{1,0:T(8,128)S(1)} %get-tuple-element.40.gate_ref, f32[1920,128]{1,0:T(8,128)S(1)} %get-tuple-element.41.factor_ref, f32[3,320,128]{2,1,0:T(8,128)S(1)} %get-tuple-element.42.refs_1_.start_ref, bf16[5120,384]{1,0:T(8,128)(2,1)S(1)} %get-tuple-element.36.refs_3_.xs_ref, ...), custom_call_target="tpu_custom_call" | custom-call | flops 1000 | bytes 1000 | tf_op jit(solution)/shard_map/scan/pallas_call | solution.py:541
  52.8 0.0 collective-permute-done.13.refs_14_
  52.9 0.0 copy-start.3
  52.9 3.1 %scan.3 = (bf16[5120,384]{1,0:T(8,128)(2,1)S(1)}, f32[40,128]{1,0:T(8,128)S(1)}) custom-call(f32[5120,384]{1,0:T(8,128)S(1)} %get-tuple-element.40.gate_ref, f32[1920,128]{1,0:T(8,128)S(1)} %get-tuple-element.41.factor_ref, f32[3,320,128]{2,1,0:T(8,128)S(1)} %get-tuple-element.42.refs_1_.start_ref, ...), custom_call_target="tpu_custom_call", output_to_operand_aliasing={{0}: (21, {}), {1}: (22, {})} | custom-call | flops 1000 | bytes 1000 | tf_op jit(solution)/shard_map/scan/pallas_call | solution.py:541
  56.0 3.3 %collective-permute-start.15 = (f32[40,128]{1,0:T(8,128)S(1)}, f32[40,128]{1,0:T(8,128)S(1)}, u32[]{:S(2)}, u32[]{:S(2)}) collective-permute-start(f32[40,128]{1,0:T(8,128)S(1)} %get-tuple-element.54), channel_id=1, source_target_pairs={{0,2},{1,3},{2,4},{3,5},{4,6},{5,7},{6,0},{7,1},{8,10},{9,11},{10,... | collective-permute-start | bytes 61448 | tf_op jit(solution)/shard_map/ppermute | solution.py:58
  59.2 1.2 %collective-permute-start.16 = (f32[40,128]{1,0:T(8,128)S(1)}, f32[40,128]{1,0:T(8,128)S(1)}, u32[]{:S(2)}, u32[]{:S(2)}) collective-permute-start(f32[40,128]{1,0:T(8,128)S(1)} %get-tuple-element.54), channel_id=1, source_target_pairs={{0,4},{1,5},{2,6},{3,7},{4,0},{5,1},{6,2},{7,3},{8,12},{9,13},{10,... | collective-permute-start | bytes 61448 | tf_op jit(solution)/shard_map/ppermute | solution.py:58
  60.4 1.3 %collective-permute-start.17 = (f32[40,128]{1,0:T(8,128)S(1)}, f32[40,128]{1,0:T(8,128)S(1)}, u32[]{:S(2)}, u32[]{:S(2)}) collective-permute-start(f32[40,128]{1,0:T(8,128)S(1)} %get-tuple-element.54), channel_id=1, source_target_pairs={{0,6},{1,7},{2,0},{3,1},{4,2},{5,3},{6,4},{7,5},{8,14},{9,15},{10,... | collective-permute-start | bytes 61448 | tf_op jit(solution)/shard_map/ppermute | solution.py:58
  61.7 0.0 collective-permute-done.15
  61.7 2.2 %collective-permute-done.16 = f32[40,128]{1,0:T(8,128)S(1)} collective-permute-done((f32[40,128]{1,0:T(8,128)S(1)}, f32[40,128]{1,0:T(8,128)S(1)}, u32[]{:S(2)}, u32[]{:S(2)}) %collective-permute-start.16) | collective-permute-done | bytes 20512 | tf_op jit(solution)/shard_map/ppermute | solution.py:58
  63.9 0.3 collective-permute-done.17
  64.2 0.9 %collective-permute-start.18 = (f32[40,128]{1,0:T(8,128)S(1)}, f32[40,128]{1,0:T(8,128)S(1)}, u32[]{:S(2)}, u32[]{:S(2)}) collective-permute-start(f32[40,128]{1,0:T(8,128)S(1)} %add_add_fusion.refs_0_), channel_id=1, source_target_pairs={{0,1},{1,0},{2,3},{3,2},{4,5},{5,4},{6,7},{7,6},{8,9},{9,8},{10,11... | collective-permute-start | bytes 61448 | tf_op jit(solution)/shard_map/ppermute | solution.py:63
  65.1 0.0 copy-done.3
  65.1 2.9 %collective-permute-done.18.refs_1_ = f32[40,128]{1,0:T(8,128)S(1)} collective-permute-done((f32[40,128]{1,0:T(8,128)S(1)}, f32[40,128]{1,0:T(8,128)S(1)}, u32[]{:S(2)}, u32[]{:S(2)}) %collective-permute-start.18) | collective-permute-done | bytes 20512 | tf_op jit(solution)/shard_map/ppermute | solution.py:63
  68.0 2.3 %norm.1 = bf16[5120,384]{1,0:T(8,128)(2,1)} custom-call(bf16[5120,384]{1,0:T(8,128)(2,1)S(1)} %get-tuple-element.53.gated_ref, f32[1,384]{1,0:T(1,128)S(1)} %broadcast_in_dim.7.gain_ref, f32[40,128]{1,0:T(8,128)S(1)} %add_add_fusion.refs_0_, f32[40,128]{1,0:T(8,128)S(1)} %collective-permute-done.18.refs_1_), custom_call_target="tpu_custom_call" | custom-call | flops 1000 | bytes 1000 | tf_op jit(solution)/shard_map/norm/pallas_call | solution.py:584
  (9 shorter events, 0.1 us)
Async XLA Ops:
  0.0 3.5 %copy-start.4 = (bf16[4,16]{1,0:T(4,128)(2,1)S(1)}, bf16[4,16]{1,0:T(4,128)(2,1)}, u32[]{:S(2)}) copy-start(bf16[4,16]{1,0:T(4,128)(2,1)} %param.16) | copy-start | bytes 388
  0.0 3.6 %copy-start.5 = (bf16[4,16]{1,0:T(4,128)(2,1)S(1)}, bf16[4,16]{1,0:T(4,128)(2,1)}, u32[]{:S(2)}) copy-start(bf16[4,16]{1,0:T(4,128)(2,1)} %param.17) | copy-start | bytes 388
  0.0 13.4 %copy-start.6 = (f32[6]{0:T(128)S(1)}, f32[6]{0:T(128)}, u32[]{:S(2)}) copy-start(f32[6]{0:T(128)} %param.18) | copy-start | bytes 76
  0.0 13.5 %copy-start.1 = (f32[5120,6]{0,1:T(8,128)S(1)}, f32[5120,6]{0,1:T(8,128)}, u32[]{:S(2)}) copy-start(f32[5120,6]{0,1:T(8,128)} %param.14) | copy-start | bytes 368644
  0.0 14.8 %copy-start.2 = (bf16[4,384]{1,0:T(4,128)(2,1)S(1)}, bf16[4,384]{1,0:T(4,128)(2,1)}, u32[]{:S(2)}) copy-start(bf16[4,384]{1,0:T(4,128)(2,1)} %param.15) | copy-start | bytes 9220
  1.1 3.2 %collective-permute-start = (bf16[48,384]{1,0:T(8,128)(2,1)S(1)}, bf16[48,384]{1,0:T(8,128)(2,1)S(1)}, u32[]{:S(2)}, u32[]{:S(2)}) collective-permute-start(bf16[48,384]{1,0:T(8,128)(2,1)S(1)} %get-tuple-element.32), channel_id=1, source_target_pairs={{0,8},{8,16},{16,24},{1,9},{9,17},{17,25},{2,10},{10,18},{18,26},{... | collective-permute-start | bytes 110600 | tf_op jit(solution)/shard_map/ppermute | solution.py:605
  5.0 16.7 %collective-permute-start.1 = (bf16[16,5120]{1,0:T(8,128)(2,1)S(1)}, bf16[16,5120]{1,0:T(8,128)(2,1)S(1)}, u32[]{:S(2)}, u32[]{:S(2)}) collective-permute-start(bf16[16,5120]{1,0:T(8,128)(2,1)S(1)} %get-tuple-element.35.refs_0_.refs_2_), channel_id=1, source_target_pairs={{0,2},{1,3},{2,4},{3,5},{4,6},{5,7},{6,0},{7,1},{8,10},{9,11},{10,... | collective-permute-start | bytes 491528 | tf_op jit(solution)/shard_map/ppermute | solution.py:58
  7.4 14.2 %collective-permute-start.2 = (bf16[16,5120]{1,0:T(8,128)(2,1)S(1)}, bf16[16,5120]{1,0:T(8,128)(2,1)S(1)}, u32[]{:S(2)}, u32[]{:S(2)}) collective-permute-start(bf16[16,5120]{1,0:T(8,128)(2,1)S(1)} %get-tuple-element.35.refs_0_.refs_2_), channel_id=1, source_target_pairs={{0,4},{1,5},{2,6},{3,7},{4,0},{5,1},{6,2},{7,3},{8,12},{9,13},{10,... | collective-permute-start | bytes 491528 | tf_op jit(solution)/shard_map/ppermute | solution.py:58
  10.0 11.7 %collective-permute-start.3 = (bf16[16,5120]{1,0:T(8,128)(2,1)S(1)}, bf16[16,5120]{1,0:T(8,128)(2,1)S(1)}, u32[]{:S(2)}, u32[]{:S(2)}) collective-permute-start(bf16[16,5120]{1,0:T(8,128)(2,1)S(1)} %get-tuple-element.35.refs_0_.refs_2_), channel_id=1, source_target_pairs={{0,6},{1,7},{2,0},{3,1},{4,2},{5,3},{6,4},{7,5},{8,14},{9,15},{10,... | collective-permute-start | bytes 491528 | tf_op jit(solution)/shard_map/ppermute | solution.py:58
  11.4 10.3 %collective-permute-start.4 = (bf16[16,5120]{1,0:T(8,128)(2,1)S(1)}, bf16[16,5120]{1,0:T(8,128)(2,1)S(1)}, u32[]{:S(2)}, u32[]{:S(2)}) collective-permute-start(bf16[16,5120]{1,0:T(8,128)(2,1)S(1)} %get-tuple-element.35.refs_0_.refs_2_), channel_id=1, source_target_pairs={{0,1},{1,0},{2,3},{3,2},{4,5},{5,4},{6,7},{7,6},{8,9},{9,8},{10,11... | collective-permute-start | bytes 491528 | tf_op jit(solution)/shard_map/ppermute | solution.py:63
  12.9 8.9 %collective-permute-start.5 = (bf16[16,5120]{1,0:T(8,128)(2,1)S(1)}, bf16[16,5120]{1,0:T(8,128)(2,1)S(1)}, u32[]{:S(2)}, u32[]{:S(2)}) collective-permute-start(bf16[16,5120]{1,0:T(8,128)(2,1)S(1)} %get-tuple-element.37.refs_8_), channel_id=1, source_target_pairs={{0,1},{1,0},{2,3},{3,2},{4,5},{5,4},{6,7},{7,6},{8,9},{9,8},{10,11... | collective-permute-start | bytes 491528 | tf_op jit(solution)/shard_map/ppermute | solution.py:63
  21.6 8.1 %copy-start = (bf16[5120,384]{1,0:T(8,128)(2,1)S(1)}, bf16[5120,384]{1,0:T(8,128)(2,1)}, u32[]{:S(2)}) copy-start(bf16[5120,384]{1,0:T(8,128)(2,1)} %z_ref.1) | copy-start | bytes 11796484
  21.8 14.0 %collective-permute-start.7 = (bf16[48,5120]{1,0:T(8,128)(2,1)S(1)}, bf16[48,5120]{1,0:T(8,128)(2,1)S(1)}, u32[]{:S(2)}, u32[]{:S(2)}) collective-permute-start(bf16[48,5120]{1,0:T(8,128)(2,1)S(1)} %pack.2.refs_2_), channel_id=1, source_target_pairs={{0,1},{1,0},{2,3},{3,2},{4,5},{5,4},{6,7},{7,6},{8,9},{9,8},{10,11... | collective-permute-start | bytes 1474568 | tf_op jit(solution)/shard_map/ppermute | solution.py:63
  23.4 9.5 %collective-permute-start.6 = (bf16[16,5120]{1,0:T(8,128)(2,1)S(1)}, bf16[16,5120]{1,0:T(8,128)(2,1)S(1)}, u32[]{:S(2)}, u32[]{:S(2)}) collective-permute-start(bf16[16,5120]{1,0:T(8,128)(2,1)S(1)} %get-tuple-element.45), channel_id=1, source_target_pairs={{0,2},{1,3},{2,4},{3,5},{4,6},{5,7},{6,0},{7,1},{8,10},{9,11},{10,... | collective-permute-start | bytes 491528 | tf_op jit(solution)/shard_map/ppermute | solution.py:58
  27.4 12.3 %collective-permute-start.10 = (bf16[16,5120]{1,0:T(8,128)(2,1)S(1)}, bf16[16,5120]{1,0:T(8,128)(2,1)S(1)}, u32[]{:S(2)}, u32[]{:S(2)}) collective-permute-start(bf16[16,5120]{1,0:T(8,128)(2,1)S(1)} %get-tuple-element.45), channel_id=1, source_target_pairs={{0,4},{1,5},{2,6},{3,7},{4,0},{5,1},{6,2},{7,3},{8,12},{9,13},{10,... | collective-permute-start | bytes 491528 | tf_op jit(solution)/shard_map/ppermute | solution.py:58
  28.2 11.5 %collective-permute-start.9 = (bf16[16,5120]{1,0:T(8,128)(2,1)S(1)}, bf16[16,5120]{1,0:T(8,128)(2,1)S(1)}, u32[]{:S(2)}, u32[]{:S(2)}) collective-permute-start(bf16[16,5120]{1,0:T(8,128)(2,1)S(1)} %get-tuple-element.45), channel_id=1, source_target_pairs={{0,6},{1,7},{2,0},{3,1},{4,2},{5,3},{6,4},{7,5},{8,14},{9,15},{10,... | collective-permute-start | bytes 491528 | tf_op jit(solution)/shard_map/ppermute | solution.py:58
  32.9 6.7 %collective-permute-start.11 = (bf16[16,5120]{1,0:T(8,128)(2,1)S(1)}, bf16[16,5120]{1,0:T(8,128)(2,1)S(1)}, u32[]{:S(2)}, u32[]{:S(2)}) collective-permute-start(bf16[16,5120]{1,0:T(8,128)(2,1)S(1)} %tie.4.refs_1_.refs_10_), channel_id=1, source_target_pairs={{0,1},{1,0},{2,3},{3,2},{4,5},{5,4},{6,7},{7,6},{8,9},{9,8},{10,11... | collective-permute-start | bytes 491528 | tf_op jit(solution)/shard_map/ppermute | solution.py:63
  37.8 4.0 %collective-permute-start.8 = (bf16[144,384]{1,0:T(8,128)(2,1)S(1)}, bf16[144,384]{1,0:T(8,128)(2,1)S(1)}, u32[]{:S(2)}, u32[]{:S(2)}) collective-permute-start(bf16[144,384]{1,0:T(8,128)(2,1)S(1)} %get-tuple-element.48.refs_2_.mine_ref), channel_id=1, source_target_pairs={{0,8},{8,0},{16,24},{24,16},{1,9},{9,1},{17,25},{25,17},{2,10},{10... | collective-permute-start | bytes 331784 | tf_op jit(solution)/shard_map/ppermute | solution.py:648
  39.7 7.8 %collective-permute-start.14 = (bf16[32,3072]{1,0:T(8,128)(2,1)S(1)}, bf16[32,3072]{1,0:T(8,128)(2,1)S(1)}, u32[]{:S(2)}, u32[]{:S(2)}) collective-permute-start(bf16[32,3072]{1,0:T(8,128)(2,1)S(1)} %get-tuple-element.49.token_ref), channel_id=1, source_target_pairs={{0,1},{1,0},{2,3},{3,2},{4,5},{5,4},{6,7},{7,6},{8,9},{9,8},{10,11... | collective-permute-start | bytes 589832 | tf_op jit(solution)/shard_map/ppermute | solution.py:63
  40.6 12.2 %collective-permute-start.13 = (bf16[32,2048]{1,0:T(8,128)(2,1)S(1)}, bf16[32,2048]{1,0:T(8,128)(2,1)S(1)}, u32[]{:S(2)}, u32[]{:S(2)}) collective-permute-start(bf16[32,2048]{1,0:T(8,128)(2,1)S(1)} %get-tuple-element.50), channel_id=1, source_target_pairs={{0,1},{1,0},{2,3},{3,2},{4,5},{5,4},{6,7},{7,6},{8,9},{9,8},{10,11... | collective-permute-start | bytes 393224 | tf_op jit(solution)/shard_map/ppermute | solution.py:63
  41.8 6.4 %collective-permute-start.12 = (bf16[144,384]{1,0:T(8,128)(2,1)S(1)}, bf16[144,384]{1,0:T(8,128)(2,1)S(1)}, u32[]{:S(2)}, u32[]{:S(2)}) collective-permute-start(bf16[144,384]{1,0:T(8,128)(2,1)S(1)} %join.1), channel_id=1, source_target_pairs={{0,16},{8,24},{1,17},{9,25},{2,18},{10,26},{3,19},{11,27},{4,20},{... | collective-permute-start | bytes 331784 | tf_op jit(solution)/shard_map/ppermute | solution.py:648
  52.9 12.3 %copy-start.3 = (f32[384]{0:T(512)S(1)}, f32[384]{0:T(512)}, u32[]{:S(2)}) copy-start(f32[384]{0:T(512)} %param.19) | copy-start | bytes 4612
  56.0 5.7 %collective-permute-start.15 = (f32[40,128]{1,0:T(8,128)S(1)}, f32[40,128]{1,0:T(8,128)S(1)}, u32[]{:S(2)}, u32[]{:S(2)}) collective-permute-start(f32[40,128]{1,0:T(8,128)S(1)} %get-tuple-element.54), channel_id=1, source_target_pairs={{0,2},{1,3},{2,4},{3,5},{4,6},{5,7},{6,0},{7,1},{8,10},{9,11},{10,... | collective-permute-start | bytes 61448 | tf_op jit(solution)/shard_map/ppermute | solution.py:58
  59.2 4.7 %collective-permute-start.16 = (f32[40,128]{1,0:T(8,128)S(1)}, f32[40,128]{1,0:T(8,128)S(1)}, u32[]{:S(2)}, u32[]{:S(2)}) collective-permute-start(f32[40,128]{1,0:T(8,128)S(1)} %get-tuple-element.54), channel_id=1, source_target_pairs={{0,4},{1,5},{2,6},{3,7},{4,0},{5,1},{6,2},{7,3},{8,12},{9,13},{10,... | collective-permute-start | bytes 61448 | tf_op jit(solution)/shard_map/ppermute | solution.py:58
  60.4 3.8 %collective-permute-start.17 = (f32[40,128]{1,0:T(8,128)S(1)}, f32[40,128]{1,0:T(8,128)S(1)}, u32[]{:S(2)}, u32[]{:S(2)}) collective-permute-start(f32[40,128]{1,0:T(8,128)S(1)} %get-tuple-element.54), channel_id=1, source_target_pairs={{0,6},{1,7},{2,0},{3,1},{4,2},{5,3},{6,4},{7,5},{8,14},{9,15},{10,... | collective-permute-start | bytes 61448 | tf_op jit(solution)/shard_map/ppermute | solution.py:58
  64.2 3.8 %collective-permute-start.18 = (f32[40,128]{1,0:T(8,128)S(1)}, f32[40,128]{1,0:T(8,128)S(1)}, u32[]{:S(2)}, u32[]{:S(2)}) collective-permute-start(f32[40,128]{1,0:T(8,128)S(1)} %add_add_fusion.refs_0_), channel_id=1, source_target_pairs={{0,1},{1,0},{2,3},{3,2},{4,5},{5,4},{6,7},{7,6},{8,9},{9,8},{10,11... | collective-permute-start | bytes 61448 | tf_op jit(solution)/shard_map/ppermute | solution.py:63

commit v7 on v5

--- a/solution.py
+++ b/solution.py
@@ -567,7 +567,7 @@
         total = total + ref[...]
     scale = lax.rsqrt(total * (1.0 / channels) + 1e-05).T
     gain = gain_ref[...]
-    step = TILE // 2
+    step = 2 * SUB
     copies = []
     for t in range(gated_ref.shape[0] // step):
         for s in range(t * step // SUB, (t + 1) * step // SUB):
@@ -590,7 +590,7 @@
         out_shape=pltpu.HBM((length, width), BF16),
         scratch_shapes=[
             pltpu.VMEM((length, width), BF16),
-            pltpu.SemaphoreType.DMA((2 * length // TILE,)),
+            pltpu.SemaphoreType.DMA((length // (2 * SUB),)),
         ],
         compiler_params=params(),
         cost_estimate=BRIEF,

time: 70.6 us -> 70.6 us (level)
  no operation moved by 1% of the time
where the time goes in v7:
time: 70.6 us; the launch traced here: 70.3 us
  starting transfers between devices  31.9 us (45%)
  Pallas kernels  25.1 us (36%)
  waiting for transfers between devices  12.8 us (18%)
    ppermute x9, starting transfers between devices, along_outer(): lax.ppermute(piece, 'head', outer_pairs(d))  18.3 us
    pallas_call x2, Pallas kernels, scan(): pl.pallas_call(functools.partial(scan_kernel, span, len(others), b_rows,...  7.67 us
    ppermute x7, waiting for transfers between devices, along_inner(): lax.ppermute(p, 'head', inner_pairs(e))  7.13 us
    ppermute x7, starting transfers between devices, along_inner(): lax.ppermute(p, 'head', inner_pairs(e))  7.01 us
    pallas_call x1, Pallas kernels, head_conv(): pl.pallas_call(functools.partial(head_conv_kernel, first, heads), grid=(c...  6.84 us
    ppermute x9, waiting for transfers between devices, along_outer(): lax.ppermute(piece, 'head', outer_pairs(d))  4.33 us
    ppermute x2, starting transfers between devices, body(): others.append(lax.ppermute(mine, 'seq', pairs))  4.16 us
    pallas_call x1, Pallas kernels, gates(): pl.pallas_call(gates_kernel, grid=(length // TILE,), in_specs=[wide, pl.B...  3.16 us
  transfers between devices with their start and end apart: 19, of which 9 were waited for; matrix products, arithmetic and copies ran while one was open for 0% of the time, Pallas kernels for 25%

profile of v7, /device:TPU:0, one launch (start us, length us, event | category | flops | bytes accessed | tf_op | source)
XLA Modules:
  0.0 70.3 jit_solution(16498614027503229274)
XLA Ops:
  0.0 0.0 copy-start.4
  0.0 0.0 copy-start.5
  0.0 0.0 copy-start.6
  0.0 0.0 copy-start.2
  0.0 1.1 %tails.1 = (bf16[48,384]{1,0:T(8,128)(2,1)S(1)}, bf16[16,5120]{1,0:T(8,128)(2,1)S(1)}, bf16[16,5120]{1,0:T(8,128)(2,1)S(1)}) custom-call(bf16[5120,384]{1,0:T(8,128)(2,1)} %before_ref.1, bf16[16,5120]{1,0:T(8,128)(2,1)} %bitcast.9, bf16[16,5120]{1,0:T(8,128)(2,1)} %bitcast.10), custom_call_target="tpu_custom_call" | custom-call | flops 1000 | bytes 1000 | tf_op jit(solution)/shard_map/tails/pallas_call | solution.py:124
  1.1 2.4 %collective-permute-start = (bf16[48,384]{1,0:T(8,128)(2,1)S(1)}, bf16[48,384]{1,0:T(8,128)(2,1)S(1)}, u32[]{:S(2)}, u32[]{:S(2)}) collective-permute-start(bf16[48,384]{1,0:T(8,128)(2,1)S(1)} %get-tuple-element.32), channel_id=1, source_target_pairs={{0,8},{8,16},{16,24},{1,9},{9,17},{17,25},{2,10},{10,18},{18,26},{... | collective-permute-start | bytes 110600 | tf_op jit(solution)/shard_map/ppermute | solution.py:607
  3.5 0.0 copy-done.4
  3.5 0.1 copy.20
  3.6 0.0 copy-done.5
  3.6 0.1 copy.21
  3.7 0.7 collective-permute-done.halo_ref
  4.4 0.6 shared_conv.1
  5.0 2.5 %collective-permute-start.1 = (bf16[16,5120]{1,0:T(8,128)(2,1)S(1)}, bf16[16,5120]{1,0:T(8,128)(2,1)S(1)}, u32[]{:S(2)}, u32[]{:S(2)}) collective-permute-start(bf16[16,5120]{1,0:T(8,128)(2,1)S(1)} %get-tuple-element.35.refs_0_.refs_2_), channel_id=1, source_target_pairs={{0,2},{1,3},{2,4},{3,5},{4,6},{5,7},{6,0},{7,1},{8,10},{9,11},{10,... | collective-permute-start | bytes 491528 | tf_op jit(solution)/shard_map/ppermute | solution.py:58
  7.4 2.6 %collective-permute-start.2 = (bf16[16,5120]{1,0:T(8,128)(2,1)S(1)}, bf16[16,5120]{1,0:T(8,128)(2,1)S(1)}, u32[]{:S(2)}, u32[]{:S(2)}) collective-permute-start(bf16[16,5120]{1,0:T(8,128)(2,1)S(1)} %get-tuple-element.35.refs_0_.refs_2_), channel_id=1, source_target_pairs={{0,4},{1,5},{2,6},{3,7},{4,0},{5,1},{6,2},{7,3},{8,12},{9,13},{10,... | collective-permute-start | bytes 491528 | tf_op jit(solution)/shard_map/ppermute | solution.py:58
  10.0 1.3 %collective-permute-start.3 = (bf16[16,5120]{1,0:T(8,128)(2,1)S(1)}, bf16[16,5120]{1,0:T(8,128)(2,1)S(1)}, u32[]{:S(2)}, u32[]{:S(2)}) collective-permute-start(bf16[16,5120]{1,0:T(8,128)(2,1)S(1)} %get-tuple-element.35.refs_0_.refs_2_), channel_id=1, source_target_pairs={{0,6},{1,7},{2,0},{3,1},{4,2},{5,3},{6,4},{7,5},{8,14},{9,15},{10,... | collective-permute-start | bytes 491528 | tf_op jit(solution)/shard_map/ppermute | solution.py:58
  11.4 1.5 %collective-permute-start.4 = (bf16[16,5120]{1,0:T(8,128)(2,1)S(1)}, bf16[16,5120]{1,0:T(8,128)(2,1)S(1)}, u32[]{:S(2)}, u32[]{:S(2)}) collective-permute-start(bf16[16,5120]{1,0:T(8,128)(2,1)S(1)} %get-tuple-element.35.refs_0_.refs_2_), channel_id=1, source_target_pairs={{0,1},{1,0},{2,3},{3,2},{4,5},{5,4},{6,7},{7,6},{8,9},{9,8},{10,11... | collective-permute-start | bytes 491528 | tf_op jit(solution)/shard_map/ppermute | solution.py:63
  12.9 0.5 collective-permute-start.5
  13.4 0.0 copy-done.6
  13.4 0.1 copy.22.rate_ref
  13.5 0.0 copy-done.1
  13.5 1.3 %rows.1 = (f32[8,5120]{1,0:T(8,128)S(1)}, bf16[5120,40]{1,0:T(8,128)(2,1)S(1)}, f32[40,384]{1,0:T(8,128)S(1)}) custom-call(f32[6,5120]{1,0:T(8,128)S(1)} %bitcast.6, f32[6,1]{1,0:T(8,128)S(1)} %copy.22.rate_ref), custom_call_target="tpu_custom_call" | custom-call | flops 1000 | bytes 1000 | tf_op jit(solution)/shard_map/rows/pallas_call | solution.py:219
  14.8 0.0 copy-done.2
  14.8 6.8 %head_conv.1 = (bf16[5120,384]{1,0:T(8,128)(2,1)S(1)}, bf16[5120,384]{1,0:T(8,128)(2,1)S(1)}) custom-call(bf16[5120,384]{1,0:T(8,128)(2,1)} %before_ref.1, bf16[5120,384]{1,0:T(8,128)(2,1)} %before_ref.1, bf16[48,384]{1,0:T(8,128)(2,1)S(1)} %collective-permute-done.halo_ref, f32[4,384]{1,0:T(4,128)S(1)} %convert_element_type.17.taps_ref, ...), custom_call_target="tpu_custom_call" | custom-call | flops 1000 | bytes 1000 | tf_op jit(solution)/shard_map/head_conv/pallas_call | solution.py:275
  21.6 0.0 copy-start
  21.7 0.0 collective-permute-done.1.refs_0_.refs_2_.refs_4_
  21.7 0.0 collective-permute-done.2.refs_1_.refs_3_.refs_5_
  21.7 0.0 collective-permute-done.3.refs_2_.refs_4_.refs_6_
  21.7 0.0 collective-permute-done.4.refs_4_.refs_1_.refs_3_
  21.7 0.1 collective-permute-done.5.refs_5_.refs_9_
  21.8 1.6 %collective-permute-start.7 = (bf16[48,5120]{1,0:T(8,128)(2,1)S(1)}, bf16[48,5120]{1,0:T(8,128)(2,1)S(1)}, u32[]{:S(2)}, u32[]{:S(2)}) collective-permute-start(bf16[48,5120]{1,0:T(8,128)(2,1)S(1)} %pack.2.refs_2_), channel_id=1, source_target_pairs={{0,1},{1,0},{2,3},{3,2},{4,5},{5,4},{6,7},{7,6},{8,9},{9,8},{10,11... | collective-permute-start | bytes 1474568 | tf_op jit(solution)/shard_map/ppermute | solution.py:63
  23.4 4.0 %collective-permute-start.6 = (bf16[16,5120]{1,0:T(8,128)(2,1)S(1)}, bf16[16,5120]{1,0:T(8,128)(2,1)S(1)}, u32[]{:S(2)}, u32[]{:S(2)}) collective-permute-start(bf16[16,5120]{1,0:T(8,128)(2,1)S(1)} %get-tuple-element.45), channel_id=1, source_target_pairs={{0,2},{1,3},{2,4},{3,5},{4,6},{5,7},{6,0},{7,1},{8,10},{9,11},{10,... | collective-permute-start | bytes 491528 | tf_op jit(solution)/shard_map/ppermute | solution.py:58
  27.4 0.8 %collective-permute-start.10 = (bf16[16,5120]{1,0:T(8,128)(2,1)S(1)}, bf16[16,5120]{1,0:T(8,128)(2,1)S(1)}, u32[]{:S(2)}, u32[]{:S(2)}) collective-permute-start(bf16[16,5120]{1,0:T(8,128)(2,1)S(1)} %get-tuple-element.45), channel_id=1, source_target_pairs={{0,4},{1,5},{2,6},{3,7},{4,0},{5,1},{6,2},{7,3},{8,12},{9,13},{10,... | collective-permute-start | bytes 491528 | tf_op jit(solution)/shard_map/ppermute | solution.py:58
  28.2 1.6 %collective-permute-start.9 = (bf16[16,5120]{1,0:T(8,128)(2,1)S(1)}, bf16[16,5120]{1,0:T(8,128)(2,1)S(1)}, u32[]{:S(2)}, u32[]{:S(2)}) collective-permute-start(bf16[16,5120]{1,0:T(8,128)(2,1)S(1)} %get-tuple-element.45), channel_id=1, source_target_pairs={{0,6},{1,7},{2,0},{3,1},{4,2},{5,3},{6,4},{7,5},{8,14},{9,15},{10,... | collective-permute-start | bytes 491528 | tf_op jit(solution)/shard_map/ppermute | solution.py:58
  29.8 0.0 copy-done
  29.8 3.2 %gates.1 = (f32[5120,384]{1,0:T(8,128)S(1)}, f32[1920,128]{1,0:T(8,128)S(1)}, f32[3,320,128]{2,1,0:T(8,128)S(1)}) custom-call(bf16[5120,384]{1,0:T(8,128)(2,1)S(1)} %copy-done, bf16[5120,40]{1,0:T(8,128)(2,1)S(1)} %get-tuple-element.38.column_ref, f32[8,5120]{1,0:T(8,128)S(1)} %get-tuple-element.39.q_ref), custom_call_target="tpu_custom_call" | custom-call | flops 1000 | bytes 1000 | tf_op jit(solution)/shard_map/gates/pallas_call | solution.py:334
  32.9 0.0 collective-permute-done.6.refs_0_
  32.9 0.4 collective-permute-start.11
  33.3 2.5 %collective-permute-done.7.refs_5_.refs_7_ = bf16[48,5120]{1,0:T(8,128)(2,1)S(1)} collective-permute-done((bf16[48,5120]{1,0:T(8,128)(2,1)S(1)}, bf16[48,5120]{1,0:T(8,128)(2,1)S(1)}, u32[]{:S(2)}, u32[]{:S(2)}) %collective-permute-start.7) | collective-permute-done | bytes 491552 | tf_op jit(solution)/shard_map/ppermute | solution.py:63
  35.9 1.9 %last_state.1 = (bf16[144,384]{1,0:T(8,128)(2,1)S(1)}, f32[5120,384]{1,0:T(8,128)S(1)}, f32[40,384]{1,0:T(8,128)S(1)}) custom-call(bf16[5120,384]{1,0:T(8,128)(2,1)S(1)} %get-tuple-element.43.wt_ref, f32[40,384]{1,0:T(8,128)S(1)} %tie.5.decay_ref, bf16[16,5120]{1,0:T(8,128)(2,1)S(1)} %get-tuple-element.35.refs_0_.refs_2_, ...), custom_call_target="tpu_custom_call" | custom-call | flops 1000 | bytes 1000 | tf_op jit(solution)/shard_map/last_state/pallas_call | solution.py:401
  37.8 0.1 collective-permute-start.8
  37.9 1.8 %collective-permute-done.10.refs_1_.refs_11_ = bf16[16,5120]{1,0:T(8,128)(2,1)S(1)} collective-permute-done((bf16[16,5120]{1,0:T(8,128)(2,1)S(1)}, bf16[16,5120]{1,0:T(8,128)(2,1)S(1)}, u32[]{:S(2)}, u32[]{:S(2)}) %collective-permute-start.10) | collective-permute-done | bytes 163872 | tf_op jit(solution)/shard_map/ppermute | solution.py:58
  39.6 0.0 collective-permute-done.9.refs_0_.refs_12_
  39.6 0.0 collective-permute-done.11.refs_3_.refs_13_
  39.7 1.0 %collective-permute-start.14 = (bf16[32,3072]{1,0:T(8,128)(2,1)S(1)}, bf16[32,3072]{1,0:T(8,128)(2,1)S(1)}, u32[]{:S(2)}, u32[]{:S(2)}) collective-permute-start(bf16[32,3072]{1,0:T(8,128)(2,1)S(1)} %get-tuple-element.49.token_ref), channel_id=1, source_target_pairs={{0,1},{1,0},{2,3},{3,2},{4,5},{5,4},{6,7},{7,6},{8,9},{9,8},{10,11... | collective-permute-start | bytes 589832 | tf_op jit(solution)/shard_map/ppermute | solution.py:63
  40.6 1.1 %collective-permute-start.13 = (bf16[32,2048]{1,0:T(8,128)(2,1)S(1)}, bf16[32,2048]{1,0:T(8,128)(2,1)S(1)}, u32[]{:S(2)}, u32[]{:S(2)}) collective-permute-start(bf16[32,2048]{1,0:T(8,128)(2,1)S(1)} %get-tuple-element.50), channel_id=1, source_target_pairs={{0,1},{1,0},{2,3},{3,2},{4,5},{5,4},{6,7},{7,6},{8,9},{9,8},{10,11... | collective-permute-start | bytes 393224 | tf_op jit(solution)/shard_map/ppermute | solution.py:63
  41.8 0.0 collective-permute-done.8.other_ref.refs_0_
  41.8 0.1 join.1
  41.8 4.1 %collective-permute-start.12 = (bf16[144,384]{1,0:T(8,128)(2,1)S(1)}, bf16[144,384]{1,0:T(8,128)(2,1)S(1)}, u32[]{:S(2)}, u32[]{:S(2)}) collective-permute-start(bf16[144,384]{1,0:T(8,128)(2,1)S(1)} %join.1), channel_id=1, source_target_pairs={{0,16},{8,24},{1,17},{9,25},{2,18},{10,26},{3,19},{11,27},{4,20},{... | collective-permute-start | bytes 331784 | tf_op jit(solution)/shard_map/ppermute | solution.py:650
  45.9 1.6 %collective-permute-done.14.refs_14_ = bf16[32,3072]{1,0:T(8,128)(2,1)S(1)} collective-permute-done((bf16[32,3072]{1,0:T(8,128)(2,1)S(1)}, bf16[32,3072]{1,0:T(8,128)(2,1)S(1)}, u32[]{:S(2)}, u32[]{:S(2)}) %collective-permute-start.14) | collective-permute-done | bytes 196640 | tf_op jit(solution)/shard_map/ppermute | solution.py:63
  47.5 0.7 %collective-permute-done.12.refs_1_ = bf16[144,384]{1,0:T(8,128)(2,1)S(1)} collective-permute-done((bf16[144,384]{1,0:T(8,128)(2,1)S(1)}, bf16[144,384]{1,0:T(8,128)(2,1)S(1)}, u32[]{:S(2)}, u32[]{:S(2)}) %collective-permute-start.12) | collective-permute-done | bytes 110624 | tf_op jit(solution)/shard_map/ppermute | solution.py:650
  48.2 4.6 %scan.2 = (bf16[5120,384]{1,0:T(8,128)(2,1)S(1)}, f32[40,128]{1,0:T(8,128)S(1)}) custom-call(f32[5120,384]{1,0:T(8,128)S(1)} %get-tuple-element.40.gate_ref, f32[1920,128]{1,0:T(8,128)S(1)} %get-tuple-element.41.factor_ref, f32[3,320,128]{2,1,0:T(8,128)S(1)} %get-tuple-element.42.refs_1_.start_ref, bf16[5120,384]{1,0:T(8,128)(2,1)S(1)} %get-tuple-element.36.refs_3_.xs_ref, ...), custom_call_target="tpu_custom_call" | custom-call | flops 1000 | bytes 1000 | tf_op jit(solution)/shard_map/scan/pallas_call | solution.py:542
  52.8 0.0 collective-permute-done.13.refs_14_
  52.8 0.0 copy-start.3
  52.8 3.1 %scan.3 = (bf16[5120,384]{1,0:T(8,128)(2,1)S(1)}, f32[40,128]{1,0:T(8,128)S(1)}) custom-call(f32[5120,384]{1,0:T(8,128)S(1)} %get-tuple-element.40.gate_ref, f32[1920,128]{1,0:T(8,128)S(1)} %get-tuple-element.41.factor_ref, f32[3,320,128]{2,1,0:T(8,128)S(1)} %get-tuple-element.42.refs_1_.start_ref, ...), custom_call_target="tpu_custom_call", output_to_operand_aliasing={{0}: (21, {}), {1}: (22, {})} | custom-call | flops 1000 | bytes 1000 | tf_op jit(solution)/shard_map/scan/pallas_call | solution.py:542
  55.9 3.2 %collective-permute-start.15 = (f32[40,128]{1,0:T(8,128)S(1)}, f32[40,128]{1,0:T(8,128)S(1)}, u32[]{:S(2)}, u32[]{:S(2)}) collective-permute-start(f32[40,128]{1,0:T(8,128)S(1)} %get-tuple-element.54), channel_id=1, source_target_pairs={{0,2},{1,3},{2,4},{3,5},{4,6},{5,7},{6,0},{7,1},{8,10},{9,11},{10,... | collective-permute-start | bytes 61448 | tf_op jit(solution)/shard_map/ppermute | solution.py:58
  59.2 1.2 %collective-permute-start.16 = (f32[40,128]{1,0:T(8,128)S(1)}, f32[40,128]{1,0:T(8,128)S(1)}, u32[]{:S(2)}, u32[]{:S(2)}) collective-permute-start(f32[40,128]{1,0:T(8,128)S(1)} %get-tuple-element.54), channel_id=1, source_target_pairs={{0,4},{1,5},{2,6},{3,7},{4,0},{5,1},{6,2},{7,3},{8,12},{9,13},{10,... | collective-permute-start | bytes 61448 | tf_op jit(solution)/shard_map/ppermute | solution.py:58
  60.3 1.2 %collective-permute-start.17 = (f32[40,128]{1,0:T(8,128)S(1)}, f32[40,128]{1,0:T(8,128)S(1)}, u32[]{:S(2)}, u32[]{:S(2)}) collective-permute-start(f32[40,128]{1,0:T(8,128)S(1)} %get-tuple-element.54), channel_id=1, source_target_pairs={{0,6},{1,7},{2,0},{3,1},{4,2},{5,3},{6,4},{7,5},{8,14},{9,15},{10,... | collective-permute-start | bytes 61448 | tf_op jit(solution)/shard_map/ppermute | solution.py:58
  61.5 0.0 collective-permute-done.15
  61.5 2.3 %collective-permute-done.16 = f32[40,128]{1,0:T(8,128)S(1)} collective-permute-done((f32[40,128]{1,0:T(8,128)S(1)}, f32[40,128]{1,0:T(8,128)S(1)}, u32[]{:S(2)}, u32[]{:S(2)}) %collective-permute-start.16) | collective-permute-done | bytes 20512 | tf_op jit(solution)/shard_map/ppermute | solution.py:58
  63.9 0.3 collective-permute-done.17
  64.1 0.9 %collective-permute-start.18 = (f32[40,128]{1,0:T(8,128)S(1)}, f32[40,128]{1,0:T(8,128)S(1)}, u32[]{:S(2)}, u32[]{:S(2)}) collective-permute-start(f32[40,128]{1,0:T(8,128)S(1)} %add_add_fusion.refs_0_), channel_id=1, source_target_pairs={{0,1},{1,0},{2,3},{3,2},{4,5},{5,4},{6,7},{7,6},{8,9},{9,8},{10,11... | collective-permute-start | bytes 61448 | tf_op jit(solution)/shard_map/ppermute | solution.py:63
  65.0 0.0 copy-done.3
  65.0 2.9 %collective-permute-done.18.refs_1_ = f32[40,128]{1,0:T(8,128)S(1)} collective-permute-done((f32[40,128]{1,0:T(8,128)S(1)}, f32[40,128]{1,0:T(8,128)S(1)}, u32[]{:S(2)}, u32[]{:S(2)}) %collective-permute-start.18) | collective-permute-done | bytes 20512 | tf_op jit(solution)/shard_map/ppermute | solution.py:63
  68.0 2.4 %norm.1 = bf16[5120,384]{1,0:T(8,128)(2,1)} custom-call(bf16[5120,384]{1,0:T(8,128)(2,1)S(1)} %get-tuple-element.53.gated_ref, f32[1,384]{1,0:T(1,128)S(1)} %broadcast_in_dim.7.gain_ref, f32[40,128]{1,0:T(8,128)S(1)} %add_add_fusion.refs_0_, f32[40,128]{1,0:T(8,128)S(1)} %collective-permute-done.18.refs_1_), custom_call_target="tpu_custom_call" | custom-call | flops 1000 | bytes 1000 | tf_op jit(solution)/shard_map/norm/pallas_call | solution.py:586
  (9 shorter events, 0.1 us)
Async XLA Ops:
  0.0 3.5 %copy-start.4 = (bf16[4,16]{1,0:T(4,128)(2,1)S(1)}, bf16[4,16]{1,0:T(4,128)(2,1)}, u32[]{:S(2)}) copy-start(bf16[4,16]{1,0:T(4,128)(2,1)} %param.16) | copy-start | bytes 388
  0.0 3.6 %copy-start.5 = (bf16[4,16]{1,0:T(4,128)(2,1)S(1)}, bf16[4,16]{1,0:T(4,128)(2,1)}, u32[]{:S(2)}) copy-start(bf16[4,16]{1,0:T(4,128)(2,1)} %param.17) | copy-start | bytes 388
  0.0 13.4 %copy-start.6 = (f32[6]{0:T(128)S(1)}, f32[6]{0:T(128)}, u32[]{:S(2)}) copy-start(f32[6]{0:T(128)} %param.18) | copy-start | bytes 76
  0.0 13.5 %copy-start.1 = (f32[5120,6]{0,1:T(8,128)S(1)}, f32[5120,6]{0,1:T(8,128)}, u32[]{:S(2)}) copy-start(f32[5120,6]{0,1:T(8,128)} %param.14) | copy-start | bytes 368644
  0.0 14.8 %copy-start.2 = (bf16[4,384]{1,0:T(4,128)(2,1)S(1)}, bf16[4,384]{1,0:T(4,128)(2,1)}, u32[]{:S(2)}) copy-start(bf16[4,384]{1,0:T(4,128)(2,1)} %param.15) | copy-start | bytes 9220
  1.1 3.2 %collective-permute-start = (bf16[48,384]{1,0:T(8,128)(2,1)S(1)}, bf16[48,384]{1,0:T(8,128)(2,1)S(1)}, u32[]{:S(2)}, u32[]{:S(2)}) collective-permute-start(bf16[48,384]{1,0:T(8,128)(2,1)S(1)} %get-tuple-element.32), channel_id=1, source_target_pairs={{0,8},{8,16},{16,24},{1,9},{9,17},{17,25},{2,10},{10,18},{18,26},{... | collective-permute-start | bytes 110600 | tf_op jit(solution)/shard_map/ppermute | solution.py:607
  5.0 16.7 %collective-permute-start.1 = (bf16[16,5120]{1,0:T(8,128)(2,1)S(1)}, bf16[16,5120]{1,0:T(8,128)(2,1)S(1)}, u32[]{:S(2)}, u32[]{:S(2)}) collective-permute-start(bf16[16,5120]{1,0:T(8,128)(2,1)S(1)} %get-tuple-element.35.refs_0_.refs_2_), channel_id=1, source_target_pairs={{0,2},{1,3},{2,4},{3,5},{4,6},{5,7},{6,0},{7,1},{8,10},{9,11},{10,... | collective-permute-start | bytes 491528 | tf_op jit(solution)/shard_map/ppermute | solution.py:58
  7.4 14.2 %collective-permute-start.2 = (bf16[16,5120]{1,0:T(8,128)(2,1)S(1)}, bf16[16,5120]{1,0:T(8,128)(2,1)S(1)}, u32[]{:S(2)}, u32[]{:S(2)}) collective-permute-start(bf16[16,5120]{1,0:T(8,128)(2,1)S(1)} %get-tuple-element.35.refs_0_.refs_2_), channel_id=1, source_target_pairs={{0,4},{1,5},{2,6},{3,7},{4,0},{5,1},{6,2},{7,3},{8,12},{9,13},{10,... | collective-permute-start | bytes 491528 | tf_op jit(solution)/shard_map/ppermute | solution.py:58
  10.0 11.7 %collective-permute-start.3 = (bf16[16,5120]{1,0:T(8,128)(2,1)S(1)}, bf16[16,5120]{1,0:T(8,128)(2,1)S(1)}, u32[]{:S(2)}, u32[]{:S(2)}) collective-permute-start(bf16[16,5120]{1,0:T(8,128)(2,1)S(1)} %get-tuple-element.35.refs_0_.refs_2_), channel_id=1, source_target_pairs={{0,6},{1,7},{2,0},{3,1},{4,2},{5,3},{6,4},{7,5},{8,14},{9,15},{10,... | collective-permute-start | bytes 491528 | tf_op jit(solution)/shard_map/ppermute | solution.py:58
  11.4 10.3 %collective-permute-start.4 = (bf16[16,5120]{1,0:T(8,128)(2,1)S(1)}, bf16[16,5120]{1,0:T(8,128)(2,1)S(1)}, u32[]{:S(2)}, u32[]{:S(2)}) collective-permute-start(bf16[16,5120]{1,0:T(8,128)(2,1)S(1)} %get-tuple-element.35.refs_0_.refs_2_), channel_id=1, source_target_pairs={{0,1},{1,0},{2,3},{3,2},{4,5},{5,4},{6,7},{7,6},{8,9},{9,8},{10,11... | collective-permute-start | bytes 491528 | tf_op jit(solution)/shard_map/ppermute | solution.py:63
  12.9 8.9 %collective-permute-start.5 = (bf16[16,5120]{1,0:T(8,128)(2,1)S(1)}, bf16[16,5120]{1,0:T(8,128)(2,1)S(1)}, u32[]{:S(2)}, u32[]{:S(2)}) collective-permute-start(bf16[16,5120]{1,0:T(8,128)(2,1)S(1)} %get-tuple-element.37.refs_8_), channel_id=1, source_target_pairs={{0,1},{1,0},{2,3},{3,2},{4,5},{5,4},{6,7},{7,6},{8,9},{9,8},{10,11... | collective-permute-start | bytes 491528 | tf_op jit(solution)/shard_map/ppermute | solution.py:63
  21.6 8.1 %copy-start = (bf16[5120,384]{1,0:T(8,128)(2,1)S(1)}, bf16[5120,384]{1,0:T(8,128)(2,1)}, u32[]{:S(2)}) copy-start(bf16[5120,384]{1,0:T(8,128)(2,1)} %z_ref.1) | copy-start | bytes 11796484
  21.8 14.0 %collective-permute-start.7 = (bf16[48,5120]{1,0:T(8,128)(2,1)S(1)}, bf16[48,5120]{1,0:T(8,128)(2,1)S(1)}, u32[]{:S(2)}, u32[]{:S(2)}) collective-permute-start(bf16[48,5120]{1,0:T(8,128)(2,1)S(1)} %pack.2.refs_2_), channel_id=1, source_target_pairs={{0,1},{1,0},{2,3},{3,2},{4,5},{5,4},{6,7},{7,6},{8,9},{9,8},{10,11... | collective-permute-start | bytes 1474568 | tf_op jit(solution)/shard_map/ppermute | solution.py:63
  23.4 9.5 %collective-permute-start.6 = (bf16[16,5120]{1,0:T(8,128)(2,1)S(1)}, bf16[16,5120]{1,0:T(8,128)(2,1)S(1)}, u32[]{:S(2)}, u32[]{:S(2)}) collective-permute-start(bf16[16,5120]{1,0:T(8,128)(2,1)S(1)} %get-tuple-element.45), channel_id=1, source_target_pairs={{0,2},{1,3},{2,4},{3,5},{4,6},{5,7},{6,0},{7,1},{8,10},{9,11},{10,... | collective-permute-start | bytes 491528 | tf_op jit(solution)/shard_map/ppermute | solution.py:58
  27.4 12.3 %collective-permute-start.10 = (bf16[16,5120]{1,0:T(8,128)(2,1)S(1)}, bf16[16,5120]{1,0:T(8,128)(2,1)S(1)}, u32[]{:S(2)}, u32[]{:S(2)}) collective-permute-start(bf16[16,5120]{1,0:T(8,128)(2,1)S(1)} %get-tuple-element.45), channel_id=1, source_target_pairs={{0,4},{1,5},{2,6},{3,7},{4,0},{5,1},{6,2},{7,3},{8,12},{9,13},{10,... | collective-permute-start | bytes 491528 | tf_op jit(solution)/shard_map/ppermute | solution.py:58
  28.2 11.5 %collective-permute-start.9 = (bf16[16,5120]{1,0:T(8,128)(2,1)S(1)}, bf16[16,5120]{1,0:T(8,128)(2,1)S(1)}, u32[]{:S(2)}, u32[]{:S(2)}) collective-permute-start(bf16[16,5120]{1,0:T(8,128)(2,1)S(1)} %get-tuple-element.45), channel_id=1, source_target_pairs={{0,6},{1,7},{2,0},{3,1},{4,2},{5,3},{6,4},{7,5},{8,14},{9,15},{10,... | collective-permute-start | bytes 491528 | tf_op jit(solution)/shard_map/ppermute | solution.py:58
  32.9 6.7 %collective-permute-start.11 = (bf16[16,5120]{1,0:T(8,128)(2,1)S(1)}, bf16[16,5120]{1,0:T(8,128)(2,1)S(1)}, u32[]{:S(2)}, u32[]{:S(2)}) collective-permute-start(bf16[16,5120]{1,0:T(8,128)(2,1)S(1)} %tie.4.refs_1_.refs_10_), channel_id=1, source_target_pairs={{0,1},{1,0},{2,3},{3,2},{4,5},{5,4},{6,7},{7,6},{8,9},{9,8},{10,11... | collective-permute-start | bytes 491528 | tf_op jit(solution)/shard_map/ppermute | solution.py:63
  37.8 4.0 %collective-permute-start.8 = (bf16[144,384]{1,0:T(8,128)(2,1)S(1)}, bf16[144,384]{1,0:T(8,128)(2,1)S(1)}, u32[]{:S(2)}, u32[]{:S(2)}) collective-permute-start(bf16[144,384]{1,0:T(8,128)(2,1)S(1)} %get-tuple-element.48.refs_2_.mine_ref), channel_id=1, source_target_pairs={{0,8},{8,0},{16,24},{24,16},{1,9},{9,1},{17,25},{25,17},{2,10},{10... | collective-permute-start | bytes 331784 | tf_op jit(solution)/shard_map/ppermute | solution.py:650
  39.7 7.8 %collective-permute-start.14 = (bf16[32,3072]{1,0:T(8,128)(2,1)S(1)}, bf16[32,3072]{1,0:T(8,128)(2,1)S(1)}, u32[]{:S(2)}, u32[]{:S(2)}) collective-permute-start(bf16[32,3072]{1,0:T(8,128)(2,1)S(1)} %get-tuple-element.49.token_ref), channel_id=1, source_target_pairs={{0,1},{1,0},{2,3},{3,2},{4,5},{5,4},{6,7},{7,6},{8,9},{9,8},{10,11... | collective-permute-start | bytes 589832 | tf_op jit(solution)/shard_map/ppermute | solution.py:63
  40.6 12.2 %collective-permute-start.13 = (bf16[32,2048]{1,0:T(8,128)(2,1)S(1)}, bf16[32,2048]{1,0:T(8,128)(2,1)S(1)}, u32[]{:S(2)}, u32[]{:S(2)}) collective-permute-start(bf16[32,2048]{1,0:T(8,128)(2,1)S(1)} %get-tuple-element.50), channel_id=1, source_target_pairs={{0,1},{1,0},{2,3},{3,2},{4,5},{5,4},{6,7},{7,6},{8,9},{9,8},{10,11... | collective-permute-start | bytes 393224 | tf_op jit(solution)/shard_map/ppermute | solution.py:63
  41.8 6.4 %collective-permute-start.12 = (bf16[144,384]{1,0:T(8,128)(2,1)S(1)}, bf16[144,384]{1,0:T(8,128)(2,1)S(1)}, u32[]{:S(2)}, u32[]{:S(2)}) collective-permute-start(bf16[144,384]{1,0:T(8,128)(2,1)S(1)} %join.1), channel_id=1, source_target_pairs={{0,16},{8,24},{1,17},{9,25},{2,18},{10,26},{3,19},{11,27},{4,20},{... | collective-permute-start | bytes 331784 | tf_op jit(solution)/shard_map/ppermute | solution.py:650
  52.8 12.2 %copy-start.3 = (f32[384]{0:T(512)S(1)}, f32[384]{0:T(512)}, u32[]{:S(2)}) copy-start(f32[384]{0:T(512)} %param.19) | copy-start | bytes 4612
  55.9 5.6 %collective-permute-start.15 = (f32[40,128]{1,0:T(8,128)S(1)}, f32[40,128]{1,0:T(8,128)S(1)}, u32[]{:S(2)}, u32[]{:S(2)}) collective-permute-start(f32[40,128]{1,0:T(8,128)S(1)} %get-tuple-element.54), channel_id=1, source_target_pairs={{0,2},{1,3},{2,4},{3,5},{4,6},{5,7},{6,0},{7,1},{8,10},{9,11},{10,... | collective-permute-start | bytes 61448 | tf_op jit(solution)/shard_map/ppermute | solution.py:58
  59.2 4.7 %collective-permute-start.16 = (f32[40,128]{1,0:T(8,128)S(1)}, f32[40,128]{1,0:T(8,128)S(1)}, u32[]{:S(2)}, u32[]{:S(2)}) collective-permute-start(f32[40,128]{1,0:T(8,128)S(1)} %get-tuple-element.54), channel_id=1, source_target_pairs={{0,4},{1,5},{2,6},{3,7},{4,0},{5,1},{6,2},{7,3},{8,12},{9,13},{10,... | collective-permute-start | bytes 61448 | tf_op jit(solution)/shard_map/ppermute | solution.py:58
  60.3 3.8 %collective-permute-start.17 = (f32[40,128]{1,0:T(8,128)S(1)}, f32[40,128]{1,0:T(8,128)S(1)}, u32[]{:S(2)}, u32[]{:S(2)}) collective-permute-start(f32[40,128]{1,0:T(8,128)S(1)} %get-tuple-element.54), channel_id=1, source_target_pairs={{0,6},{1,7},{2,0},{3,1},{4,2},{5,3},{6,4},{7,5},{8,14},{9,15},{10,... | collective-permute-start | bytes 61448 | tf_op jit(solution)/shard_map/ppermute | solution.py:58
  64.1 3.8 %collective-permute-start.18 = (f32[40,128]{1,0:T(8,128)S(1)}, f32[40,128]{1,0:T(8,128)S(1)}, u32[]{:S(2)}, u32[]{:S(2)}) collective-permute-start(f32[40,128]{1,0:T(8,128)S(1)} %add_add_fusion.refs_0_), channel_id=1, source_target_pairs={{0,1},{1,0},{2,3},{3,2},{4,5},{5,4},{6,7},{7,6},{8,9},{9,8},{10,11... | collective-permute-start | bytes 61448 | tf_op jit(solution)/shard_map/ppermute | solution.py:63

commit v8 on v7

--- a/solution.py
+++ b/solution.py
@@ -572,7 +572,10 @@
     for t in range(gated_ref.shape[0] // step):
         for s in range(t * step // SUB, (t + 1) * step // SUB):
             at = slice(s * SUB, (s + 1) * SUB)
-            rows[at] = (gated_ref[at].astype(F32) * scale[:, s : s + 1] * gain).astype(BF16)
+            wide = jnp.broadcast_to(scale[:, s : s + 1], (SUB, SUB))
+            for p in range(gated_ref.shape[1] // SUB):
+                cols = slice(p * SUB, (p + 1) * SUB)
+                rows[at, cols] = (gated_ref[at, cols].astype(F32) * wide * gain[:, cols]).astype(BF16)
         at = slice(t * step, (t + 1) * step)
         copies.append(pltpu.make_async_copy(rows.at[at], out_ref.at[at], sems.at[t]))
         copies[-1].start()

time: 70.6 us -> 70.6 us (level)
  no operation moved by 1% of the time
where the time goes in v8:
time: 70.6 us; the launch traced here: 70.3 us
  starting transfers between devices  31.9 us (45%)
  Pallas kernels  25.1 us (36%)
  waiting for transfers between devices  12.8 us (18%)
    ppermute x9, starting transfers between devices, along_outer(): lax.ppermute(piece, 'head', outer_pairs(d))  18.3 us
    pallas_call x2, Pallas kernels, scan(): pl.pallas_call(functools.partial(scan_kernel, span, len(others), b_rows,...  7.67 us
    ppermute x7, waiting for transfers between devices, along_inner(): lax.ppermute(p, 'head', inner_pairs(e))  7.13 us
    ppermute x7, starting transfers between devices, along_inner(): lax.ppermute(p, 'head', inner_pairs(e))  7.01 us
    pallas_call x1, Pallas kernels, head_conv(): pl.pallas_call(functools.partial(head_conv_kernel, first, heads), grid=(c...  6.84 us
    ppermute x9, waiting for transfers between devices, along_outer(): lax.ppermute(piece, 'head', outer_pairs(d))  4.33 us
    ppermute x2, starting transfers between devices, body(): others.append(lax.ppermute(mine, 'seq', pairs))  4.16 us
    pallas_call x1, Pallas kernels, gates(): pl.pallas_call(gates_kernel, grid=(length // TILE,), in_specs=[wide, pl.B...  3.16 us
  transfers between devices with their start and end apart: 19, of which 9 were waited for; matrix products, arithmetic and copies ran while one was open for 0% of the time, Pallas kernels for 25%

profile of v8, /device:TPU:0, one launch (start us, length us, event | category | flops | bytes accessed | tf_op | source)
XLA Modules:
  0.0 70.3 jit_solution(5062542346557404018)
XLA Ops:
  0.0 0.0 copy-start.4
  0.0 0.0 copy-start.5
  0.0 0.0 copy-start.6
  0.0 0.0 copy-start.2
  0.0 1.1 %tails.1 = (bf16[48,384]{1,0:T(8,128)(2,1)S(1)}, bf16[16,5120]{1,0:T(8,128)(2,1)S(1)}, bf16[16,5120]{1,0:T(8,128)(2,1)S(1)}) custom-call(bf16[5120,384]{1,0:T(8,128)(2,1)} %before_ref.1, bf16[16,5120]{1,0:T(8,128)(2,1)} %bitcast.9, bf16[16,5120]{1,0:T(8,128)(2,1)} %bitcast.10), custom_call_target="tpu_custom_call" | custom-call | flops 1000 | bytes 1000 | tf_op jit(solution)/shard_map/tails/pallas_call | solution.py:124
  1.1 2.4 %collective-permute-start = (bf16[48,384]{1,0:T(8,128)(2,1)S(1)}, bf16[48,384]{1,0:T(8,128)(2,1)S(1)}, u32[]{:S(2)}, u32[]{:S(2)}) collective-permute-start(bf16[48,384]{1,0:T(8,128)(2,1)S(1)} %get-tuple-element.32), channel_id=1, source_target_pairs={{0,8},{8,16},{16,24},{1,9},{9,17},{17,25},{2,10},{10,18},{18,26},{... | collective-permute-start | bytes 110600 | tf_op jit(solution)/shard_map/ppermute | solution.py:610
  3.5 0.0 copy-done.4
  3.5 0.1 copy.20
  3.6 0.0 copy-done.5
  3.6 0.1 copy.21
  3.7 0.7 collective-permute-done.halo_ref
  4.4 0.6 shared_conv.1
  5.0 2.5 %collective-permute-start.1 = (bf16[16,5120]{1,0:T(8,128)(2,1)S(1)}, bf16[16,5120]{1,0:T(8,128)(2,1)S(1)}, u32[]{:S(2)}, u32[]{:S(2)}) collective-permute-start(bf16[16,5120]{1,0:T(8,128)(2,1)S(1)} %get-tuple-element.35.refs_0_.refs_2_), channel_id=1, source_target_pairs={{0,2},{1,3},{2,4},{3,5},{4,6},{5,7},{6,0},{7,1},{8,10},{9,11},{10,... | collective-permute-start | bytes 491528 | tf_op jit(solution)/shard_map/ppermute | solution.py:58
  7.4 2.6 %collective-permute-start.2 = (bf16[16,5120]{1,0:T(8,128)(2,1)S(1)}, bf16[16,5120]{1,0:T(8,128)(2,1)S(1)}, u32[]{:S(2)}, u32[]{:S(2)}) collective-permute-start(bf16[16,5120]{1,0:T(8,128)(2,1)S(1)} %get-tuple-element.35.refs_0_.refs_2_), channel_id=1, source_target_pairs={{0,4},{1,5},{2,6},{3,7},{4,0},{5,1},{6,2},{7,3},{8,12},{9,13},{10,... | collective-permute-start | bytes 491528 | tf_op jit(solution)/shard_map/ppermute | solution.py:58
  10.0 1.3 %collective-permute-start.3 = (bf16[16,5120]{1,0:T(8,128)(2,1)S(1)}, bf16[16,5120]{1,0:T(8,128)(2,1)S(1)}, u32[]{:S(2)}, u32[]{:S(2)}) collective-permute-start(bf16[16,5120]{1,0:T(8,128)(2,1)S(1)} %get-tuple-element.35.refs_0_.refs_2_), channel_id=1, source_target_pairs={{0,6},{1,7},{2,0},{3,1},{4,2},{5,3},{6,4},{7,5},{8,14},{9,15},{10,... | collective-permute-start | bytes 491528 | tf_op jit(solution)/shard_map/ppermute | solution.py:58
  11.4 1.5 %collective-permute-start.4 = (bf16[16,5120]{1,0:T(8,128)(2,1)S(1)}, bf16[16,5120]{1,0:T(8,128)(2,1)S(1)}, u32[]{:S(2)}, u32[]{:S(2)}) collective-permute-start(bf16[16,5120]{1,0:T(8,128)(2,1)S(1)} %get-tuple-element.35.refs_0_.refs_2_), channel_id=1, source_target_pairs={{0,1},{1,0},{2,3},{3,2},{4,5},{5,4},{6,7},{7,6},{8,9},{9,8},{10,11... | collective-permute-start | bytes 491528 | tf_op jit(solution)/shard_map/ppermute | solution.py:63
  12.9 0.5 collective-permute-start.5
  13.4 0.0 copy-done.6
  13.4 0.1 copy.22.rate_ref
  13.5 0.0 copy-done.1
  13.5 1.3 %rows.1 = (f32[8,5120]{1,0:T(8,128)S(1)}, bf16[5120,40]{1,0:T(8,128)(2,1)S(1)}, f32[40,384]{1,0:T(8,128)S(1)}) custom-call(f32[6,5120]{1,0:T(8,128)S(1)} %bitcast.6, f32[6,1]{1,0:T(8,128)S(1)} %copy.22.rate_ref), custom_call_target="tpu_custom_call" | custom-call | flops 1000 | bytes 1000 | tf_op jit(solution)/shard_map/rows/pallas_call | solution.py:219
  14.8 0.0 copy-done.2
  14.8 6.8 %head_conv.1 = (bf16[5120,384]{1,0:T(8,128)(2,1)S(1)}, bf16[5120,384]{1,0:T(8,128)(2,1)S(1)}) custom-call(bf16[5120,384]{1,0:T(8,128)(2,1)} %before_ref.1, bf16[5120,384]{1,0:T(8,128)(2,1)} %before_ref.1, bf16[48,384]{1,0:T(8,128)(2,1)S(1)} %collective-permute-done.halo_ref, f32[4,384]{1,0:T(4,128)S(1)} %convert_element_type.17.taps_ref, ...), custom_call_target="tpu_custom_call" | custom-call | flops 1000 | bytes 1000 | tf_op jit(solution)/shard_map/head_conv/pallas_call | solution.py:275
  21.6 0.0 copy-start
  21.7 0.0 collective-permute-done.1.refs_0_.refs_2_.refs_4_
  21.7 0.0 collective-permute-done.2.refs_1_.refs_3_.refs_5_
  21.7 0.0 collective-permute-done.3.refs_2_.refs_4_.refs_6_
  21.7 0.0 collective-permute-done.4.refs_4_.refs_1_.refs_3_
  21.7 0.1 collective-permute-done.5.refs_5_.refs_9_
  21.8 1.6 %collective-permute-start.7 = (bf16[48,5120]{1,0:T(8,128)(2,1)S(1)}, bf16[48,5120]{1,0:T(8,128)(2,1)S(1)}, u32[]{:S(2)}, u32[]{:S(2)}) collective-permute-start(bf16[48,5120]{1,0:T(8,128)(2,1)S(1)} %pack.2.refs_2_), channel_id=1, source_target_pairs={{0,1},{1,0},{2,3},{3,2},{4,5},{5,4},{6,7},{7,6},{8,9},{9,8},{10,11... | collective-permute-start | bytes 1474568 | tf_op jit(solution)/shard_map/ppermute | solution.py:63
  23.4 4.0 %collective-permute-start.6 = (bf16[16,5120]{1,0:T(8,128)(2,1)S(1)}, bf16[16,5120]{1,0:T(8,128)(2,1)S(1)}, u32[]{:S(2)}, u32[]{:S(2)}) collective-permute-start(bf16[16,5120]{1,0:T(8,128)(2,1)S(1)} %get-tuple-element.45), channel_id=1, source_target_pairs={{0,2},{1,3},{2,4},{3,5},{4,6},{5,7},{6,0},{7,1},{8,10},{9,11},{10,... | collective-permute-start | bytes 491528 | tf_op jit(solution)/shard_map/ppermute | solution.py:58
  27.4 0.8 %collective-permute-start.10 = (bf16[16,5120]{1,0:T(8,128)(2,1)S(1)}, bf16[16,5120]{1,0:T(8,128)(2,1)S(1)}, u32[]{:S(2)}, u32[]{:S(2)}) collective-permute-start(bf16[16,5120]{1,0:T(8,128)(2,1)S(1)} %get-tuple-element.45), channel_id=1, source_target_pairs={{0,4},{1,5},{2,6},{3,7},{4,0},{5,1},{6,2},{7,3},{8,12},{9,13},{10,... | collective-permute-start | bytes 491528 | tf_op jit(solution)/shard_map/ppermute | solution.py:58
  28.2 1.6 %collective-permute-start.9 = (bf16[16,5120]{1,0:T(8,128)(2,1)S(1)}, bf16[16,5120]{1,0:T(8,128)(2,1)S(1)}, u32[]{:S(2)}, u32[]{:S(2)}) collective-permute-start(bf16[16,5120]{1,0:T(8,128)(2,1)S(1)} %get-tuple-element.45), channel_id=1, source_target_pairs={{0,6},{1,7},{2,0},{3,1},{4,2},{5,3},{6,4},{7,5},{8,14},{9,15},{10,... | collective-permute-start | bytes 491528 | tf_op jit(solution)/shard_map/ppermute | solution.py:58
  29.8 0.0 copy-done
  29.8 3.2 %gates.1 = (f32[5120,384]{1,0:T(8,128)S(1)}, f32[1920,128]{1,0:T(8,128)S(1)}, f32[3,320,128]{2,1,0:T(8,128)S(1)}) custom-call(bf16[5120,384]{1,0:T(8,128)(2,1)S(1)} %copy-done, bf16[5120,40]{1,0:T(8,128)(2,1)S(1)} %get-tuple-element.38.column_ref, f32[8,5120]{1,0:T(8,128)S(1)} %get-tuple-element.39.q_ref), custom_call_target="tpu_custom_call" | custom-call | flops 1000 | bytes 1000 | tf_op jit(solution)/shard_map/gates/pallas_call | solution.py:334
  32.9 0.0 collective-permute-done.6.refs_0_
  32.9 0.4 collective-permute-start.11
  33.3 2.5 %collective-permute-done.7.refs_5_.refs_7_ = bf16[48,5120]{1,0:T(8,128)(2,1)S(1)} collective-permute-done((bf16[48,5120]{1,0:T(8,128)(2,1)S(1)}, bf16[48,5120]{1,0:T(8,128)(2,1)S(1)}, u32[]{:S(2)}, u32[]{:S(2)}) %collective-permute-start.7) | collective-permute-done | bytes 491552 | tf_op jit(solution)/shard_map/ppermute | solution.py:63
  35.9 1.9 %last_state.1 = (bf16[144,384]{1,0:T(8,128)(2,1)S(1)}, f32[5120,384]{1,0:T(8,128)S(1)}, f32[40,384]{1,0:T(8,128)S(1)}) custom-call(bf16[5120,384]{1,0:T(8,128)(2,1)S(1)} %get-tuple-element.43.wt_ref, f32[40,384]{1,0:T(8,128)S(1)} %tie.5.decay_ref, bf16[16,5120]{1,0:T(8,128)(2,1)S(1)} %get-tuple-element.35.refs_0_.refs_2_, ...), custom_call_target="tpu_custom_call" | custom-call | flops 1000 | bytes 1000 | tf_op jit(solution)/shard_map/last_state/pallas_call | solution.py:401
  37.8 0.1 collective-permute-start.8
  37.9 1.8 %collective-permute-done.10.refs_1_.refs_11_ = bf16[16,5120]{1,0:T(8,128)(2,1)S(1)} collective-permute-done((bf16[16,5120]{1,0:T(8,128)(2,1)S(1)}, bf16[16,5120]{1,0:T(8,128)(2,1)S(1)}, u32[]{:S(2)}, u32[]{:S(2)}) %collective-permute-start.10) | collective-permute-done | bytes 163872 | tf_op jit(solution)/shard_map/ppermute | solution.py:58
  39.6 0.0 collective-permute-done.9.refs_0_.refs_12_
  39.6 0.0 collective-permute-done.11.refs_3_.refs_13_
  39.7 1.0 %collective-permute-start.14 = (bf16[32,3072]{1,0:T(8,128)(2,1)S(1)}, bf16[32,3072]{1,0:T(8,128)(2,1)S(1)}, u32[]{:S(2)}, u32[]{:S(2)}) collective-permute-start(bf16[32,3072]{1,0:T(8,128)(2,1)S(1)} %get-tuple-element.49.token_ref), channel_id=1, source_target_pairs={{0,1},{1,0},{2,3},{3,2},{4,5},{5,4},{6,7},{7,6},{8,9},{9,8},{10,11... | collective-permute-start | bytes 589832 | tf_op jit(solution)/shard_map/ppermute | solution.py:63
  40.6 1.1 %collective-permute-start.13 = (bf16[32,2048]{1,0:T(8,128)(2,1)S(1)}, bf16[32,2048]{1,0:T(8,128)(2,1)S(1)}, u32[]{:S(2)}, u32[]{:S(2)}) collective-permute-start(bf16[32,2048]{1,0:T(8,128)(2,1)S(1)} %get-tuple-element.50), channel_id=1, source_target_pairs={{0,1},{1,0},{2,3},{3,2},{4,5},{5,4},{6,7},{7,6},{8,9},{9,8},{10,11... | collective-permute-start | bytes 393224 | tf_op jit(solution)/shard_map/ppermute | solution.py:63
  41.8 0.0 collective-permute-done.8.other_ref.refs_0_
  41.8 0.1 join.1
  41.8 4.1 %collective-permute-start.12 = (bf16[144,384]{1,0:T(8,128)(2,1)S(1)}, bf16[144,384]{1,0:T(8,128)(2,1)S(1)}, u32[]{:S(2)}, u32[]{:S(2)}) collective-permute-start(bf16[144,384]{1,0:T(8,128)(2,1)S(1)} %join.1), channel_id=1, source_target_pairs={{0,16},{8,24},{1,17},{9,25},{2,18},{10,26},{3,19},{11,27},{4,20},{... | collective-permute-start | bytes 331784 | tf_op jit(solution)/shard_map/ppermute | solution.py:653
  45.9 1.6 %collective-permute-done.14.refs_14_ = bf16[32,3072]{1,0:T(8,128)(2,1)S(1)} collective-permute-done((bf16[32,3072]{1,0:T(8,128)(2,1)S(1)}, bf16[32,3072]{1,0:T(8,128)(2,1)S(1)}, u32[]{:S(2)}, u32[]{:S(2)}) %collective-permute-start.14) | collective-permute-done | bytes 196640 | tf_op jit(solution)/shard_map/ppermute | solution.py:63
  47.5 0.7 %collective-permute-done.12.refs_1_ = bf16[144,384]{1,0:T(8,128)(2,1)S(1)} collective-permute-done((bf16[144,384]{1,0:T(8,128)(2,1)S(1)}, bf16[144,384]{1,0:T(8,128)(2,1)S(1)}, u32[]{:S(2)}, u32[]{:S(2)}) %collective-permute-start.12) | collective-permute-done | bytes 110624 | tf_op jit(solution)/shard_map/ppermute | solution.py:653
  48.2 4.6 %scan.2 = (bf16[5120,384]{1,0:T(8,128)(2,1)S(1)}, f32[40,128]{1,0:T(8,128)S(1)}) custom-call(f32[5120,384]{1,0:T(8,128)S(1)} %get-tuple-element.40.gate_ref, f32[1920,128]{1,0:T(8,128)S(1)} %get-tuple-element.41.factor_ref, f32[3,320,128]{2,1,0:T(8,128)S(1)} %get-tuple-element.42.refs_1_.start_ref, bf16[5120,384]{1,0:T(8,128)(2,1)S(1)} %get-tuple-element.36.refs_3_.xs_ref, ...), custom_call_target="tpu_custom_call" | custom-call | flops 1000 | bytes 1000 | tf_op jit(solution)/shard_map/scan/pallas_call | solution.py:542
  52.8 0.0 collective-permute-done.13.refs_14_
  52.8 0.0 copy-start.3
  52.8 3.1 %scan.3 = (bf16[5120,384]{1,0:T(8,128)(2,1)S(1)}, f32[40,128]{1,0:T(8,128)S(1)}) custom-call(f32[5120,384]{1,0:T(8,128)S(1)} %get-tuple-element.40.gate_ref, f32[1920,128]{1,0:T(8,128)S(1)} %get-tuple-element.41.factor_ref, f32[3,320,128]{2,1,0:T(8,128)S(1)} %get-tuple-element.42.refs_1_.start_ref, ...), custom_call_target="tpu_custom_call", output_to_operand_aliasing={{0}: (21, {}), {1}: (22, {})} | custom-call | flops 1000 | bytes 1000 | tf_op jit(solution)/shard_map/scan/pallas_call | solution.py:542
  55.9 3.2 %collective-permute-start.15 = (f32[40,128]{1,0:T(8,128)S(1)}, f32[40,128]{1,0:T(8,128)S(1)}, u32[]{:S(2)}, u32[]{:S(2)}) collective-permute-start(f32[40,128]{1,0:T(8,128)S(1)} %get-tuple-element.54), channel_id=1, source_target_pairs={{0,2},{1,3},{2,4},{3,5},{4,6},{5,7},{6,0},{7,1},{8,10},{9,11},{10,... | collective-permute-start | bytes 61448 | tf_op jit(solution)/shard_map/ppermute | solution.py:58
  59.2 1.2 %collective-permute-start.16 = (f32[40,128]{1,0:T(8,128)S(1)}, f32[40,128]{1,0:T(8,128)S(1)}, u32[]{:S(2)}, u32[]{:S(2)}) collective-permute-start(f32[40,128]{1,0:T(8,128)S(1)} %get-tuple-element.54), channel_id=1, source_target_pairs={{0,4},{1,5},{2,6},{3,7},{4,0},{5,1},{6,2},{7,3},{8,12},{9,13},{10,... | collective-permute-start | bytes 61448 | tf_op jit(solution)/shard_map/ppermute | solution.py:58
  60.3 1.2 %collective-permute-start.17 = (f32[40,128]{1,0:T(8,128)S(1)}, f32[40,128]{1,0:T(8,128)S(1)}, u32[]{:S(2)}, u32[]{:S(2)}) collective-permute-start(f32[40,128]{1,0:T(8,128)S(1)} %get-tuple-element.54), channel_id=1, source_target_pairs={{0,6},{1,7},{2,0},{3,1},{4,2},{5,3},{6,4},{7,5},{8,14},{9,15},{10,... | collective-permute-start | bytes 61448 | tf_op jit(solution)/shard_map/ppermute | solution.py:58
  61.5 0.0 collective-permute-done.15
  61.5 2.3 %collective-permute-done.16 = f32[40,128]{1,0:T(8,128)S(1)} collective-permute-done((f32[40,128]{1,0:T(8,128)S(1)}, f32[40,128]{1,0:T(8,128)S(1)}, u32[]{:S(2)}, u32[]{:S(2)}) %collective-permute-start.16) | collective-permute-done | bytes 20512 | tf_op jit(solution)/shard_map/ppermute | solution.py:58
  63.9 0.3 collective-permute-done.17
  64.1 0.9 %collective-permute-start.18 = (f32[40,128]{1,0:T(8,128)S(1)}, f32[40,128]{1,0:T(8,128)S(1)}, u32[]{:S(2)}, u32[]{:S(2)}) collective-permute-start(f32[40,128]{1,0:T(8,128)S(1)} %add_add_fusion.refs_0_), channel_id=1, source_target_pairs={{0,1},{1,0},{2,3},{3,2},{4,5},{5,4},{6,7},{7,6},{8,9},{9,8},{10,11... | collective-permute-start | bytes 61448 | tf_op jit(solution)/shard_map/ppermute | solution.py:63
  65.0 0.0 copy-done.3
  65.0 2.9 %collective-permute-done.18.refs_1_ = f32[40,128]{1,0:T(8,128)S(1)} collective-permute-done((f32[40,128]{1,0:T(8,128)S(1)}, f32[40,128]{1,0:T(8,128)S(1)}, u32[]{:S(2)}, u32[]{:S(2)}) %collective-permute-start.18) | collective-permute-done | bytes 20512 | tf_op jit(solution)/shard_map/ppermute | solution.py:63
  68.0 2.4 %norm.1 = bf16[5120,384]{1,0:T(8,128)(2,1)} custom-call(bf16[5120,384]{1,0:T(8,128)(2,1)S(1)} %get-tuple-element.53.gated_ref, f32[1,384]{1,0:T(1,128)S(1)} %broadcast_in_dim.7.gain_ref, f32[40,128]{1,0:T(8,128)S(1)} %add_add_fusion.refs_0_, f32[40,128]{1,0:T(8,128)S(1)} %collective-permute-done.18.refs_1_), custom_call_target="tpu_custom_call" | custom-call | flops 1000 | bytes 1000 | tf_op jit(solution)/shard_map/norm/pallas_call | solution.py:589
  (9 shorter events, 0.1 us)
Async XLA Ops:
  0.0 3.5 %copy-start.4 = (bf16[4,16]{1,0:T(4,128)(2,1)S(1)}, bf16[4,16]{1,0:T(4,128)(2,1)}, u32[]{:S(2)}) copy-start(bf16[4,16]{1,0:T(4,128)(2,1)} %param.16) | copy-start | bytes 388
  0.0 3.6 %copy-start.5 = (bf16[4,16]{1,0:T(4,128)(2,1)S(1)}, bf16[4,16]{1,0:T(4,128)(2,1)}, u32[]{:S(2)}) copy-start(bf16[4,16]{1,0:T(4,128)(2,1)} %param.17) | copy-start | bytes 388
  0.0 13.4 %copy-start.6 = (f32[6]{0:T(128)S(1)}, f32[6]{0:T(128)}, u32[]{:S(2)}) copy-start(f32[6]{0:T(128)} %param.18) | copy-start | bytes 76
  0.0 13.5 %copy-start.1 = (f32[5120,6]{0,1:T(8,128)S(1)}, f32[5120,6]{0,1:T(8,128)}, u32[]{:S(2)}) copy-start(f32[5120,6]{0,1:T(8,128)} %param.14) | copy-start | bytes 368644
  0.0 14.8 %copy-start.2 = (bf16[4,384]{1,0:T(4,128)(2,1)S(1)}, bf16[4,384]{1,0:T(4,128)(2,1)}, u32[]{:S(2)}) copy-start(bf16[4,384]{1,0:T(4,128)(2,1)} %param.15) | copy-start | bytes 9220
  1.1 3.2 %collective-permute-start = (bf16[48,384]{1,0:T(8,128)(2,1)S(1)}, bf16[48,384]{1,0:T(8,128)(2,1)S(1)}, u32[]{:S(2)}, u32[]{:S(2)}) collective-permute-start(bf16[48,384]{1,0:T(8,128)(2,1)S(1)} %get-tuple-element.32), channel_id=1, source_target_pairs={{0,8},{8,16},{16,24},{1,9},{9,17},{17,25},{2,10},{10,18},{18,26},{... | collective-permute-start | bytes 110600 | tf_op jit(solution)/shard_map/ppermute | solution.py:610
  5.0 16.7 %collective-permute-start.1 = (bf16[16,5120]{1,0:T(8,128)(2,1)S(1)}, bf16[16,5120]{1,0:T(8,128)(2,1)S(1)}, u32[]{:S(2)}, u32[]{:S(2)}) collective-permute-start(bf16[16,5120]{1,0:T(8,128)(2,1)S(1)} %get-tuple-element.35.refs_0_.refs_2_), channel_id=1, source_target_pairs={{0,2},{1,3},{2,4},{3,5},{4,6},{5,7},{6,0},{7,1},{8,10},{9,11},{10,... | collective-permute-start | bytes 491528 | tf_op jit(solution)/shard_map/ppermute | solution.py:58
  7.4 14.2 %collective-permute-start.2 = (bf16[16,5120]{1,0:T(8,128)(2,1)S(1)}, bf16[16,5120]{1,0:T(8,128)(2,1)S(1)}, u32[]{:S(2)}, u32[]{:S(2)}) collective-permute-start(bf16[16,5120]{1,0:T(8,128)(2,1)S(1)} %get-tuple-element.35.refs_0_.refs_2_), channel_id=1, source_target_pairs={{0,4},{1,5},{2,6},{3,7},{4,0},{5,1},{6,2},{7,3},{8,12},{9,13},{10,... | collective-permute-start | bytes 491528 | tf_op jit(solution)/shard_map/ppermute | solution.py:58
  10.0 11.7 %collective-permute-start.3 = (bf16[16,5120]{1,0:T(8,128)(2,1)S(1)}, bf16[16,5120]{1,0:T(8,128)(2,1)S(1)}, u32[]{:S(2)}, u32[]{:S(2)}) collective-permute-start(bf16[16,5120]{1,0:T(8,128)(2,1)S(1)} %get-tuple-element.35.refs_0_.refs_2_), channel_id=1, source_target_pairs={{0,6},{1,7},{2,0},{3,1},{4,2},{5,3},{6,4},{7,5},{8,14},{9,15},{10,... | collective-permute-start | bytes 491528 | tf_op jit(solution)/shard_map/ppermute | solution.py:58
  11.4 10.3 %collective-permute-start.4 = (bf16[16,5120]{1,0:T(8,128)(2,1)S(1)}, bf16[16,5120]{1,0:T(8,128)(2,1)S(1)}, u32[]{:S(2)}, u32[]{:S(2)}) collective-permute-start(bf16[16,5120]{1,0:T(8,128)(2,1)S(1)} %get-tuple-element.35.refs_0_.refs_2_), channel_id=1, source_target_pairs={{0,1},{1,0},{2,3},{3,2},{4,5},{5,4},{6,7},{7,6},{8,9},{9,8},{10,11... | collective-permute-start | bytes 491528 | tf_op jit(solution)/shard_map/ppermute | solution.py:63
  12.9 8.9 %collective-permute-start.5 = (bf16[16,5120]{1,0:T(8,128)(2,1)S(1)}, bf16[16,5120]{1,0:T(8,128)(2,1)S(1)}, u32[]{:S(2)}, u32[]{:S(2)}) collective-permute-start(bf16[16,5120]{1,0:T(8,128)(2,1)S(1)} %get-tuple-element.37.refs_8_), channel_id=1, source_target_pairs={{0,1},{1,0},{2,3},{3,2},{4,5},{5,4},{6,7},{7,6},{8,9},{9,8},{10,11... | collective-permute-start | bytes 491528 | tf_op jit(solution)/shard_map/ppermute | solution.py:63
  21.6 8.1 %copy-start = (bf16[5120,384]{1,0:T(8,128)(2,1)S(1)}, bf16[5120,384]{1,0:T(8,128)(2,1)}, u32[]{:S(2)}) copy-start(bf16[5120,384]{1,0:T(8,128)(2,1)} %z_ref.1) | copy-start | bytes 11796484
  21.8 14.0 %collective-permute-start.7 = (bf16[48,5120]{1,0:T(8,128)(2,1)S(1)}, bf16[48,5120]{1,0:T(8,128)(2,1)S(1)}, u32[]{:S(2)}, u32[]{:S(2)}) collective-permute-start(bf16[48,5120]{1,0:T(8,128)(2,1)S(1)} %pack.2.refs_2_), channel_id=1, source_target_pairs={{0,1},{1,0},{2,3},{3,2},{4,5},{5,4},{6,7},{7,6},{8,9},{9,8},{10,11... | collective-permute-start | bytes 1474568 | tf_op jit(solution)/shard_map/ppermute | solution.py:63
  23.4 9.5 %collective-permute-start.6 = (bf16[16,5120]{1,0:T(8,128)(2,1)S(1)}, bf16[16,5120]{1,0:T(8,128)(2,1)S(1)}, u32[]{:S(2)}, u32[]{:S(2)}) collective-permute-start(bf16[16,5120]{1,0:T(8,128)(2,1)S(1)} %get-tuple-element.45), channel_id=1, source_target_pairs={{0,2},{1,3},{2,4},{3,5},{4,6},{5,7},{6,0},{7,1},{8,10},{9,11},{10,... | collective-permute-start | bytes 491528 | tf_op jit(solution)/shard_map/ppermute | solution.py:58
  27.4 12.3 %collective-permute-start.10 = (bf16[16,5120]{1,0:T(8,128)(2,1)S(1)}, bf16[16,5120]{1,0:T(8,128)(2,1)S(1)}, u32[]{:S(2)}, u32[]{:S(2)}) collective-permute-start(bf16[16,5120]{1,0:T(8,128)(2,1)S(1)} %get-tuple-element.45), channel_id=1, source_target_pairs={{0,4},{1,5},{2,6},{3,7},{4,0},{5,1},{6,2},{7,3},{8,12},{9,13},{10,... | collective-permute-start | bytes 491528 | tf_op jit(solution)/shard_map/ppermute | solution.py:58
  28.2 11.5 %collective-permute-start.9 = (bf16[16,5120]{1,0:T(8,128)(2,1)S(1)}, bf16[16,5120]{1,0:T(8,128)(2,1)S(1)}, u32[]{:S(2)}, u32[]{:S(2)}) collective-permute-start(bf16[16,5120]{1,0:T(8,128)(2,1)S(1)} %get-tuple-element.45), channel_id=1, source_target_pairs={{0,6},{1,7},{2,0},{3,1},{4,2},{5,3},{6,4},{7,5},{8,14},{9,15},{10,... | collective-permute-start | bytes 491528 | tf_op jit(solution)/shard_map/ppermute | solution.py:58
  32.9 6.7 %collective-permute-start.11 = (bf16[16,5120]{1,0:T(8,128)(2,1)S(1)}, bf16[16,5120]{1,0:T(8,128)(2,1)S(1)}, u32[]{:S(2)}, u32[]{:S(2)}) collective-permute-start(bf16[16,5120]{1,0:T(8,128)(2,1)S(1)} %tie.4.refs_1_.refs_10_), channel_id=1, source_target_pairs={{0,1},{1,0},{2,3},{3,2},{4,5},{5,4},{6,7},{7,6},{8,9},{9,8},{10,11... | collective-permute-start | bytes 491528 | tf_op jit(solution)/shard_map/ppermute | solution.py:63
  37.8 4.0 %collective-permute-start.8 = (bf16[144,384]{1,0:T(8,128)(2,1)S(1)}, bf16[144,384]{1,0:T(8,128)(2,1)S(1)}, u32[]{:S(2)}, u32[]{:S(2)}) collective-permute-start(bf16[144,384]{1,0:T(8,128)(2,1)S(1)} %get-tuple-element.48.refs_2_.mine_ref), channel_id=1, source_target_pairs={{0,8},{8,0},{16,24},{24,16},{1,9},{9,1},{17,25},{25,17},{2,10},{10... | collective-permute-start | bytes 331784 | tf_op jit(solution)/shard_map/ppermute | solution.py:653
  39.7 7.8 %collective-permute-start.14 = (bf16[32,3072]{1,0:T(8,128)(2,1)S(1)}, bf16[32,3072]{1,0:T(8,128)(2,1)S(1)}, u32[]{:S(2)}, u32[]{:S(2)}) collective-permute-start(bf16[32,3072]{1,0:T(8,128)(2,1)S(1)} %get-tuple-element.49.token_ref), channel_id=1, source_target_pairs={{0,1},{1,0},{2,3},{3,2},{4,5},{5,4},{6,7},{7,6},{8,9},{9,8},{10,11... | collective-permute-start | bytes 589832 | tf_op jit(solution)/shard_map/ppermute | solution.py:63
  40.6 12.2 %collective-permute-start.13 = (bf16[32,2048]{1,0:T(8,128)(2,1)S(1)}, bf16[32,2048]{1,0:T(8,128)(2,1)S(1)}, u32[]{:S(2)}, u32[]{:S(2)}) collective-permute-start(bf16[32,2048]{1,0:T(8,128)(2,1)S(1)} %get-tuple-element.50), channel_id=1, source_target_pairs={{0,1},{1,0},{2,3},{3,2},{4,5},{5,4},{6,7},{7,6},{8,9},{9,8},{10,11... | collective-permute-start | bytes 393224 | tf_op jit(solution)/shard_map/ppermute | solution.py:63
  41.8 6.4 %collective-permute-start.12 = (bf16[144,384]{1,0:T(8,128)(2,1)S(1)}, bf16[144,384]{1,0:T(8,128)(2,1)S(1)}, u32[]{:S(2)}, u32[]{:S(2)}) collective-permute-start(bf16[144,384]{1,0:T(8,128)(2,1)S(1)} %join.1), channel_id=1, source_target_pairs={{0,16},{8,24},{1,17},{9,25},{2,18},{10,26},{3,19},{11,27},{4,20},{... | collective-permute-start | bytes 331784 | tf_op jit(solution)/shard_map/ppermute | solution.py:653
  52.8 12.2 %copy-start.3 = (f32[384]{0:T(512)S(1)}, f32[384]{0:T(512)}, u32[]{:S(2)}) copy-start(f32[384]{0:T(512)} %param.19) | copy-start | bytes 4612
  55.9 5.6 %collective-permute-start.15 = (f32[40,128]{1,0:T(8,128)S(1)}, f32[40,128]{1,0:T(8,128)S(1)}, u32[]{:S(2)}, u32[]{:S(2)}) collective-permute-start(f32[40,128]{1,0:T(8,128)S(1)} %get-tuple-element.54), channel_id=1, source_target_pairs={{0,2},{1,3},{2,4},{3,5},{4,6},{5,7},{6,0},{7,1},{8,10},{9,11},{10,... | collective-permute-start | bytes 61448 | tf_op jit(solution)/shard_map/ppermute | solution.py:58
  59.2 4.7 %collective-permute-start.16 = (f32[40,128]{1,0:T(8,128)S(1)}, f32[40,128]{1,0:T(8,128)S(1)}, u32[]{:S(2)}, u32[]{:S(2)}) collective-permute-start(f32[40,128]{1,0:T(8,128)S(1)} %get-tuple-element.54), channel_id=1, source_target_pairs={{0,4},{1,5},{2,6},{3,7},{4,0},{5,1},{6,2},{7,3},{8,12},{9,13},{10,... | collective-permute-start | bytes 61448 | tf_op jit(solution)/shard_map/ppermute | solution.py:58
  60.3 3.8 %collective-permute-start.17 = (f32[40,128]{1,0:T(8,128)S(1)}, f32[40,128]{1,0:T(8,128)S(1)}, u32[]{:S(2)}, u32[]{:S(2)}) collective-permute-start(f32[40,128]{1,0:T(8,128)S(1)} %get-tuple-element.54), channel_id=1, source_target_pairs={{0,6},{1,7},{2,0},{3,1},{4,2},{5,3},{6,4},{7,5},{8,14},{9,15},{10,... | collective-permute-start | bytes 61448 | tf_op jit(solution)/shard_map/ppermute | solution.py:58
  64.1 3.8 %collective-permute-start.18 = (f32[40,128]{1,0:T(8,128)S(1)}, f32[40,128]{1,0:T(8,128)S(1)}, u32[]{:S(2)}, u32[]{:S(2)}) collective-permute-start(f32[40,128]{1,0:T(8,128)S(1)} %add_add_fusion.refs_0_), channel_id=1, source_target_pairs={{0,1},{1,0},{2,3},{3,2},{4,5},{5,4},{6,7},{7,6},{8,9},{9,8},{10,11... | collective-permute-start | bytes 61448 | tf_op jit(solution)/shard_map/ppermute | solution.py:63
